TPU v7x, 128 devices: a whole 4x4x4 slice. The times are simulated.
128 devices in a mesh: lat: 4 (over x), lon: 32 (over z, y, core).
Axes of the slice: x: 4, y: 4, z: 4, core: 2. Of those that a mesh axis runs over, the one named last changes fastest.
Arguments:
- grid_field: bfloat16 [128, 4096, 192], P('lat', 'lon'), may hold values from -6 to 6
- conv_weight: bfloat16 [9, 192, 192], replicated, may hold values from -0.15625 to 0.15625
- observed: float32 [32768, 128], P(('lat', 'lon')), may hold values from -6 to 6
- hidden_mask: int32 [32768, 128], P(('lat', 'lon')), may hold values 0 or 1
- tile_route: int32 [32768, 1], P(('lat', 'lon')), may hold values from 0 to 127; in each aligned block of 256 rows (0 to 255, 256 to 511, ...) at most 4 rows name the same one
- station_spot: int32 [32768], P(('lat', 'lon')), may hold values from 0 to 62991
- neighbours: int32 [32768, 16], P(('lat', 'lon')), may hold values from 0 to 255
- neighbour_count: int32 [32768], P(('lat', 'lon')), may hold values from 2 to 16
- edge_bias: float32 [32768, 16], P(('lat', 'lon')), may hold values from -9 to 300
- live_count: int32 [128], P(('lat', 'lon')), may hold values from 32 to 256, as said below
- in_weight: bfloat16 [448, 192], replicated, may hold values from -0.25 to 0.25
- norm_gain: float32 [192], replicated, may hold values from 0.1 to 1.9
- qkv_weight: bfloat16 [192, 576], replicated, may hold values from -0.4375 to 0.4375
- out_weight: bfloat16 [192, 192], replicated, may hold values from -0.4375 to 0.4375
- final_gain: float32 [192], replicated, may hold values from 0.1 to 1.9
- head_weight: bfloat16 [192, 128], replicated, may hold values from -0.4375 to 0.4375
Outputs:
- predicted: float32 [32768, 128], P(('lat', 'lon'))
- grid_gradient: float32 [128, 4096, 192], P('lat', 'lon')
Inputs may be any that keep to these rules, and one draw needn't show every extreme that they name: `tile_route`: within the stations of one region no tile is named by more than 4 stations, and some tile reaches 4 in every draw. `neighbours`: entries at positions j >= neighbour_count are padding. Stations 0 to live_count - 1 of a region are present; some region has all 256 in every draw.
All inputs are finite; a program needn't handle non-finite values. No bound on the sum of `hidden_mask` on one device may be relied on, other than what follows from the above.
Results may differ from a plain program's by a relative error of at most 0.02.
Values may be sent and summed in bfloat16 or wider, within the bound.
A program may use at most 192 MiB of HBM per device.

v0:
```python
import math

import jax
import jax.numpy as jnp
from jax import lax
from jax.sharding import Mesh
from jax.sharding import PartitionSpec as P

CHANNELS = 192
HEADS = 3
HEAD_DIM = 64
LON = ("lon_0", "lon_1", "lon_2")
LAT_LON = ("lat", "lon_0", "lon_1", "lon_2")


EPS = 1e-06


def padded(cells, sides, width):
    for axis, dim in sides:
        count = lax.axis_size(axis)
        head = lax.slice_in_dim(cells, 0, width, axis=dim)
        tail = lax.slice_in_dim(cells, cells.shape[dim] - width, cells.shape[dim], axis=dim)
        cells = jnp.concatenate(
            [
                lax.ppermute(tail, axis, [(i, (i + 1) % count) for i in range(count)]),
                cells,
                lax.ppermute(head, axis, [((i + 1) % count, i) for i in range(count)]),
            ],
            axis=dim,
        )
    return cells


def split_up(value, dim, peers):
    before, after = (value.shape[:dim], value.shape[dim + 1 :])
    return jnp.moveaxis(value.reshape(*before, peers, -1, *after), dim, 0)


def in_order(pieces, dim):
    shape = list(pieces.shape[1:])
    shape[dim] *= pieces.shape[0]
    return jnp.moveaxis(pieces, 0, dim).reshape(shape)


def turned_blocks(pieces, axes, sequence):
    inside = pieces.shape[1:]
    whole = pieces.reshape(*(lax.axis_size(a) for a in axes), *inside)
    for k in sequence:
        whole = lax.all_to_all(whole, axes[k], k, k, tiled=True)
    return whole.reshape(-1, *inside)


def exchange_by_chip(value, groups, sequence, split_dim, concat_dim):
    peers = lax.axis_size(groups[0]) * lax.axis_size(groups[1])
    pieces = split_up(value, split_dim, peers)
    return in_order(turned_blocks(pieces, groups, sequence), concat_dim)


def seal_poles(extended):
    position = lax.axis_index("lat")
    last_index = lax.axis_size("lat") - 1
    keep = jnp.ones((extended.shape[0],), extended.dtype)
    keep = keep.at[0].set(jnp.where(position > 0, 1.0, 0.0).astype(extended.dtype))
    keep = keep.at[extended.shape[0] - 1].set(
        jnp.where(position < last_index, 1.0, 0.0).astype(extended.dtype)
    )
    return extended * keep[:, None, None]


def convolve(extended, taps, tile_rows, tile_cols, contract, reverse_taps):
    ext_rows, ext_cols, channels = extended.shape
    flat = extended.reshape(ext_rows * ext_cols, channels)
    products = lax.dot_general(
        flat, taps, (((1,), (contract,)), ((), ())), preferred_element_type=jnp.float32
    )
    products = products.reshape(ext_rows, ext_cols, 9, -1)
    total = None
    for offset in range(9):
        tap_index = 8 - offset if reverse_taps else offset
        term = products[
            offset // 3 : offset // 3 + tile_rows, offset % 3 : offset % 3 + tile_cols, tap_index
        ]
        total = term if total is None else total + term
    return total


def locate(spots, tile_cols):
    fine_width = 4 * (tile_cols - 1)
    fine_row = spots // fine_width
    fine_col = spots % fine_width
    base_cell = fine_row // 4 * tile_cols + fine_col // 4
    frac_row = ((fine_row % 4).astype(jnp.float32) + 0.5) / 4.0
    frac_col = ((fine_col % 4).astype(jnp.float32) + 0.5) / 4.0
    cells = jnp.stack(
        [base_cell, base_cell + 1, base_cell + tile_cols, base_cell + tile_cols + 1], axis=-1
    )
    weights = jnp.stack(
        [
            (1.0 - frac_row) * (1.0 - frac_col),
            (1.0 - frac_row) * frac_col,
            frac_row * (1.0 - frac_col),
            frac_row * frac_col,
        ],
        axis=-1,
    )
    return (cells, weights)


def blend(parts, weights):
    blended = weights[..., 0:1] * parts[..., 0, :]
    for corner in range(1, 4):
        blended = blended + weights[..., corner : corner + 1] * parts[..., corner, :]
    return blended


def rms_scale(values, gain):
    return values * lax.rsqrt(jnp.mean(values * values, axis=1, keepdims=True) + EPS) * gain


def station_forward(
    interp_rows,
    observed,
    hidden_mask,
    neighbours,
    valid,
    edge_bias,
    alive,
    in_weight,
    norm_gain,
    qkv_weight,
    out_weight,
    final_gain,
    head_weight,
):
    station_rows = observed.shape[0]
    mask_float = hidden_mask.astype(jnp.float32)
    joined = jnp.concatenate(
        [observed * (1.0 - mask_float), mask_float, interp_rows], axis=1
    ).astype(jnp.bfloat16)
    embedded = jnp.dot(joined, in_weight, preferred_element_type=jnp.float32)
    normed = rms_scale(embedded, norm_gain).astype(jnp.bfloat16)
    projected = jnp.dot(normed, qkv_weight, preferred_element_type=jnp.float32).astype(jnp.bfloat16)
    query_rows = projected[:, :CHANNELS].reshape(station_rows, HEADS, HEAD_DIM)
    key_rows = projected[:, CHANNELS : 2 * CHANNELS]
    value_rows = projected[:, 2 * CHANNELS :]
    near_keys = key_rows[neighbours].reshape(station_rows, -1, HEADS, HEAD_DIM)
    near_values = value_rows[neighbours].reshape(station_rows, -1, HEADS, HEAD_DIM)
    own_keys = key_rows.reshape(station_rows, HEADS, HEAD_DIM)
    own_values = value_rows.reshape(station_rows, HEADS, HEAD_DIM)
    score_scale = 1.0 / math.sqrt(HEAD_DIM)
    near_score = (
        jnp.einsum("shd,skhd->shk", query_rows, near_keys, preferred_element_type=jnp.float32)
        * score_scale
        + edge_bias[:, None, :]
    )
    near_score = jnp.where(valid[:, None, :], near_score, -1e30)
    own_score = (
        jnp.einsum("shd,shd->sh", query_rows, own_keys, preferred_element_type=jnp.float32)
        * score_scale
    )
    top_score = jnp.maximum(jnp.max(near_score, axis=2), own_score)
    near_weight = jnp.exp(near_score - top_score[:, :, None])
    own_weight = jnp.exp(own_score - top_score)
    weight_sum = jnp.sum(near_weight, axis=2) + own_weight
    near_prob = (near_weight / weight_sum[:, :, None]).astype(jnp.bfloat16)
    own_prob = (own_weight / weight_sum).astype(jnp.bfloat16)
    mixed_rows = jnp.einsum(
        "shk,skhd->shd", near_prob, near_values, preferred_element_type=jnp.float32
    )
    mixed_rows = mixed_rows + own_prob.astype(jnp.float32)[:, :, None] * own_values.astype(
        jnp.float32
    )
    mixed_rows = mixed_rows.reshape(station_rows, CHANNELS).astype(jnp.bfloat16)
    residual = embedded + jnp.dot(mixed_rows, out_weight, preferred_element_type=jnp.float32)
    final_rows = rms_scale(residual, final_gain).astype(jnp.bfloat16)
    return jnp.dot(final_rows, head_weight, preferred_element_type=jnp.float32) * alive[:, None]


def on_device(
    grid_field,
    conv_weight,
    observed,
    hidden_mask,
    tile_route,
    station_spot,
    neighbours,
    neighbour_count,
    edge_bias,
    live_count,
    in_weight,
    norm_gain,
    qkv_weight,
    out_weight,
    final_gain,
    head_weight,
):
    tile_rows, tile_cols, channels = grid_field.shape
    station_rows = observed.shape[0]
    regions = lax.axis_size("lat") * lax.axis_size(LON)
    capacity = max(2, 2 * station_rows // regions)
    extended = seal_poles(padded(grid_field, (("lat", 0), (LON, 1)), 1))
    pre_act = convolve(extended, conv_weight, tile_rows, tile_cols, 1, False)
    field = (grid_field.astype(jnp.float32) + jax.nn.silu(pre_act)).astype(jnp.bfloat16)
    flat_field = field.reshape(tile_rows * tile_cols, channels)
    target = tile_route[:, 0]
    member = (target[:, None] == jnp.arange(regions, dtype=jnp.int32)[None, :]).astype(jnp.bfloat16)
    station_index = jnp.arange(station_rows, dtype=jnp.int32)
    earlier = (station_index[:, None] > station_index[None, :]).astype(jnp.bfloat16)
    before = jnp.dot(earlier, member, preferred_element_type=jnp.float32)
    rank = jnp.sum(before * member.astype(jnp.float32), axis=1).astype(jnp.int32)
    slot = target * capacity + rank
    requests = (
        jnp.zeros((regions * capacity,), jnp.int32)
        .at[slot]
        .set(station_spot)
        .reshape(regions, capacity)
    )
    asked = lax.all_to_all(requests, LAT_LON, split_axis=0, concat_axis=0, tiled=True)
    cells, weights = locate(asked, tile_cols)
    picked = flat_field[cells]
    blended = blend(picked.astype(jnp.float32), weights).astype(jnp.bfloat16)
    answer = exchange_by_chip(blended, (("lat", "lon_0", "lon_1"), "lon_2"), (0, 1), 0, 0)
    interp = answer.reshape(regions * capacity, channels)[slot]
    live_here = live_count[0]
    alive = (station_index < live_here).astype(jnp.float32)
    valid = (
        jnp.arange(neighbours.shape[1], dtype=jnp.int32)[None, :] < neighbour_count[:, None]
    ) & (neighbours < live_here)

    def forward(interp_rows):
        return station_forward(
            interp_rows,
            observed,
            hidden_mask,
            neighbours,
            valid,
            edge_bias,
            alive,
            in_weight,
            norm_gain,
            qkv_weight,
            out_weight,
            final_gain,
            head_weight,
        )

    predicted, pullback = jax.vjp(forward, interp.astype(jnp.float32))
    d_pred = 2.0 * alive[:, None] * hidden_mask.astype(jnp.float32) * (predicted - observed)
    d_interp = pullback(d_pred)[0]
    received_cells, received_weights = locate(asked, tile_cols)
    outgoing = (
        jnp.zeros((regions * capacity, channels), jnp.float32)
        .at[slot]
        .set(d_interp)
        .reshape(regions, capacity, channels)
    )
    incoming = lax.all_to_all(
        outgoing.astype(jnp.bfloat16), LAT_LON, split_axis=0, concat_axis=0, tiled=True
    ).astype(outgoing.dtype)
    spread = received_weights[..., None] * incoming[:, :, None, :]
    d_field = jnp.zeros((tile_rows * tile_cols, channels), jnp.float32)
    d_field = (
        d_field.at[received_cells.reshape(-1)]
        .add(spread.reshape(-1, channels))
        .reshape(tile_rows, tile_cols, channels)
    )
    gate_sigmoid = jax.nn.sigmoid(pre_act)
    d_pre = (d_field * gate_sigmoid * (1.0 + pre_act * (1.0 - gate_sigmoid))).astype(jnp.bfloat16)
    d_ext = seal_poles(padded(d_pre, (("lat", 0), (LON, 1)), 1))
    grid_gradient = d_field + convolve(d_ext, conv_weight, tile_rows, tile_cols, 2, True)
    return (predicted, grid_gradient)


def solution(mesh):
    split = Mesh(
        mesh.devices.reshape(mesh.shape["lat"], 4, 4, 2), ("lat", "lon_0", "lon_1", "lon_2")
    )
    return jax.shard_map(
        on_device,
        mesh=split,
        in_specs=(
            P("lat", LON, None),
            P(),
            P(LAT_LON, None),
            P(LAT_LON, None),
            P(LAT_LON, None),
            P(LAT_LON),
            P(LAT_LON, None),
            P(LAT_LON),
            P(LAT_LON, None),
            P(LAT_LON),
            P(),
            P(),
            P(),
            P(),
            P(),
            P(),
        ),
        out_specs=(P(LAT_LON, None), P("lat", LON, None)),
        check_vma=False,
    )
```

profile of v0, /device:TPU:0, one launch (start us, length us, event | category | flops | bytes accessed | tf_op | source)
XLA Modules:
  0.0 380.3 jit_solution(3688115065962955513)
XLA Ops:
  0.7 1.0 fusion.42
  2.4 1.6 scatter_custom_fusion
  4.0 0.7 all_to_all.15
  4.7 11.1 %all-to-all-start = ((s32[128,1,4]{2,1,0:T(1,128)}), s32[128,1,4]{2,1,0:T(1,128)S(1)}, u32[]{:S(2)}, u32[]{:S(2)}) async-start(s32[128,1,4]{2,1,0:T(1,128)} %bitcast.7), calls=%async_computation | async-start | bytes 131072 | tf_op jit(solution)/shard_map/all_to_all | solution.py:219
  15.8 3.2 copy.447
  19.7 1.0 collective-permute-start
  20.7 2.3 collective-permute-start.1
  30.4 0.8 pad_maximum_fusion.5
  31.2 5.2 %collective-permute-start.3 = (bf16[34,1,192]{2,1,0:T(2,128)(2,1)S(1)}, bf16[34,1,192]{2,1,0:T(2,128)(2,1)S(1)}, u32[]{:S(2)}, u32[]{:S(2)}) collective-permute-start(bf16[34,1,192]{2,1,0:T(2,128)(2,1)S(1)} %get-tuple-element.84), channel_id=1, source_target_pairs={{1,0},{2,1},{3,2},{4,3},{5,4},{6,5},{7,6},{8,7},{9,8},{10,9},{11,1... | collective-permute-start | bytes 39176 | tf_op jit(solution)/shard_map/ppermute | solution.py:28
  36.4 0.9 copy.469
  37.3 1.2 reshape.884
  38.6 18.5 %fusion.6 = f32[34,130,9,192]{3,1,2,0:T(8,128)} fusion(bf16[34,1,192]{2,1,0:T(2,128)(2,1)S(1)} %collective-permute-done.3, bf16[1,128,192]{2,1,0:T(8,128)(2,1)} %collective-permute-done.1, bf16[32,128,192]{2,1,0:T(8,128)(2,1)S(1)} %copy.447, bf16[1,128,192]{2,1,0:T(8,128)(2,1)S(1)} %collective-permute-done, ...), kind=kOutput, calls=%fused_computation.43 | convolution fusion | flops 2943083520 | bytes 32911940 | tf_op jit(solution)/shard_map/dot_general | solution.py:74
  57.1 17.5 %add_convert_fusion = (bf16[32,128,192]{2,1,0:T(8,128)(2,1)S(1)}, f32[32,128,192]{2,1,0:T(8,128)}) fusion(bf16[32,128,192]{2,1,0:T(8,128)(2,1)} %copy-done.3, f32[34,130,9,192]{3,1,2,0:T(8,128)} %fusion.6), kind=kLoop, calls=%fused_computation.37 | loop fusion | flops 11796480 | bytes 34603008 | tf_op jit(solution)/shard_map/convert_element_type | solution.py:204
  74.5 9.1 %gather_fusion = bf16[2048,192]{1,0:T(8,128)(2,1)} fusion(bf16[4096,192]{1,0:T(8,128)(2,1)S(1)} %bitcast.141, s32[2048]{0:T(1024)S(1)} %broadcast_clamp_fusion.1), kind=kCustom, calls=%fused_computation | custom fusion | bytes 1581056 | tf_op jit(solution)/shard_map/gather | solution.py:221
  83.6 1.6 reshape.986
  85.2 1.5 fusion.133
  88.1 0.9 copy.460
  89.0 5.7 %all-to-all-start.1 = ((bf16[64,2,1,4,192]{4,3,1,2,0:T(4,128)(2,1)}), bf16[64,2,1,4,192]{4,3,1,2,0:T(4,128)(2,1)S(1)}, u32[]{:S(2)}, u32[]{:S(2)}) async-start(bf16[64,2,1,4,192]{4,3,1,2,0:T(4,128)(2,1)} %copy.460), calls=%async_computation.1 | async-start | bytes 524288 | tf_op jit(solution)/shard_map/all_to_all | solution.py:50
  95.3 9.8 %all-to-all-done.1 = bf16[64,2,1,4,192]{4,3,1,2,0:T(4,128)(2,1)S(1)} async-done(((bf16[64,2,1,4,192]{4,3,1,2,0:T(4,128)(2,1)}), bf16[64,2,1,4,192]{4,3,1,2,0:T(4,128)(2,1)S(1)}, u32[]{:S(2)}, u32[]{:S(2)}) %all-to-all-start.1) | async-done | bytes 196640 | tf_op jit(solution)/shard_map/all_to_all | solution.py:50
  105.2 5.0 %all_to_all.24 = bf16[64,2,1,4,192]{4,3,0,2,1:T(4,128)(2,1)S(1)} all-to-all(bf16[64,2,1,4,192]{4,3,0,2,1:T(4,128)(2,1)S(1)} %copy.461), channel_id=1, replica_groups=mesh['lat'=4,'lon_0'=4,'lon_1'=4,'lon_2'=2] {'lon_2'}, dimensions={1} | all-to-all | bytes 393216 | tf_op jit(solution)/shard_map/all_to_all | solution.py:50
  110.5 1.3 gather_fusion.1
  112.8 0.9 copy.529
  114.1 14.6 %gather_fusion.2 = bf16[4096,192]{1,0:T(8,128)(2,1)S(1)} fusion(bf16[256,192]{1,0:T(8,128)(2,1)S(1)} %copy.465, s32[4096]{0:T(1024)S(1)} %broadcast_clamp_fusion), kind=kCustom, calls=%fused_computation.2 | custom fusion | bytes 3162112 | tf_op jit(solution)/shard_map/jvp()/gather | solution.py:147
  128.8 17.0 %gather_fusion.3 = bf16[4096,192]{1,0:T(8,128)(2,1)} fusion(bf16[256,192]{1,0:T(8,128)(2,1)S(1)} %copy.467, s32[4096]{0:T(1024)S(1)} %broadcast_clamp_fusion), kind=kCustom, calls=%fused_computation.3 | custom fusion | bytes 3162112 | tf_op jit(solution)/shard_map/jvp()/gather | solution.py:148
  145.8 8.5 %reshape.883 = bf16[256,16,3,64]{3,2,1,0:T(4,128)(2,1)} reshape(bf16[4096,192]{1,0:T(8,128)(2,1)} %gather_fusion.3) | data formatting | bytes 3145728 | tf_op jit(solution)/shard_map/jvp()/reshape | solution.py:148
  154.3 4.0 %reshape.881 = bf16[256,16,3,64]{3,2,1,0:T(4,128)(2,1)} reshape(bf16[4096,192]{1,0:T(8,128)(2,1)S(1)} %gather_fusion.2) | data formatting | bytes 3145728 | tf_op jit(solution)/shard_map/jvp()/reshape | solution.py:147
  158.3 6.9 %multiply_reduce_fusion.3 = f32[256,3,16]{1,2,0:T(8,128)S(1)} fusion(f32[256,3,64]{2,1,0:T(4,128)} %copy.529, bf16[256,16,3,64]{3,2,1,0:T(4,128)(2,1)} %reshape.881), kind=kLoop, calls=%fused_computation.12 | loop fusion | flops 2347008 | bytes 1818624 | tf_op jit(solution)/shard_map/jvp(shd,skhd->shk)/dot_general | solution.py:153
  165.2 1.6 fusion.35
  166.9 1.6 fusion.122
  169.2 3.6 convert_reduce_fusion
  173.5 8.8 %multiply_reduce_fusion.2 = f32[256,3,64]{2,1,0:T(4,128)} fusion(f32[256,3,16]{1,2,0:T(8,128)} %get-tuple-element.80, bf16[256,16,3,64]{3,2,1,0:T(4,128)(2,1)} %reshape.883), kind=kLoop, calls=%fused_computation.11 | loop fusion | flops 2310144 | bytes 1818624
  182.3 1.2 copy.508
  183.6 1.1 multiply_reduce_fusion.6
  184.8 0.9 convolution_multiply_fusion
  185.7 1.3 multiply_reduce_fusion.5
  187.1 1.7 fusion.70
  189.6 1.9 copy.471
  191.4 1.0 copy.472
  192.4 0.8 copy.473
  193.2 12.6 %fusion = (bf16[256,16,3,64]{3,2,1,0:T(4,128)(2,1)}, bf16[256,3,16]{1,2,0:T(8,128)(2,1)}) fusion(f32[256,3,16]{1,2,0:T(8,128)} %get-tuple-element.80, f32[256,3,64]{2,1,0:T(4,128)} %copy.471, bf16[256,16,3,64]{3,2,1,0:T(4,128)(2,1)} %reshape.883), kind=kLoop, calls=%fused_computation.15 | loop fusion | flops 3919872 | bytes 3416064 | tf_op jit(solution)/shard_map/transpose(jvp(shk,skhd->shd))/convert_element_type | solution.py:168
  205.8 8.6 %reshape.945 = bf16[4096,192]{1,0:T(8,128)(2,1)} reshape(bf16[256,16,3,64]{3,2,1,0:T(4,128)(2,1)} %get-tuple-element.95) | data formatting | bytes 3145728 | tf_op jit(solution)/shard_map/transpose(jvp())/reshape | solution.py:148
  214.4 3.3 fusion.28
  217.8 1.6 fusion.125
  219.7 0.9 select_multiply_fusion
  220.6 1.3 copy-done.1
  222.0 6.4 %fusion.1 = (bf16[256,16,3,64]{3,2,1,0:T(4,128)(2,1)}, bf16[256,3,64]{2,1,0:T(4,128)(2,1)S(1)}) fusion(f32[256,3,64]{2,1,0:T(4,128)S(1)} %copy-done.6, f32[256,3,16]{1,2,0:T(8,128)S(1)} %select_multiply_fusion, bf16[256,16,3,64]{3,2,1,0:T(4,128)(2,1)S(1)} %copy-done.1), kind=kLoop, calls=%fused_computation.16 | loop fusion | flops 3883008 | bytes 3489792 | tf_op jit(solution)/shard_map/transpose(jvp(shd,skhd->shk))/convert_element_type | solution.py:153
  228.5 8.5 %reshape.953 = bf16[4096,192]{1,0:T(8,128)(2,1)} reshape(bf16[256,16,3,64]{3,2,1,0:T(4,128)(2,1)} %get-tuple-element.87) | data formatting | bytes 3145728 | tf_op jit(solution)/shard_map/transpose(jvp())/reshape | solution.py:147
  237.4 23.2 %scatter_fusion = bf16[256,192]{1,0:T(8,128)(2,1)S(1)} fusion(bf16[256,192]{1,0:T(8,128)(2,1)S(1)} %copy.472, s32[4096]{0:T(1024)S(1)} %reshape.919, bf16[4096,192]{1,0:T(8,128)(2,1)} %reshape.945), kind=kCustom, calls=%fused_computation.5 | custom fusion | flops 786432 | bytes 4734976 | tf_op jit(solution)/shard_map/transpose(jvp())/scatter-add | solution.py:148
  260.7 23.4 %scatter_fusion.1 = bf16[256,192]{1,0:T(8,128)(2,1)S(1)} fusion(bf16[256,192]{1,0:T(8,128)(2,1)S(1)} %copy.477, s32[4096]{0:T(1024)S(1)} %reshape.919, bf16[4096,192]{1,0:T(8,128)(2,1)} %reshape.953), kind=kCustom, calls=%fused_computation.6 | custom fusion | flops 786432 | bytes 4734976 | tf_op jit(solution)/shard_map/transpose(jvp())/scatter-add | solution.py:147
  285.0 1.7 scatter_custom_fusion.3
  286.8 0.8 convert_element_type.271
  287.5 4.8 %all-to-all-start.3 = ((bf16[128,4,192]{2,1,0:T(4,128)(2,1)}), bf16[128,4,192]{2,1,0:T(4,128)(2,1)S(1)}, u32[]{:S(2)}, u32[]{:S(2)}) async-start(bf16[128,4,192]{2,1,0:T(4,128)(2,1)} %convert_element_type.271), calls=%async_computation.3 | async-start | bytes 524288 | tf_op jit(solution)/shard_map/all_to_all | solution.py:258
  292.8 10.3 %all-to-all-done.3 = bf16[128,4,192]{2,1,0:T(4,128)(2,1)S(1)} async-done(((bf16[128,4,192]{2,1,0:T(4,128)(2,1)}), bf16[128,4,192]{2,1,0:T(4,128)(2,1)S(1)}, u32[]{:S(2)}, u32[]{:S(2)}) %all-to-all-start.3) | async-done | bytes 196640 | tf_op jit(solution)/shard_map/all_to_all | solution.py:258
  303.1 1.9 mul.530
  305.0 2.0 mul.531
  307.0 14.8 %scatter_custom_fusion.4 = f32[4096,192]{1,0:T(8,128)} fusion(s32[2048]{0:T(1024)} %bitcast.166, f32[2048,192]{1,0:T(8,128)S(1)} %mul.531, f32[]{:T(128)} %constant.190.clone.1, f32[2048]{0:T(1024)S(1)} %mul.494), kind=kCustom, calls=%fused_computation.67 | custom fusion | flops 786432 | bytes 4727296 | tf_op jit(solution)/shard_map/scatter-add | solution.py:265
  321.8 4.9 %multiply_convert_fusion.2 = bf16[32,128,192]{2,1,0:T(8,128)(2,1)S(1)} fusion(f32[32,128,192]{2,1,0:T(8,128)} %get-tuple-element.79, f32[32,128,192]{2,1,0:T(8,128)} %bitcast.142), kind=kLoop, calls=%fused_computation.36 | loop fusion | flops 7077888 | bytes 7864320 | tf_op jit(solution)/shard_map/convert_element_type | solution.py:269
  327.4 2.7 collective-permute-start.5
  330.1 2.2 collective-permute-done.4
  332.5 5.2 %collective-permute-start.7 = (bf16[34,1,192]{2,1,0:T(2,128)(2,1)S(1)}, bf16[34,1,192]{2,1,0:T(2,128)(2,1)S(1)}, u32[]{:S(2)}, u32[]{:S(2)}) collective-permute-start(bf16[34,1,192]{2,1,0:T(2,128)(2,1)S(1)} %get-tuple-element.82), channel_id=1, source_target_pairs={{1,0},{2,1},{3,2},{4,3},{5,4},{6,5},{7,6},{8,7},{9,8},{10,9},{11,1... | collective-permute-start | bytes 39176 | tf_op jit(solution)/shard_map/ppermute | solution.py:28
  337.7 1.4 collective-permute-done.6
  339.3 18.4 %fusion.17 = f32[34,130,9,192]{3,1,0,2:T(8,128)} fusion(bf16[34,1,192]{2,1,0:T(2,128)(2,1)S(1)} %collective-permute-done.7, bf16[1,128,192]{2,1,0:T(8,128)(2,1)S(1)} %collective-permute-done.5, bf16[32,128,192]{2,1,0:T(8,128)(2,1)} %copy-done.4, bf16[1,128,192]{2,1,0:T(8,128)(2,1)S(1)} %collective-permute-done.4, ...), kind=kOutput, calls=%fused_computation.54 | convolution fusion | flops 2943083520 | bytes 32911940 | tf_op jit(solution)/shard_map/dot_general | solution.py:74
  357.7 17.1 %fusion.3 = f32[32,128,192]{2,1,0:T(8,128)} fusion(f32[32,128,192]{2,1,0:T(8,128)S(1)} %bitcast.143, f32[34,130,9,192]{3,1,0,2:T(8,128)} %fusion.17), kind=kLoop, calls=%fused_computation.19 | loop fusion | flops 7077888 | bytes 34603008 | tf_op jit(solution)/shard_map/add | solution.py:271
  374.8 5.3 %copy.489 = f32[32,128,192]{1,2,0:T(8,128)} copy(f32[32,128,192]{2,1,0:T(8,128)} %fusion.3) | data formatting | bytes 6291456
  (226 shorter events, 17.0 us)
Async XLA Ops:
  0.6 37.9 %copy-start = (bf16[9,192,192]{2,1,0:T(8,128)(2,1)S(1)}, bf16[9,192,192]{2,1,0:T(8,128)(2,1)}, u32[]{:S(2)}) copy-start(bf16[9,192,192]{2,1,0:T(8,128)(2,1)} %param.25) | copy-start | bytes 1990660
  0.6 24.1 %copy-start.46 = (s32[256,16]{0,1:T(8,128)S(1)}, s32[256,16]{0,1:T(8,128)}, u32[]{:S(2)}) copy-start(s32[256,16]{0,1:T(8,128)} %param.30) | copy-start | bytes 49156
  0.7 24.1 %copy-start.34 = (s32[256,128]{1,0:T(8,128)S(1)}, s32[256,128]{1,0:T(8,128)}, u32[]{:S(2)}) copy-start(s32[256,128]{1,0:T(8,128)} %param.27) | copy-start | bytes 393220
  0.7 24.7 %copy-start.37 = (f32[256,128]{1,0:T(8,128)S(1)}, f32[256,128]{1,0:T(8,128)}, u32[]{:S(2)}) copy-start(f32[256,128]{1,0:T(8,128)} %param.26) | copy-start | bytes 393220
  2.4 21.8 %copy-start.62 = (s32[256,1]{0,1:T(1,128)}, s32[256,1]{0,1:T(1,128)S(1)}, u32[]{:S(2)}) copy-start(s32[256,1]{0,1:T(1,128)S(1)} %compare_select_fusion.3) | copy-start | bytes 3076
  4.7 23.7 %all-to-all-start = ((s32[128,1,4]{2,1,0:T(1,128)}), s32[128,1,4]{2,1,0:T(1,128)S(1)}, u32[]{:S(2)}, u32[]{:S(2)}) async-start(s32[128,1,4]{2,1,0:T(1,128)} %bitcast.7), calls=%async_computation | async-start | bytes 131072 | tf_op jit(solution)/shard_map/all_to_all | solution.py:219
  15.8 10.4 %copy-start.67 = (s32[256]{0:T(256)S(1)}, s32[256]{0:T(256)}, u32[]{:S(2)}) copy-start(s32[256]{0:T(256)} %param.31) | copy-start | bytes 3076
  15.8 11.7 %copy-start.50 = (f32[256,16]{0,1:T(8,128)S(1)}, f32[256,16]{0,1:T(8,128)}, u32[]{:S(2)}) copy-start(f32[256,16]{0,1:T(8,128)} %param.32) | copy-start | bytes 49156
  19.0 19.5 %copy-start.3 = (bf16[32,128,192]{2,1,0:T(8,128)(2,1)}, bf16[32,128,192]{2,1,0:T(8,128)(2,1)S(1)}, u32[]{:S(2)}) copy-start(bf16[32,128,192]{2,1,0:T(8,128)(2,1)S(1)} %copy.447) | copy-start | bytes 4718596
  19.7 10.6 %collective-permute-start = (bf16[1,128,192]{2,1,0:T(8,128)(2,1)}, bf16[1,128,192]{2,1,0:T(8,128)(2,1)S(1)}, u32[]{:S(2)}, u32[]{:S(2)}) collective-permute-start(bf16[1,128,192]{2,1,0:T(8,128)(2,1)} %get-tuple-element.93), channel_id=1, source_target_pairs={{0,32},{32,64},{64,96},{96,0},{1,33},{33,65},{65,97},{97,1},{2,34}... | collective-permute-start | bytes 147464 | tf_op jit(solution)/shard_map/ppermute | solution.py:26
  20.7 9.7 %collective-permute-start.1 = (bf16[1,128,192]{2,1,0:T(8,128)(2,1)}, bf16[1,128,192]{2,1,0:T(8,128)(2,1)}, u32[]{:S(2)}, u32[]{:S(2)}) collective-permute-start(bf16[1,128,192]{2,1,0:T(8,128)(2,1)} %get-tuple-element.94), channel_id=1, source_target_pairs={{32,0},{64,32},{96,64},{0,96},{33,1},{65,33},{97,65},{1,97},{34,2}... | collective-permute-start | bytes 147464 | tf_op jit(solution)/shard_map/ppermute | solution.py:28
  27.7 141.5 %copy-start.7 = (f32[256,16]{1,0:T(8,128)}, f32[256,16]{1,0:T(8,128)S(1)}, u32[]{:S(2)}) copy-start(f32[256,16]{1,0:T(8,128)S(1)} %copy.466) | copy-start | bytes 49156
  28.4 10.2 %copy-start.52 = (bf16[34]{0:T(256)(128)(2,1)S(1)}, bf16[34]{0:T(256)(128)(2,1)}, u32[]{:S(2)}) copy-start(bf16[34]{0:T(256)(128)(2,1)} %copy-done.51) | copy-start | bytes 208
  31.1 7.4 %collective-permute-start.2 = (bf16[34,1,192]{2,1,0:T(2,128)(2,1)S(1)}, bf16[34,1,192]{2,1,0:T(2,128)(2,1)S(1)}, u32[]{:S(2)}, u32[]{:S(2)}) collective-permute-start(bf16[34,1,192]{2,1,0:T(2,128)(2,1)S(1)} %get-tuple-element.83), channel_id=1, source_target_pairs={{0,1},{1,2},{2,3},{3,4},{4,5},{5,6},{6,7},{7,8},{8,9},{9,10},{10,1... | collective-permute-start | bytes 39176 | tf_op jit(solution)/shard_map/ppermute | solution.py:26
  31.2 7.3 %collective-permute-start.3 = (bf16[34,1,192]{2,1,0:T(2,128)(2,1)S(1)}, bf16[34,1,192]{2,1,0:T(2,128)(2,1)S(1)}, u32[]{:S(2)}, u32[]{:S(2)}) collective-permute-start(bf16[34,1,192]{2,1,0:T(2,128)(2,1)S(1)} %get-tuple-element.84), channel_id=1, source_target_pairs={{1,0},{2,1},{3,2},{4,3},{5,4},{6,5},{7,6},{8,7},{9,8},{10,9},{11,1... | collective-permute-start | bytes 39176 | tf_op jit(solution)/shard_map/ppermute | solution.py:28
  88.0 23.7 %copy-start.41 = (bf16[448,192]{0,1:T(8,128)(2,1)S(1)}, bf16[448,192]{0,1:T(8,128)(2,1)}, u32[]{:S(2)}) copy-start(bf16[448,192]{0,1:T(8,128)(2,1)} %param.34) | copy-start | bytes 516100
  88.0 23.7 %copy-start.44 = (bf16[256,128]{1,0:T(8,128)(2,1)S(1)}, bf16[256,128]{1,0:T(8,128)(2,1)}, u32[]{:S(2)}) copy-start(bf16[256,128]{1,0:T(8,128)(2,1)} %convert_convert_fusion) | copy-start | bytes 196612
  88.0 23.7 %copy-start.45 = (bf16[256,128]{1,0:T(8,128)(2,1)S(1)}, bf16[256,128]{1,0:T(8,128)(2,1)}, u32[]{:S(2)}) copy-start(bf16[256,128]{1,0:T(8,128)(2,1)} %multiply_convert_fusion.6) | copy-start | bytes 196612
  89.0 23.1 %copy-start.39 = (bf16[192,576]{1,0:T(8,128)(2,1)S(1)}, bf16[192,576]{1,0:T(8,128)(2,1)}, u32[]{:S(2)}) copy-start(bf16[192,576]{1,0:T(8,128)(2,1)} %param.36) | copy-start | bytes 663556
  89.0 23.1 %copy-start.65 = (f32[192]{0:T(256)S(1)}, f32[192]{0:T(256)}, u32[]{:S(2)}) copy-start(f32[192]{0:T(256)} %param.35) | copy-start | bytes 2308
  89.0 16.2 %all-to-all-start.1 = ((bf16[64,2,1,4,192]{4,3,1,2,0:T(4,128)(2,1)}), bf16[64,2,1,4,192]{4,3,1,2,0:T(4,128)(2,1)S(1)}, u32[]{:S(2)}, u32[]{:S(2)}) async-start(bf16[64,2,1,4,192]{4,3,1,2,0:T(4,128)(2,1)} %copy.460), calls=%async_computation.1 | async-start | bytes 524288 | tf_op jit(solution)/shard_map/all_to_all | solution.py:50
  114.0 54.5 %copy-start.13 = (f32[256,3]{1,0:T(8,128)}, f32[256,3]{1,0:T(8,128)S(1)}, u32[]{:S(2)}) copy-start(f32[256,3]{1,0:T(8,128)S(1)} %copy.501) | copy-start | bytes 9220
  158.3 6.9 %copy-start.25 = (pred[256,16]{1,0:T(8,128)(4,1)S(1)}, pred[256,16]{1,0:T(8,128)(4,1)}, u32[]{:S(2)}) copy-start(pred[256,16]{1,0:T(8,128)(4,1)} %copy.463) | copy-start | bytes 12292
  166.8 5.9 %copy-start.11 = (f32[256,3]{1,0:T(8,128)}, f32[256,3]{1,0:T(8,128)S(1)}, u32[]{:S(2)}) copy-start(f32[256,3]{1,0:T(8,128)S(1)} %fusion.35) | copy-start | bytes 9220
  166.8 5.9 %copy-start.15 = (f32[256,3]{1,0:T(8,128)}, f32[256,3]{1,0:T(8,128)S(1)}, u32[]{:S(2)}) copy-start(f32[256,3]{1,0:T(8,128)S(1)} %multiply_maximum_fusion) | copy-start | bytes 9220
  169.2 3.6 copy-start.9
  169.2 3.6 copy-start.17
  173.5 10.0 %copy-start.32 = (bf16[256,192]{0,1:T(8,128)(2,1)S(1)}, bf16[256,192]{0,1:T(8,128)(2,1)}, u32[]{:S(2)}) copy-start(bf16[256,192]{0,1:T(8,128)(2,1)} %copy-done.31) | copy-start | bytes 294916
  173.5 10.0 %copy-start.47 = (f32[256,3]{0,1:T(4,128)S(1)}, f32[256,3]{0,1:T(4,128)}, u32[]{:S(2)}) copy-start(f32[256,3]{0,1:T(4,128)} %copy.468) | copy-start | bytes 9220
  173.5 10.1 %copy-start.21 = (f32[256,192]{0,1:T(8,128)S(1)}, f32[256,192]{0,1:T(8,128)}, u32[]{:S(2)}) copy-start(f32[256,192]{0,1:T(8,128)} %copy-done.20) | copy-start | bytes 589828
  173.5 11.3 %copy-start.43 = (bf16[192,128]{1,0:T(8,128)(2,1)S(1)}, bf16[192,128]{1,0:T(8,128)(2,1)}, u32[]{:S(2)}) copy-start(bf16[192,128]{1,0:T(8,128)(2,1)} %param.39) | copy-start | bytes 147460
  173.5 11.3 %copy-start.61 = (f32[192]{0:T(256)S(1)}, f32[192]{0:T(256)}, u32[]{:S(2)}) copy-start(f32[192]{0:T(256)} %param.38) | copy-start | bytes 2308
  184.7 21.1 %copy-start.48 = (f32[256]{0:T(256)}, f32[256]{0:T(256)S(1)}, u32[]{:S(2)}) copy-start(f32[256]{0:T(256)S(1)} %fusion.117) | copy-start | bytes 3076
  187.1 4.3 %copy-start.23 = (f32[256,192]{0,1:T(8,128)}, f32[256,192]{0,1:T(8,128)S(1)}, u32[]{:S(2)}) copy-start(f32[256,192]{0,1:T(8,128)S(1)} %get-tuple-element.115) | copy-start | bytes 589828
  187.1 18.7 %copy-start.54 = (f32[256]{0:T(256)}, f32[256]{0:T(256)S(1)}, u32[]{:S(2)}) copy-start(f32[256]{0:T(256)S(1)} %multiply_multiply_fusion.1) | copy-start | bytes 3076
  205.8 8.6 %copy-start.8 = (f32[256,16]{1,0:T(8,128)S(1)}, f32[256,16]{1,0:T(8,128)}, u32[]{:S(2)}) copy-start(f32[256,16]{1,0:T(8,128)} %copy-done.7) | copy-start | bytes 49156
  205.8 8.6 %copy-start.26 = (pred[256,16]{1,0:T(8,128)(4,1)S(1)}, pred[256,16]{1,0:T(8,128)(4,1)}, u32[]{:S(2)}) copy-start(pred[256,16]{1,0:T(8,128)(4,1)} %copy.463) | copy-start | bytes 12292
  214.4 3.3 copy-start.10
  214.4 3.3 copy-start.18
  214.4 3.3 copy-start.33
  214.4 3.4 copy-start.5
  214.4 3.4 copy-start.16
  222.0 6.4 %copy-start.30 = (bf16[256,192]{0,1:T(8,128)(2,1)S(1)}, bf16[256,192]{0,1:T(8,128)(2,1)}, u32[]{:S(2)}) copy-start(bf16[256,192]{0,1:T(8,128)(2,1)} %copy-done.29) | copy-start | bytes 294916
  228.5 8.8 %copy-start.28 = (bf16[256,192]{0,1:T(8,128)(2,1)S(1)}, bf16[256,192]{0,1:T(8,128)(2,1)}, u32[]{:S(2)}) copy-start(bf16[256,192]{0,1:T(8,128)(2,1)} %copy-done.27) | copy-start | bytes 294916
  260.6 23.5 %copy-start.22 = (f32[256,192]{0,1:T(8,128)S(1)}, f32[256,192]{0,1:T(8,128)}, u32[]{:S(2)}) copy-start(f32[256,192]{0,1:T(8,128)} %copy-done.20) | copy-start | bytes 589828
  260.6 23.5 %copy-start.40 = (bf16[192,576]{1,0:T(8,128)(2,1)S(1)}, bf16[192,576]{1,0:T(8,128)(2,1)}, u32[]{:S(2)}) copy-start(bf16[192,576]{1,0:T(8,128)(2,1)} %param.36) | copy-start | bytes 663556
  260.6 23.5 %copy-start.66 = (f32[192]{0:T(256)S(1)}, f32[192]{0:T(256)}, u32[]{:S(2)}) copy-start(f32[192]{0:T(256)} %param.35) | copy-start | bytes 2308
  260.6 23.9 %copy-start.64 = (f32[256]{0:T(256)S(1)}, f32[256]{0:T(256)}, u32[]{:S(2)}) copy-start(f32[256]{0:T(256)} %copy-done.63) | copy-start | bytes 3076
  260.6 23.9 %copy-start.24 = (f32[256,192]{0,1:T(8,128)S(1)}, f32[256,192]{0,1:T(8,128)}, u32[]{:S(2)}) copy-start(f32[256,192]{0,1:T(8,128)} %copy-done.23) | copy-start | bytes 589828
  260.6 23.9 %copy-start.42 = (bf16[448,192]{0,1:T(8,128)(2,1)S(1)}, bf16[448,192]{0,1:T(8,128)(2,1)}, u32[]{:S(2)}) copy-start(bf16[448,192]{0,1:T(8,128)(2,1)} %param.34) | copy-start | bytes 516100
  260.7 23.9 %copy-start.49 = (f32[256]{0:T(256)S(1)}, f32[256]{0:T(256)}, u32[]{:S(2)}) copy-start(f32[256]{0:T(256)} %copy-done.48) | copy-start | bytes 3076
  260.7 23.9 %copy-start.55 = (f32[256]{0:T(256)S(1)}, f32[256]{0:T(256)}, u32[]{:S(2)}) copy-start(f32[256]{0:T(256)} %copy-done.54) | copy-start | bytes 3076
  260.7 23.9 %copy-start.57 = (f32[256]{0:T(256)S(1)}, f32[256]{0:T(256)}, u32[]{:S(2)}) copy-start(f32[256]{0:T(256)} %copy-done.56) | copy-start | bytes 3076
  284.5 7.9 %copy-start.58 = (f32[128,4,1]{0,1,2:T(4,128)S(1)}, f32[128,4,1]{0,1,2:T(4,128)}, u32[]{:S(2)}) copy-start(f32[128,4,1]{0,1,2:T(4,128)} %get-tuple-element.61) | copy-start | bytes 6148
  284.5 7.9 %copy-start.59 = (f32[128,4,1]{0,1,2:T(4,128)S(1)}, f32[128,4,1]{0,1,2:T(4,128)}, u32[]{:S(2)}) copy-start(f32[128,4,1]{0,1,2:T(4,128)} %get-tuple-element.62) | copy-start | bytes 6148
  284.5 7.9 %copy-start.60 = (f32[128,4,1]{0,1,2:T(4,128)S(1)}, f32[128,4,1]{0,1,2:T(4,128)}, u32[]{:S(2)}) copy-start(f32[128,4,1]{0,1,2:T(4,128)} %get-tuple-element.60) | copy-start | bytes 6148
  287.5 15.5 %all-to-all-start.3 = ((bf16[128,4,192]{2,1,0:T(4,128)(2,1)}), bf16[128,4,192]{2,1,0:T(4,128)(2,1)S(1)}, u32[]{:S(2)}, u32[]{:S(2)}) async-start(bf16[128,4,192]{2,1,0:T(4,128)(2,1)} %convert_element_type.271), calls=%async_computation.3 | async-start | bytes 524288 | tf_op jit(solution)/shard_map/all_to_all | solution.py:258
  326.7 12.4 %copy-start.4 = (bf16[32,128,192]{2,1,0:T(8,128)(2,1)}, bf16[32,128,192]{2,1,0:T(8,128)(2,1)S(1)}, u32[]{:S(2)}) copy-start(bf16[32,128,192]{2,1,0:T(8,128)(2,1)S(1)} %multiply_convert_fusion.2) | copy-start | bytes 4718596
  326.7 12.6 %copy-start.53 = (bf16[34]{0:T(256)(128)(2,1)S(1)}, bf16[34]{0:T(256)(128)(2,1)}, u32[]{:S(2)}) copy-start(bf16[34]{0:T(256)(128)(2,1)} %copy-done.51) | copy-start | bytes 208
  326.8 5.5 %collective-permute-start.4 = (bf16[1,128,192]{2,1,0:T(8,128)(2,1)S(1)}, bf16[1,128,192]{2,1,0:T(8,128)(2,1)S(1)}, u32[]{:S(2)}, u32[]{:S(2)}) collective-permute-start(bf16[1,128,192]{2,1,0:T(8,128)(2,1)S(1)} %get-tuple-element.85), channel_id=1, source_target_pairs={{0,32},{32,64},{64,96},{96,0},{1,33},{33,65},{65,97},{97,1},{2,34}... | collective-permute-start | bytes 147464 | tf_op jit(solution)/shard_map/ppermute | solution.py:26
  327.4 4.9 %collective-permute-start.5 = (bf16[1,128,192]{2,1,0:T(8,128)(2,1)S(1)}, bf16[1,128,192]{2,1,0:T(8,128)(2,1)S(1)}, u32[]{:S(2)}, u32[]{:S(2)}) collective-permute-start(bf16[1,128,192]{2,1,0:T(8,128)(2,1)S(1)} %get-tuple-element.86), channel_id=1, source_target_pairs={{32,0},{64,32},{96,64},{0,96},{33,1},{65,33},{97,65},{1,97},{34,2}... | collective-permute-start | bytes 147464 | tf_op jit(solution)/shard_map/ppermute | solution.py:28
  332.4 6.8 %collective-permute-start.6 = (bf16[34,1,192]{2,1,0:T(2,128)(2,1)S(1)}, bf16[34,1,192]{2,1,0:T(2,128)(2,1)S(1)}, u32[]{:S(2)}, u32[]{:S(2)}) collective-permute-start(bf16[34,1,192]{2,1,0:T(2,128)(2,1)S(1)} %get-tuple-element.81), channel_id=1, source_target_pairs={{0,1},{1,2},{2,3},{3,4},{4,5},{5,6},{6,7},{7,8},{8,9},{9,10},{10,1... | collective-permute-start | bytes 39176 | tf_op jit(solution)/shard_map/ppermute | solution.py:26
  332.5 6.9 %collective-permute-start.7 = (bf16[34,1,192]{2,1,0:T(2,128)(2,1)S(1)}, bf16[34,1,192]{2,1,0:T(2,128)(2,1)S(1)}, u32[]{:S(2)}, u32[]{:S(2)}) collective-permute-start(bf16[34,1,192]{2,1,0:T(2,128)(2,1)S(1)} %get-tuple-element.82), channel_id=1, source_target_pairs={{1,0},{2,1},{3,2},{4,3},{5,4},{6,5},{7,6},{8,7},{9,8},{10,9},{11,1... | collective-permute-start | bytes 39176 | tf_op jit(solution)/shard_map/ppermute | solution.py:28
  339.3 18.4 %copy-start.2 = (f32[4096,192]{1,0:T(8,128)S(1)}, f32[4096,192]{1,0:T(8,128)}, u32[]{:S(2)}) copy-start(f32[4096,192]{1,0:T(8,128)} %scatter_custom_fusion.4) | copy-start | bytes 9437188
  (15 other events, 22.3 us)
where the time goes:
time: 386 us; the launch traced here: 380 us
  other arithmetic  156 us (40%)
  local copies, waits for them, and re-layouts  110 us (28%)
  matrix products  44.3 us (11%)
  starting transfers between devices  38.8 us (10%)
  waiting for transfers between devices  23.9 us (6%)
  blocking collectives  4.98 us (1%)
    dot_general x2, matrix products, convolve(): lax.dot_general(flat, taps, (((1,), (contract,)), ((), ())), preferred_el...  36.9 us
    scatter-add x1, other arithmetic, station_forward(): near_keys = key_rows[neighbours].reshape(station_rows, -1, HEADS, HEAD_DIM)  23.4 us
    scatter-add x1, other arithmetic, station_forward(): value_rows[neighbours].reshape(station_rows, -1, HEADS, HEAD_DIM)  23.2 us
    convert_element_type x1, other arithmetic, on_device(): (grid_field.astype(jnp.float32) + jax.nn.silu(pre_act)).astype(jnp.bfloat16)  17.5 us
    reshape x2, local copies, waits for them, and re-layouts, station_forward(): value_rows[neighbours].reshape(station_rows, -1, HEADS, HEAD_DIM)  17.1 us
    add x1, other arithmetic, on_device(): d_field + convolve(d_ext, conv_weight, tile_rows, tile_cols, 2, True)  17.1 us
    gather x1, local copies, waits for them, and re-layouts, station_forward(): value_rows[neighbours].reshape(station_rows, -1, HEADS, HEAD_DIM)  17 us
    ppermute x4, starting transfers between devices, padded(): lax.ppermute(head, axis, [((i + 1) % count, i) for i in range(count)])  15.4 us
  transfers between devices with their start and end apart: 11, of which 5 were waited for; matrix products, arithmetic and copies ran while one was open for 3% of the time, Pallas kernels for 0%

commit v1 on v0

--- a/solution.py
+++ b/solution.py
@@ -3,6 +3,8 @@
 import jax
 import jax.numpy as jnp
 from jax import lax
+from jax.experimental import pallas as pl
+from jax.experimental.pallas import tpu as pltpu
 from jax.sharding import Mesh
 from jax.sharding import PartitionSpec as P
 
@@ -14,6 +16,78 @@
 
 
 EPS = 1e-06
+
+
+def direct_exchange(pieces, number):
+    peers, rows, lanes = pieces.shape
+    sizes = [lax.axis_size(a) for a in LAT_LON]
+
+    def kernel(x_ref, o_ref, held, send_sem, recv_sem):
+        me = lax.axis_index("lat")
+        for axis in LAT_LON[1:]:
+            me = me * lax.axis_size(axis) + lax.axis_index(axis)
+
+        def coords(p):
+            found = []
+            for size in reversed(sizes):
+                found.append(lax.rem(p, size))
+                p = p // size
+            return tuple(reversed(found))
+
+        barrier = pltpu.get_barrier_semaphore()
+
+        def greet(i, carry):
+            peer = lax.rem(me + i, peers)
+            pl.semaphore_signal(
+                barrier, inc=1, device_id=coords(peer), device_id_type=pl.DeviceIdType.MESH
+            )
+            return carry
+
+        lax.fori_loop(1, peers, greet, 0)
+        pl.semaphore_wait(barrier, peers - 1)
+
+        def send(i, carry):
+            peer = lax.rem(me + i, peers)
+            pltpu.make_async_remote_copy(
+                src_ref=x_ref.at[peer],
+                dst_ref=held.at[me],
+                send_sem=send_sem,
+                recv_sem=recv_sem,
+                device_id=coords(peer),
+                device_id_type=pl.DeviceIdType.MESH,
+            ).start()
+            return carry
+
+        lax.fori_loop(1, peers, send, 0)
+        held[me] = x_ref[me]
+        rest = held.at[pl.ds(0, peers - 1)]
+        pltpu.make_async_copy(rest, rest, recv_sem).wait()
+        pltpu.make_async_copy(rest, rest, send_sem).wait()
+        o_ref[...] = held[...]
+
+    return pl.pallas_call(
+        kernel,
+        out_shape=jax.ShapeDtypeStruct(pieces.shape, pieces.dtype),
+        in_specs=[pl.BlockSpec(memory_space=pltpu.VMEM)],
+        out_specs=pl.BlockSpec(memory_space=pltpu.VMEM),
+        scratch_shapes=[
+            pltpu.VMEM(pieces.shape, pieces.dtype),
+            pltpu.SemaphoreType.DMA,
+            pltpu.SemaphoreType.DMA,
+        ],
+        compiler_params=pltpu.CompilerParams(
+            collective_id=number, has_side_effects=True, vmem_limit_bytes=16 << 20
+        ),
+        name=f"exchange_{number}",
+    )(pieces)
+
+
+def send_rows(rows, number):
+    regions, capacity, channels = rows.shape
+    wide = jnp.pad(rows, ((0, 0), (0, 0), (0, 256 - channels)))
+    pieces = wide.reshape(regions, capacity * 2, 128)
+    back = direct_exchange(pieces, number)
+    return back.reshape(regions, capacity, 256)[:, :, :channels]
 
 
 def padded(cells, sides, width):
@@ -216,11 +290,12 @@
         .set(station_spot)
         .reshape(regions, capacity)
     )
-    asked = lax.all_to_all(requests, LAT_LON, split_axis=0, concat_axis=0, tiled=True)
+    wide_requests = jnp.pad(requests, ((0, 0), (0, 128 - capacity))).reshape(regions, 1, 128)
+    asked = direct_exchange(wide_requests, 0).reshape(regions, 128)[:, :capacity]
     cells, weights = locate(asked, tile_cols)
     picked = flat_field[cells]
     blended = blend(picked.astype(jnp.float32), weights).astype(jnp.bfloat16)
-    answer = exchange_by_chip(blended, (("lat", "lon_0", "lon_1"), "lon_2"), (0, 1), 0, 0)
+    answer = send_rows(blended, 1)
     interp = answer.reshape(regions * capacity, channels)[slot]
     live_here = live_count[0]
     alive = (station_index < live_here).astype(jnp.float32)
@@ -255,9 +330,7 @@
         .set(d_interp)
         .reshape(regions, capacity, channels)
     )
-    incoming = lax.all_to_all(
-        outgoing.astype(jnp.bfloat16), LAT_LON, split_axis=0, concat_axis=0, tiled=True
-    ).astype(outgoing.dtype)
+    incoming = send_rows(outgoing.astype(jnp.bfloat16), 2).astype(outgoing.dtype)
     spread = received_weights[..., None] * incoming[:, :, None, :]
     d_field = jnp.zeros((tile_rows * tile_cols, channels), jnp.float32)
     d_field = (

time: 386 us -> 405 us (1.049)
  Pallas kernels: 0 us -> 50 us
  starting transfers between devices: 38.8 us -> 16.8 us
  waiting for transfers between devices: 23.9 us -> 3.87 us
  local copies, waits for them, and re-layouts: 110 us -> 120 us
  other arithmetic: 156 us -> 161 us
  blocking collectives: 4.98 us -> 0 us
    pallas_call x0 -> x3, Pallas kernels: none -> 50 us  [direct_exchange(): pl.pallas_call(kernel, out_shape=jax.ShapeDtypeStruct(pieces.shape, piece...]
    all_to_all x3 -> x0, starting transfers between devices: 21.6 us -> none  [the longest x1 11.1 us: on_device(): lax.all_to_all(requests, LAT_LON, split_axis=0, concat_axis=0, tiled=True)]
    all_to_all x3 -> x0, waiting for transfers between devices: 20.1 us -> none  [the longest x1 10.3 us: on_device(): lax.all_to_all(outgoing.astype(jnp.bfloat16), LAT_LON, split_axis=0, conc...]
    all_to_all x1 -> x0, blocking collectives: 4.98 us -> none  [turned_blocks(): whole = lax.all_to_all(whole, axes[k], k, k, tiled=True)]
    another operation x1 -> x5, local copies, waits for them, and re-layouts: 0.88 us -> 4.94 us  [locate(): jnp.stack([base_cell, base_cell + 1, base_cell + tile_cols, base_cell + t...]
    unnamed x144 -> x138, local copies, waits for them, and re-layouts: 13.2 us -> 12.7 us
  transfers between devices with their start and end apart: 11 -> 8, of which waited for: 5 -> 2; matrix products, arithmetic and copies ran while one was open for 3% -> 6% of each run, Pallas kernels for 0% -> 5%
where the time goes in v1:
time: 405 us; the launch traced here: 398 us
  other arithmetic  161 us (40%)
  local copies, waits for them, and re-layouts  120 us (30%)
  Pallas kernels  50 us (12%)
  matrix products  43.9 us (11%)
  starting transfers between devices  16.8 us (4%)
    pallas_call x3, Pallas kernels, direct_exchange(): pl.pallas_call(kernel, out_shape=jax.ShapeDtypeStruct(pieces.shape, piece...  50 us
    dot_general x2, matrix products, convolve(): lax.dot_general(flat, taps, (((1,), (contract,)), ((), ())), preferred_el...  37.3 us
    scatter-add x1, other arithmetic, station_forward(): near_keys = key_rows[neighbours].reshape(station_rows, -1, HEADS, HEAD_DIM)  23.4 us
    scatter-add x1, other arithmetic, station_forward(): value_rows[neighbours].reshape(station_rows, -1, HEADS, HEAD_DIM)  23.2 us
    convert_element_type x1, other arithmetic, on_device(): (grid_field.astype(jnp.float32) + jax.nn.silu(pre_act)).astype(jnp.bfloat16)  17.5 us
    gather x1, local copies, waits for them, and re-layouts, station_forward(): value_rows[neighbours].reshape(station_rows, -1, HEADS, HEAD_DIM)  17.3 us
    reshape x2, local copies, waits for them, and re-layouts, station_forward(): value_rows[neighbours].reshape(station_rows, -1, HEADS, HEAD_DIM)  17.1 us
    add x1, other arithmetic, on_device(): d_field + convolve(d_ext, conv_weight, tile_rows, tile_cols, 2, True)  17.1 us
  transfers between devices with their start and end apart: 8, of which 2 were waited for; matrix products, arithmetic and copies ran while one was open for 6% of the time, Pallas kernels for 5%

profile of v1, /device:TPU:0, one launch (start us, length us, event | category | flops | bytes accessed | tf_op | source)
XLA Modules:
  0.0 398.0 jit_solution(16868483022172189250)
XLA Ops:
  0.7 3.2 copy.389
  4.7 1.6 collective-permute-start
  6.2 1.7 collective-permute-start.1
  9.4 1.6 scatter_custom_fusion
  11.1 18.0 %exchange_0.1 = s32[128,1,128]{2,1,0:T(1,128)S(1)} custom-call(s32[128,1,128]{2,1,0:T(1,128)S(1)} %bitcast.120), custom_call_target="tpu_custom_call" | custom-call | tf_op jit(solution)/shard_map/exchange_0/pallas_call | solution.py:68
  33.7 0.9 pad_add_fusion
  34.6 1.6 copy.412
  36.2 1.2 reshape.456
  38.0 0.9 copy.396
  38.9 0.9 copy.395
  39.8 0.9 copy.394
  42.6 1.6 pad_maximum_fusion
  45.6 5.1 %collective-permute-start.3 = (bf16[34,1,192]{2,1,0:T(2,128)(2,1)S(1)}, bf16[34,1,192]{2,1,0:T(2,128)(2,1)S(1)}, u32[]{:S(2)}, u32[]{:S(2)}) collective-permute-start(bf16[34,1,192]{2,1,0:T(2,128)(2,1)S(1)} %get-tuple-element.82), channel_id=1, source_target_pairs={{1,0},{2,1},{3,2},{4,3},{5,4},{6,5},{7,6},{8,7},{9,8},{10,9},{11,1... | collective-permute-start | bytes 39176 | tf_op jit(solution)/shard_map/ppermute | solution.py:102
  51.3 0.9 copy.399
  53.2 2.6 copy.413
  55.8 1.8 mul.355
  58.2 18.7 %fusion.6 = f32[34,130,9,192]{3,1,2,0:T(8,128)} fusion(bf16[34,1,192]{2,1,0:T(2,128)(2,1)S(1)} %collective-permute-done.3, bf16[1,128,192]{2,1,0:T(8,128)(2,1)} %collective-permute-done.1, bf16[32,128,192]{2,1,0:T(8,128)(2,1)S(1)} %copy.389, bf16[1,128,192]{2,1,0:T(8,128)(2,1)} %collective-permute-done, bf16[34,1,192]{2,1,0:T(2,128)(2,1)S(1)} %collective-permute-done.2, ...), kind=kOutput, calls=%fused_computation.43 | convolution fusion | flops 2943083520 | bytes 32911940 | tf_op jit(solution)/shard_map/dot_general | solution.py:148
  76.9 17.5 %add_convert_fusion = (bf16[32,128,192]{2,1,0:T(8,128)(2,1)S(1)}, f32[32,128,192]{2,1,0:T(8,128)}) fusion(bf16[32,128,192]{2,1,0:T(8,128)(2,1)} %copy-done.3, f32[34,130,9,192]{3,1,2,0:T(8,128)} %fusion.6), kind=kLoop, calls=%fused_computation.37 | loop fusion | flops 11796480 | bytes 34603008 | tf_op jit(solution)/shard_map/convert_element_type | solution.py:278
  94.4 9.1 %gather_fusion = bf16[2048,192]{1,0:T(8,128)(2,1)} fusion(bf16[4096,192]{1,0:T(8,128)(2,1)S(1)} %bitcast.121, s32[2048]{0:T(1024)S(1)} %broadcast_clamp_fusion.1), kind=kCustom, calls=%fused_computation | custom fusion | bytes 1581056 | tf_op jit(solution)/shard_map/gather | solution.py:296
  103.4 1.6 reshape.560
  105.1 2.8 fusion.127
  107.8 1.3 copy.398
  109.1 1.2 copy.404
  110.4 1.2 copy.402
  112.5 16.1 %exchange_1.1 = bf16[128,8,128]{2,1,0:T(8,128)(2,1)S(1)} custom-call(bf16[128,8,128]{2,1,0:T(8,128)(2,1)S(1)} %copy.467.x_ref), custom_call_target="tpu_custom_call" | custom-call | tf_op jit(solution)/shard_map/exchange_1/pallas_call | solution.py:68
  128.9 1.3 gather_fusion.1
  131.3 0.9 copy.471
  132.6 14.6 %gather_fusion.2 = bf16[4096,192]{1,0:T(8,128)(2,1)S(1)} fusion(bf16[256,192]{1,0:T(8,128)(2,1)S(1)} %copy.408, s32[4096]{0:T(1024)S(1)} %broadcast_clamp_fusion), kind=kCustom, calls=%fused_computation.2 | custom fusion | bytes 3162112 | tf_op jit(solution)/shard_map/jvp()/gather | solution.py:221
  147.2 17.3 %gather_fusion.3 = bf16[4096,192]{1,0:T(8,128)(2,1)} fusion(bf16[256,192]{1,0:T(8,128)(2,1)S(1)} %copy.410, s32[4096]{0:T(1024)S(1)} %broadcast_clamp_fusion), kind=kCustom, calls=%fused_computation.3 | custom fusion | bytes 3162112 | tf_op jit(solution)/shard_map/jvp()/gather | solution.py:222
  164.4 8.6 %reshape.455 = bf16[256,16,3,64]{3,2,1,0:T(4,128)(2,1)} reshape(bf16[4096,192]{1,0:T(8,128)(2,1)} %gather_fusion.3) | data formatting | bytes 3145728 | tf_op jit(solution)/shard_map/jvp()/reshape | solution.py:222
  173.0 4.0 reshape.453
  177.0 6.9 %multiply_reduce_fusion.3 = f32[256,3,16]{1,2,0:T(8,128)S(1)} fusion(f32[256,3,64]{2,1,0:T(4,128)} %copy.471, bf16[256,16,3,64]{3,2,1,0:T(4,128)(2,1)} %reshape.453), kind=kLoop, calls=%fused_computation.12 | loop fusion | flops 2347008 | bytes 1818624 | tf_op jit(solution)/shard_map/jvp(shd,skhd->shk)/dot_general | solution.py:227
  183.9 1.6 fusion.35
  185.5 1.6 fusion.117
  187.8 3.6 convert_reduce_fusion
  192.1 8.8 %multiply_reduce_fusion.2 = f32[256,3,64]{2,1,0:T(4,128)} fusion(f32[256,3,16]{1,2,0:T(8,128)} %get-tuple-element.78, bf16[256,16,3,64]{3,2,1,0:T(4,128)(2,1)} %reshape.455), kind=kLoop, calls=%fused_computation.11 | loop fusion | flops 2310144 | bytes 1818624
  200.9 1.2 copy.451
  202.2 1.1 multiply_reduce_fusion.6
  203.4 0.9 convolution_multiply_fusion
  204.3 1.3 multiply_reduce_fusion.5
  205.7 1.8 fusion.70
  208.2 1.9 copy.414
  210.0 1.0 copy.415
  211.8 12.3 %fusion = (bf16[256,16,3,64]{3,2,1,0:T(4,128)(2,1)}, bf16[256,3,16]{1,2,0:T(8,128)(2,1)}) fusion(f32[256,3,16]{1,2,0:T(8,128)} %get-tuple-element.78, f32[256,3,64]{2,1,0:T(4,128)} %copy.414, bf16[256,16,3,64]{3,2,1,0:T(4,128)(2,1)} %reshape.455), kind=kLoop, calls=%fused_computation.15 | loop fusion | flops 3919872 | bytes 3416064 | tf_op jit(solution)/shard_map/transpose(jvp(shk,skhd->shd))/convert_element_type | solution.py:242
  224.1 8.5 %reshape.519 = bf16[4096,192]{1,0:T(8,128)(2,1)} reshape(bf16[256,16,3,64]{3,2,1,0:T(4,128)(2,1)} %get-tuple-element.93) | data formatting | bytes 3145728 | tf_op jit(solution)/shard_map/transpose(jvp())/reshape | solution.py:222
  232.7 3.3 fusion.28
  236.1 2.0 fusion.119
  239.2 1.3 copy-done.1
  240.6 6.4 %fusion.1 = (bf16[256,16,3,64]{3,2,1,0:T(4,128)(2,1)}, bf16[256,3,64]{2,1,0:T(4,128)(2,1)S(1)}) fusion(f32[256,3,64]{2,1,0:T(4,128)S(1)} %copy-done.6, f32[256,3,16]{1,2,0:T(8,128)S(1)} %select_multiply_fusion, bf16[256,16,3,64]{3,2,1,0:T(4,128)(2,1)S(1)} %copy-done.1), kind=kLoop, calls=%fused_computation.16 | loop fusion | flops 3883008 | bytes 3489792 | tf_op jit(solution)/shard_map/transpose(jvp(shd,skhd->shk))/convert_element_type | solution.py:227
  247.2 8.5 %reshape.527 = bf16[4096,192]{1,0:T(8,128)(2,1)} reshape(bf16[256,16,3,64]{3,2,1,0:T(4,128)(2,1)} %get-tuple-element.85) | data formatting | bytes 3145728 | tf_op jit(solution)/shard_map/transpose(jvp())/reshape | solution.py:221
  256.1 23.2 %scatter_fusion = bf16[256,192]{1,0:T(8,128)(2,1)S(1)} fusion(bf16[256,192]{1,0:T(8,128)(2,1)S(1)} %copy.415, s32[4096]{0:T(1024)S(1)} %reshape.493, bf16[4096,192]{1,0:T(8,128)(2,1)} %reshape.519), kind=kCustom, calls=%fused_computation.5 | custom fusion | flops 786432 | bytes 4734976 | tf_op jit(solution)/shard_map/transpose(jvp())/scatter-add | solution.py:222
  279.4 23.4 %scatter_fusion.1 = bf16[256,192]{1,0:T(8,128)(2,1)S(1)} fusion(bf16[256,192]{1,0:T(8,128)(2,1)S(1)} %copy.420, s32[4096]{0:T(1024)S(1)} %reshape.493, bf16[4096,192]{1,0:T(8,128)(2,1)} %reshape.527), kind=kCustom, calls=%fused_computation.6 | custom fusion | flops 786432 | bytes 4734976 | tf_op jit(solution)/shard_map/transpose(jvp())/scatter-add | solution.py:221
  303.7 1.7 scatter_custom_fusion.3
  305.7 15.9 %exchange_2.1 = bf16[128,8,128]{2,1,0:T(8,128)(2,1)S(1)} custom-call(bf16[128,8,128]{2,1,0:T(8,128)(2,1)S(1)} %reshape.463.x_ref), custom_call_target="tpu_custom_call" | custom-call | tf_op jit(solution)/shard_map/exchange_2/pallas_call | solution.py:68
  322.6 1.7 mul.392
  324.3 15.2 %scatter_custom_fusion.4 = f32[4096,192]{1,0:T(8,128)} fusion(s32[2048]{0:T(1024)} %bitcast.144, f32[2048,192]{1,0:T(8,128)} %mul.392, f32[]{:T(128)} %constant.191.clone.1, f32[2048]{0:T(1024)S(1)} %copy-done.50), kind=kCustom, calls=%fused_computation.67 | custom fusion | flops 786432 | bytes 5251584 | tf_op jit(solution)/shard_map/scatter-add | solution.py:338
  339.5 4.9 %multiply_convert_fusion.2 = bf16[32,128,192]{2,1,0:T(8,128)(2,1)S(1)} fusion(f32[32,128,192]{2,1,0:T(8,128)} %get-tuple-element.77, f32[32,128,192]{2,1,0:T(8,128)} %bitcast.122), kind=kLoop, calls=%fused_computation.36 | loop fusion | flops 7077888 | bytes 7864320 | tf_op jit(solution)/shard_map/convert_element_type | solution.py:342
  345.3 2.5 collective-permute-start.5
  347.8 2.2 collective-permute-done.4
  350.2 5.1 %collective-permute-start.7 = (bf16[34,1,192]{2,1,0:T(2,128)(2,1)S(1)}, bf16[34,1,192]{2,1,0:T(2,128)(2,1)S(1)}, u32[]{:S(2)}, u32[]{:S(2)}) collective-permute-start(bf16[34,1,192]{2,1,0:T(2,128)(2,1)S(1)} %get-tuple-element.80), channel_id=1, source_target_pairs={{1,0},{2,1},{3,2},{4,3},{5,4},{6,5},{7,6},{8,7},{9,8},{10,9},{11,1... | collective-permute-start | bytes 39176 | tf_op jit(solution)/shard_map/ppermute | solution.py:102
  355.2 1.6 collective-permute-done.6
  356.8 18.6 %fusion.17 = f32[34,130,9,192]{3,1,0,2:T(8,128)} fusion(bf16[34,1,192]{2,1,0:T(2,128)(2,1)S(1)} %collective-permute-done.7, bf16[1,128,192]{2,1,0:T(8,128)(2,1)S(1)} %collective-permute-done.5, bf16[32,128,192]{2,1,0:T(8,128)(2,1)} %copy-done.4, bf16[1,128,192]{2,1,0:T(8,128)(2,1)S(1)} %collective-permute-done.4, ...), kind=kOutput, calls=%fused_computation.54 | convolution fusion | flops 2943083520 | bytes 32911940 | tf_op jit(solution)/shard_map/dot_general | solution.py:148
  375.5 17.1 %fusion.3 = f32[32,128,192]{2,1,0:T(8,128)} fusion(f32[32,128,192]{2,1,0:T(8,128)S(1)} %bitcast.123, f32[34,130,9,192]{3,1,0,2:T(8,128)} %fusion.17), kind=kLoop, calls=%fused_computation.19 | loop fusion | flops 7077888 | bytes 34603008 | tf_op jit(solution)/shard_map/add | solution.py:344
  392.5 5.3 %copy.432 = f32[32,128,192]{1,2,0:T(8,128)} copy(f32[32,128,192]{2,1,0:T(8,128)} %fusion.3) | data formatting | bytes 6291456
  (223 shorter events, 22.6 us)
Async XLA Ops:
  0.6 57.6 %copy-start = (bf16[9,192,192]{2,1,0:T(8,128)(2,1)S(1)}, bf16[9,192,192]{2,1,0:T(8,128)(2,1)}, u32[]{:S(2)}) copy-start(bf16[9,192,192]{2,1,0:T(8,128)(2,1)} %param.25) | copy-start | bytes 1990660
  0.6 7.9 %copy-start.66 = (s32[256,1]{0,1:T(1,128)S(1)}, s32[256,1]{0,1:T(1,128)}, u32[]{:S(2)}) copy-start(s32[256,1]{0,1:T(1,128)} %param.28) | copy-start | bytes 3076
  0.7 8.8 %copy-start.48 = (s32[256,16]{0,1:T(8,128)S(1)}, s32[256,16]{0,1:T(8,128)}, u32[]{:S(2)}) copy-start(s32[256,16]{0,1:T(8,128)} %param.30) | copy-start | bytes 49156
  0.7 28.5 %copy-start.35 = (s32[256,128]{1,0:T(8,128)S(1)}, s32[256,128]{1,0:T(8,128)}, u32[]{:S(2)}) copy-start(s32[256,128]{1,0:T(8,128)} %param.27) | copy-start | bytes 393220
  0.7 29.1 %copy-start.39 = (f32[256,128]{1,0:T(8,128)S(1)}, f32[256,128]{1,0:T(8,128)}, u32[]{:S(2)}) copy-start(f32[256,128]{1,0:T(8,128)} %param.26) | copy-start | bytes 393220
  3.9 53.7 %copy-start.3 = (bf16[32,128,192]{2,1,0:T(8,128)(2,1)}, bf16[32,128,192]{2,1,0:T(8,128)(2,1)S(1)}, u32[]{:S(2)}) copy-start(bf16[32,128,192]{2,1,0:T(8,128)(2,1)S(1)} %copy.389) | copy-start | bytes 4718596
  4.7 40.0 %collective-permute-start = (bf16[1,128,192]{2,1,0:T(8,128)(2,1)}, bf16[1,128,192]{2,1,0:T(8,128)(2,1)}, u32[]{:S(2)}, u32[]{:S(2)}) collective-permute-start(bf16[1,128,192]{2,1,0:T(8,128)(2,1)} %get-tuple-element.91), channel_id=1, source_target_pairs={{0,32},{32,64},{64,96},{96,0},{1,33},{33,65},{65,97},{97,1},{2,34}... | collective-permute-start | bytes 147464 | tf_op jit(solution)/shard_map/ppermute | solution.py:100
  6.2 38.5 %collective-permute-start.1 = (bf16[1,128,192]{2,1,0:T(8,128)(2,1)}, bf16[1,128,192]{2,1,0:T(8,128)(2,1)}, u32[]{:S(2)}, u32[]{:S(2)}) collective-permute-start(bf16[1,128,192]{2,1,0:T(8,128)(2,1)} %get-tuple-element.92), channel_id=1, source_target_pairs={{32,0},{64,32},{96,64},{0,96},{33,1},{65,33},{97,65},{1,97},{34,2}... | collective-permute-start | bytes 147464 | tf_op jit(solution)/shard_map/ppermute | solution.py:102
  34.6 17.6 %copy-start.37 = (f32[128,4]{1,0:T(8,128)S(1)}, f32[128,4]{1,0:T(8,128)}, u32[]{:S(2)}) copy-start(f32[128,4]{1,0:T(8,128)} %get-tuple-element.99) | copy-start | bytes 6148
  34.6 18.5 %copy-start.53 = (f32[256,16]{0,1:T(8,128)S(1)}, f32[256,16]{0,1:T(8,128)}, u32[]{:S(2)}) copy-start(f32[256,16]{0,1:T(8,128)} %param.32) | copy-start | bytes 49156
  45.5 12.2 %collective-permute-start.2 = (bf16[34,1,192]{2,1,0:T(2,128)(2,1)S(1)}, bf16[34,1,192]{2,1,0:T(2,128)(2,1)S(1)}, u32[]{:S(2)}, u32[]{:S(2)}) collective-permute-start(bf16[34,1,192]{2,1,0:T(2,128)(2,1)S(1)} %get-tuple-element.81), channel_id=1, source_target_pairs={{0,1},{1,2},{2,3},{3,4},{4,5},{5,6},{6,7},{7,8},{8,9},{9,10},{10,1... | collective-permute-start | bytes 39176 | tf_op jit(solution)/shard_map/ppermute | solution.py:100
  45.6 12.1 %collective-permute-start.3 = (bf16[34,1,192]{2,1,0:T(2,128)(2,1)S(1)}, bf16[34,1,192]{2,1,0:T(2,128)(2,1)S(1)}, u32[]{:S(2)}, u32[]{:S(2)}) collective-permute-start(bf16[34,1,192]{2,1,0:T(2,128)(2,1)S(1)} %get-tuple-element.82), channel_id=1, source_target_pairs={{1,0},{2,1},{3,2},{4,3},{5,4},{6,5},{7,6},{8,7},{9,8},{10,9},{11,1... | collective-permute-start | bytes 39176 | tf_op jit(solution)/shard_map/ppermute | solution.py:102
  53.2 134.6 %copy-start.7 = (f32[256,16]{1,0:T(8,128)}, f32[256,16]{1,0:T(8,128)S(1)}, u32[]{:S(2)}) copy-start(f32[256,16]{1,0:T(8,128)S(1)} %copy.409) | copy-start | bytes 49156
  107.8 3.8 copy-start.20
  112.1 18.1 %copy-start.46 = (bf16[256,128]{1,0:T(8,128)(2,1)S(1)}, bf16[256,128]{1,0:T(8,128)(2,1)}, u32[]{:S(2)}) copy-start(bf16[256,128]{1,0:T(8,128)(2,1)} %convert_convert_fusion) | copy-start | bytes 196612
  112.1 18.1 %copy-start.47 = (bf16[256,128]{1,0:T(8,128)(2,1)S(1)}, bf16[256,128]{1,0:T(8,128)(2,1)}, u32[]{:S(2)}) copy-start(bf16[256,128]{1,0:T(8,128)(2,1)} %multiply_convert_fusion.6) | copy-start | bytes 196612
  112.2 18.0 %copy-start.43 = (bf16[448,192]{0,1:T(8,128)(2,1)S(1)}, bf16[448,192]{0,1:T(8,128)(2,1)}, u32[]{:S(2)}) copy-start(bf16[448,192]{0,1:T(8,128)(2,1)} %param.34) | copy-start | bytes 516100
  112.2 18.3 %copy-start.41 = (bf16[192,576]{1,0:T(8,128)(2,1)S(1)}, bf16[192,576]{1,0:T(8,128)(2,1)}, u32[]{:S(2)}) copy-start(bf16[192,576]{1,0:T(8,128)(2,1)} %param.36) | copy-start | bytes 663556
  112.2 18.3 %copy-start.64 = (f32[192]{0:T(256)S(1)}, f32[192]{0:T(256)}, u32[]{:S(2)}) copy-start(f32[192]{0:T(256)} %param.35) | copy-start | bytes 2308
  132.4 54.7 %copy-start.13 = (f32[256,3]{1,0:T(8,128)}, f32[256,3]{1,0:T(8,128)S(1)}, u32[]{:S(2)}) copy-start(f32[256,3]{1,0:T(8,128)S(1)} %copy.444) | copy-start | bytes 9220
  177.0 6.9 %copy-start.26 = (pred[256,16]{1,0:T(8,128)(4,1)S(1)}, pred[256,16]{1,0:T(8,128)(4,1)}, u32[]{:S(2)}) copy-start(pred[256,16]{1,0:T(8,128)(4,1)} %copy.406) | copy-start | bytes 12292
  185.5 5.9 %copy-start.11 = (f32[256,3]{1,0:T(8,128)}, f32[256,3]{1,0:T(8,128)S(1)}, u32[]{:S(2)}) copy-start(f32[256,3]{1,0:T(8,128)S(1)} %fusion.35) | copy-start | bytes 9220
  185.5 5.9 %copy-start.15 = (f32[256,3]{1,0:T(8,128)}, f32[256,3]{1,0:T(8,128)S(1)}, u32[]{:S(2)}) copy-start(f32[256,3]{1,0:T(8,128)S(1)} %multiply_maximum_fusion) | copy-start | bytes 9220
  187.8 3.6 copy-start.9
  187.8 3.6 copy-start.17
  192.1 10.0 %copy-start.33 = (bf16[256,192]{0,1:T(8,128)(2,1)S(1)}, bf16[256,192]{0,1:T(8,128)(2,1)}, u32[]{:S(2)}) copy-start(bf16[256,192]{0,1:T(8,128)(2,1)} %copy-done.32) | copy-start | bytes 294916
  192.1 10.1 %copy-start.49 = (f32[256,3]{0,1:T(4,128)S(1)}, f32[256,3]{0,1:T(4,128)}, u32[]{:S(2)}) copy-start(f32[256,3]{0,1:T(4,128)} %copy.411) | copy-start | bytes 9220
  192.1 10.1 %copy-start.22 = (f32[256,192]{0,1:T(8,128)S(1)}, f32[256,192]{0,1:T(8,128)}, u32[]{:S(2)}) copy-start(f32[256,192]{0,1:T(8,128)} %copy-done.21) | copy-start | bytes 589828
  192.1 11.3 %copy-start.45 = (bf16[192,128]{1,0:T(8,128)(2,1)S(1)}, bf16[192,128]{1,0:T(8,128)(2,1)}, u32[]{:S(2)}) copy-start(bf16[192,128]{1,0:T(8,128)(2,1)} %param.39) | copy-start | bytes 147460
  192.1 11.3 %copy-start.60 = (f32[192]{0:T(256)S(1)}, f32[192]{0:T(256)}, u32[]{:S(2)}) copy-start(f32[192]{0:T(256)} %param.38) | copy-start | bytes 2308
  203.4 20.7 %copy-start.51 = (f32[256]{0:T(256)}, f32[256]{0:T(256)S(1)}, u32[]{:S(2)}) copy-start(f32[256]{0:T(256)S(1)} %fusion.112) | copy-start | bytes 3076
  205.7 4.3 %copy-start.24 = (f32[256,192]{0,1:T(8,128)}, f32[256,192]{0,1:T(8,128)S(1)}, u32[]{:S(2)}) copy-start(f32[256,192]{0,1:T(8,128)S(1)} %get-tuple-element.111) | copy-start | bytes 589828
  205.7 18.4 %copy-start.56 = (f32[256]{0:T(256)}, f32[256]{0:T(256)S(1)}, u32[]{:S(2)}) copy-start(f32[256]{0:T(256)S(1)} %multiply_multiply_fusion.1) | copy-start | bytes 3076
  224.1 8.6 %copy-start.8 = (f32[256,16]{1,0:T(8,128)S(1)}, f32[256,16]{1,0:T(8,128)}, u32[]{:S(2)}) copy-start(f32[256,16]{1,0:T(8,128)} %copy-done.7) | copy-start | bytes 49156
  224.1 8.6 %copy-start.27 = (pred[256,16]{1,0:T(8,128)(4,1)S(1)}, pred[256,16]{1,0:T(8,128)(4,1)}, u32[]{:S(2)}) copy-start(pred[256,16]{1,0:T(8,128)(4,1)} %copy.406) | copy-start | bytes 12292
  232.6 3.3 copy-start.10
  232.6 3.3 copy-start.18
  232.6 3.3 copy-start.34
  232.6 3.4 copy-start.5
  232.6 3.4 copy-start.16
  236.1 2.1 copy-start.12
  236.1 2.1 copy-start.14
  236.1 2.2 copy-start.40
  236.1 2.2 copy-start.19
  238.3 2.2 copy-start.1
  238.3 2.3 copy-start.6
  240.6 6.5 %copy-start.31 = (bf16[256,192]{0,1:T(8,128)(2,1)S(1)}, bf16[256,192]{0,1:T(8,128)(2,1)}, u32[]{:S(2)}) copy-start(bf16[256,192]{0,1:T(8,128)(2,1)} %copy-done.30) | copy-start | bytes 294916
  247.1 8.8 %copy-start.29 = (bf16[256,192]{0,1:T(8,128)(2,1)S(1)}, bf16[256,192]{0,1:T(8,128)(2,1)}, u32[]{:S(2)}) copy-start(bf16[256,192]{0,1:T(8,128)(2,1)} %copy-done.28) | copy-start | bytes 294916
  279.3 23.5 %copy-start.23 = (f32[256,192]{0,1:T(8,128)S(1)}, f32[256,192]{0,1:T(8,128)}, u32[]{:S(2)}) copy-start(f32[256,192]{0,1:T(8,128)} %copy-done.21) | copy-start | bytes 589828
  279.3 23.5 %copy-start.42 = (bf16[192,576]{1,0:T(8,128)(2,1)S(1)}, bf16[192,576]{1,0:T(8,128)(2,1)}, u32[]{:S(2)}) copy-start(bf16[192,576]{1,0:T(8,128)(2,1)} %param.36) | copy-start | bytes 663556
  279.3 23.5 %copy-start.65 = (f32[192]{0:T(256)S(1)}, f32[192]{0:T(256)}, u32[]{:S(2)}) copy-start(f32[192]{0:T(256)} %param.35) | copy-start | bytes 2308
  279.3 23.9 %copy-start.63 = (f32[256]{0:T(256)S(1)}, f32[256]{0:T(256)}, u32[]{:S(2)}) copy-start(f32[256]{0:T(256)} %copy-done.62) | copy-start | bytes 3076
  279.3 23.9 %copy-start.25 = (f32[256,192]{0,1:T(8,128)S(1)}, f32[256,192]{0,1:T(8,128)}, u32[]{:S(2)}) copy-start(f32[256,192]{0,1:T(8,128)} %copy-done.24) | copy-start | bytes 589828
  279.3 23.9 %copy-start.44 = (bf16[448,192]{0,1:T(8,128)(2,1)S(1)}, bf16[448,192]{0,1:T(8,128)(2,1)}, u32[]{:S(2)}) copy-start(bf16[448,192]{0,1:T(8,128)(2,1)} %param.34) | copy-start | bytes 516100
  279.3 23.9 %copy-start.52 = (f32[256]{0:T(256)S(1)}, f32[256]{0:T(256)}, u32[]{:S(2)}) copy-start(f32[256]{0:T(256)} %copy-done.51) | copy-start | bytes 3076
  279.3 23.9 %copy-start.57 = (f32[256]{0:T(256)S(1)}, f32[256]{0:T(256)}, u32[]{:S(2)}) copy-start(f32[256]{0:T(256)} %copy-done.56) | copy-start | bytes 3076
  279.3 23.9 %copy-start.59 = (f32[256]{0:T(256)S(1)}, f32[256]{0:T(256)}, u32[]{:S(2)}) copy-start(f32[256]{0:T(256)} %copy-done.58) | copy-start | bytes 3076
  344.4 12.4 %copy-start.4 = (bf16[32,128,192]{2,1,0:T(8,128)(2,1)}, bf16[32,128,192]{2,1,0:T(8,128)(2,1)S(1)}, u32[]{:S(2)}) copy-start(bf16[32,128,192]{2,1,0:T(8,128)(2,1)S(1)} %multiply_convert_fusion.2) | copy-start | bytes 4718596
  344.4 12.4 %copy-start.55 = (bf16[34]{0:T(256)(128)(2,1)S(1)}, bf16[34]{0:T(256)(128)(2,1)}, u32[]{:S(2)}) copy-start(bf16[34]{0:T(256)(128)(2,1)} %copy-done.54) | copy-start | bytes 208
  344.4 5.5 %collective-permute-start.4 = (bf16[1,128,192]{2,1,0:T(8,128)(2,1)S(1)}, bf16[1,128,192]{2,1,0:T(8,128)(2,1)S(1)}, u32[]{:S(2)}, u32[]{:S(2)}) collective-permute-start(bf16[1,128,192]{2,1,0:T(8,128)(2,1)S(1)} %get-tuple-element.83), channel_id=1, source_target_pairs={{0,32},{32,64},{64,96},{96,0},{1,33},{33,65},{65,97},{97,1},{2,34}... | collective-permute-start | bytes 147464 | tf_op jit(solution)/shard_map/ppermute | solution.py:100
  345.3 4.7 %collective-permute-start.5 = (bf16[1,128,192]{2,1,0:T(8,128)(2,1)S(1)}, bf16[1,128,192]{2,1,0:T(8,128)(2,1)S(1)}, u32[]{:S(2)}, u32[]{:S(2)}) collective-permute-start(bf16[1,128,192]{2,1,0:T(8,128)(2,1)S(1)} %get-tuple-element.84), channel_id=1, source_target_pairs={{32,0},{64,32},{96,64},{0,96},{33,1},{65,33},{97,65},{1,97},{34,2}... | collective-permute-start | bytes 147464 | tf_op jit(solution)/shard_map/ppermute | solution.py:102
  350.1 6.8 %collective-permute-start.6 = (bf16[34,1,192]{2,1,0:T(2,128)(2,1)S(1)}, bf16[34,1,192]{2,1,0:T(2,128)(2,1)S(1)}, u32[]{:S(2)}, u32[]{:S(2)}) collective-permute-start(bf16[34,1,192]{2,1,0:T(2,128)(2,1)S(1)} %get-tuple-element.79), channel_id=1, source_target_pairs={{0,1},{1,2},{2,3},{3,4},{4,5},{5,6},{6,7},{7,8},{8,9},{9,10},{10,1... | collective-permute-start | bytes 39176 | tf_op jit(solution)/shard_map/ppermute | solution.py:100
  350.2 6.7 %collective-permute-start.7 = (bf16[34,1,192]{2,1,0:T(2,128)(2,1)S(1)}, bf16[34,1,192]{2,1,0:T(2,128)(2,1)S(1)}, u32[]{:S(2)}, u32[]{:S(2)}) collective-permute-start(bf16[34,1,192]{2,1,0:T(2,128)(2,1)S(1)} %get-tuple-element.80), channel_id=1, source_target_pairs={{1,0},{2,1},{3,2},{4,3},{5,4},{6,5},{7,6},{8,7},{9,8},{10,9},{11,1... | collective-permute-start | bytes 39176 | tf_op jit(solution)/shard_map/ppermute | solution.py:102
  356.8 18.6 %copy-start.2 = (f32[4096,192]{1,0:T(8,128)S(1)}, f32[4096,192]{1,0:T(8,128)}, u32[]{:S(2)}) copy-start(f32[4096,192]{1,0:T(8,128)} %scatter_custom_fusion.4) | copy-start | bytes 9437188
  (11 other events, 13.3 us)

commit v2 on v0

v2 whole, which is shorter than its diff:
```python
import jax
import jax.numpy as jnp
from jax import lax
from jax.experimental import pallas as pl
from jax.experimental.pallas import tpu as pltpu
from jax.sharding import PartitionSpec as P

CH = 192
HEADS = 3
HEAD_DIM = 64
ROWS = 32
COLS = 128
FINE = 4 * (COLS - 1)
CAP = 4
N = 128
N_LAT = 4
N_LON = 32
SLOTS = N * CAP
STATIONS = 256
TAPS = 9 * CH
DEPTH = TAPS + 2 * ROWS
EPS = 1e-06
F32 = jnp.float32
BF16 = jnp.bfloat16
LAT_LON = ("lat", "lon")


def nn(a, b):
    return lax.dot_general(a, b, (((1,), (0,)), ((), ())), preferred_element_type=F32)


def nt(a, b):
    return lax.dot_general(a, b, (((1,), (1,)), ((), ())), preferred_element_type=F32)


def lane_iota(shape):
    return lax.broadcasted_iota(jnp.int32, shape, len(shape) - 1)


def row_iota(shape):
    return lax.broadcasted_iota(jnp.int32, shape, len(shape) - 2)


def as_columns(row):
    return jnp.transpose(jnp.broadcast_to(row, (128, row.shape[1])))


def kernel(
    x_ref,
    conv_ref,
    observed_ref,
    mask_ref,
    tile_ref,
    spot_ref,
    neighbours_ref,
    count_ref,
    bias_ref,
    live_ref,
    in_ref,
    gain1_ref,
    qkv_ref,
    out_ref,
    gain2_ref,
    head_ref,
    predicted_ref,
    grad_ref,
    shifted,
    taps_f,
    taps_b,
    field,
    slope,
    spread,
    answer_out,
    answer_in,
    grads_out,
    grads_in,
    ask_out,
    ask_in,
    wide,
    row_in,
    side_out,
    side_in,
    corner_in,
    select,
    select_t,
    scores_bias,
    grads_t,
    embedded0,
    gain1,
    gain2,
    in_low,
    in_low_t,
    qkv_t,
    out_t,
    head_t,
    mask_t,
    observed_t,
    halo_send,
    halo_recv,
    a2a_send,
    a2a_recv,
):
    lat = lax.axis_index("lat")
    lon = lax.axis_index("lon")
    me = lat * N_LON + lon
    barrier = pltpu.get_barrier_semaphore()

    def coords(peer):
        return (peer // N_LON, lax.rem(peer, N_LON))

    def greet(i, carry):
        pl.semaphore_signal(
            barrier, inc=1, device_id=coords(lax.rem(me + i, N)), device_id_type=pl.DeviceIdType.MESH
        )
        return carry

    lax.fori_loop(1, N, greet, 0)

    tile_row = tile_ref[...].astype(F32)
    tile_cols = as_columns(tile_row)
    tile_cols = jnp.concatenate([tile_cols, tile_cols], axis=1)
    square = (STATIONS, STATIONS)
    same = (tile_cols == tile_row) & (row_iota(square) < lane_iota(square))
    rank = jnp.sum(same.astype(F32), axis=0, keepdims=True)
    slot = tile_row * CAP + rank
    spot = spot_ref[...].astype(F32)
    spot_high = jnp.floor(spot * (1.0 / 256.0))
    spot_low = spot - 256.0 * spot_high
    part = row_iota((128, STATIONS))
    wanted = jnp.where(part < CAP, spot_high, spot_low)
    wanted = jnp.where((part & (CAP - 1)).astype(F32) == rank, wanted, 0.0)
    wanted = jnp.where(part < 2 * CAP, wanted, 0.0).astype(BF16)
    is_tile = (row_iota((N, STATIONS)).astype(F32) == tile_row).astype(BF16)
    ask_out[...] = nt(is_tile, wanted).reshape(N, 1, 128)

    def fill_shifted(y, value):
        lane = lane_iota((CH, COLS))
        shifted[y, 1] = value.astype(BF16)
        shifted[y, 0] = jnp.where(lane == 0, 0.0, pltpu.roll(value, 1, 1)).astype(BF16)
        shifted[y, 2] = jnp.where(lane == COLS - 1, 0.0, pltpu.roll(value, COLS - 1, 1)).astype(BF16)

    def gather_ends(y, value, ends):
        lane = lane_iota((CH, COLS))
        ends = jnp.where(lane == y, value[:, 0:1], ends)
        return jnp.where(lane == y + ROWS, value[:, COLS - 1 : COLS], ends)

    def put_ends(turn, ends):
        sides = jnp.transpose(ends)[0 : 2 * ROWS].astype(BF16)
        side_out[turn, :, 0:CH] = sides
        side_out[turn, :, CH:] = jnp.zeros((2 * ROWS, 256 - CH), BF16)

    def fill_row(y, ends):
        value = x_ref[y].astype(F32)
        fill_shifted(y + 1, value)
        return gather_ends(y, value, ends)

    ends = lax.fori_loop(0, ROWS, fill_row, jnp.zeros((CH, COLS), F32))
    put_ends(0, ends)

    up, down = lax.rem(lat + N_LAT - 1, N_LAT), lax.rem(lat + 1, N_LAT)
    left, right = lax.rem(lon + N_LON - 1, N_LON), lax.rem(lon + 1, N_LON)

    def halo_copies(turn):
        first, last = shifted.at[1, 1], shifted.at[ROWS, 1]
        mine = side_out.at[turn]
        plan = [
            (first, row_in.at[turn, 1], (up, lon)),
            (last, row_in.at[turn, 0], (down, lon)),
            (mine.at[pl.ds(0, ROWS)], side_in.at[turn, 1], (lat, left)),
            (mine.at[pl.ds(ROWS, ROWS)], side_in.at[turn, 0], (lat, right)),
            (mine.at[pl.ds(0, 16)], corner_in.at[turn, 3], (up, left)),
            (mine.at[pl.ds(ROWS, 16)], corner_in.at[turn, 2], (up, right)),
            (mine.at[pl.ds(16, 16)], corner_in.at[turn, 1], (down, left)),
            (mine.at[pl.ds(ROWS + 16, 16)], corner_in.at[turn, 0], (down, right)),
        ]
        return [
            pltpu.make_async_remote_copy(
                src_ref=source,
                dst_ref=target,
                send_sem=halo_send.at[turn, k],
                recv_sem=halo_recv.at[turn, k],
                device_id=where,
                device_id_type=pl.DeviceIdType.MESH,
            )
            for k, (source, target, where) in enumerate(plan)
        ]

    def start_exchange(turn, source, target):
        def send(i, carry):
            peer = lax.rem(me + i, N)
            pltpu.make_async_remote_copy(
                src_ref=source.at[peer],
                dst_ref=target.at[me],
                send_sem=a2a_send.at[turn],
                recv_sem=a2a_recv.at[turn],
                device_id=coords(peer),
                device_id_type=pl.DeviceIdType.MESH,
            ).start()
            return carry

        lax.fori_loop(1, N, send, 0)
        target[me] = source[me]

    def wait_received(turn, target):
        rest = target.at[pl.ds(0, N - 1)]
        pltpu.make_async_copy(rest, rest, a2a_recv.at[turn]).wait()

    def wait_sent(turn, source):
        rest = source.at[pl.ds(0, N - 1)]
        pltpu.make_async_copy(rest, rest, a2a_send.at[turn]).wait()

    pl.semaphore_wait(barrier, N - 1)
    first_halo = halo_copies(0)
    for copy in first_halo:
        copy.start()
    start_exchange(0, ask_out, ask_in)

    for tap in range(9):
        taps_f[:, CH * tap : CH * (tap + 1)] = jnp.transpose(conv_ref[tap].astype(F32)).astype(BF16)
        taps_b[:, CH * tap : CH * (tap + 1)] = conv_ref[8 - tap]
    select_t[...] = (row_iota((SLOTS, STATIONS)).astype(F32) == slot).astype(BF16)
    slot_cols = as_columns(slot)
    slot_cols = jnp.concatenate([slot_cols] * (SLOTS // 128), axis=1)
    select[...] = (lane_iota((STATIONS, SLOTS)).astype(F32) == slot_cols).astype(BF16)
    for wide_gain, gain in ((gain1, gain1_ref), (gain2, gain2_ref)):
        cols = as_columns(gain[...])
        wide_gain[...] = jnp.concatenate([cols, cols], axis=1)
    observed_t[...] = jnp.transpose(observed_ref[...])
    mask_t[...] = jnp.transpose(mask_ref[...].astype(F32))
    shown = (observed_t[...] * (1.0 - mask_t[...])).astype(BF16)
    embedded0[...] = nn(in_ref[:, 0:128], shown) + nn(in_ref[:, 128:256], mask_t[...].astype(BF16))
    low = in_ref[:, 256:448].astype(F32)
    in_low[...] = jnp.concatenate([low, jnp.zeros((CH, 64), F32)], axis=1).astype(BF16)
    in_low_t[...] = jnp.transpose(low).astype(BF16)
    qkv_t[...] = jnp.transpose(qkv_ref[...].astype(F32)).astype(BF16)
    out_t[...] = jnp.transpose(out_ref[...].astype(F32)).astype(BF16)
    head_t[...] = jnp.transpose(head_ref[...].astype(F32)).astype(BF16)

    live = live_ref[...].astype(F32)
    station = lane_iota((1, STATIONS)).astype(F32)
    near = neighbours_ref[...].astype(F32)
    used = (row_iota((16, STATIONS)).astype(F32) < count_ref[...].astype(F32)) & (near < live)
    near = jnp.where(used, near, -1.0)
    near = jnp.concatenate([near, station, jnp.full((7, STATIONS), -1.0, F32)], axis=0)
    bias = jnp.concatenate([bias_ref[...], jnp.zeros((8, STATIONS), F32)], axis=0)
    top = jnp.full((24, STATIONS), -1e30, F32)
    for j in range(17):
        top = jnp.where(near == near[j : j + 1], jnp.maximum(top, bias[j : j + 1]), top)
    together = jnp.zeros((24, STATIONS), F32)
    for j in range(17):
        together = together + jnp.where(near == near[j : j + 1], jnp.exp(bias[j : j + 1] - top), 0.0)
    level = top + jnp.log(together)
    other = row_iota(square).astype(F32)
    dense = jnp.full(square, -1e30, F32)
    for j in range(17):
        dense = jnp.where(other == near[j : j + 1], level[j : j + 1], dense)
    scores_bias[...] = dense

    wait_received(0, ask_in)
    asked = ask_in[...].reshape(N, 128).astype(BF16)
    repeat = (row_iota((SLOTS, N)) // CAP == lane_iota((SLOTS, N))).astype(BF16)
    asked = nn(repeat, asked)
    place = lane_iota((SLOTS, 128))
    turn_of = row_iota((SLOTS, 128)) & (CAP - 1)
    spots = jnp.where(place == turn_of, asked * 256.0, 0.0) + jnp.where(place == turn_of + CAP, asked, 0.0)
    spots = jnp.sum(spots, axis=1, keepdims=True)
    fine_row = jnp.floor((spots + 0.5) * (1.0 / FINE))
    fine_col = spots - FINE * fine_row
    at_row = jnp.broadcast_to((fine_row + 0.5) * 0.25, (SLOTS, COLS))
    at_col = jnp.broadcast_to((fine_col + 0.5) * 0.25, (SLOTS, COLS))
    along = jnp.maximum(1.0 - jnp.abs(at_col - place.astype(F32)), 0.0).astype(BF16)
    at_row = at_row.astype(BF16)

    def fill_spread(y, carry):
        away = jnp.abs(at_row - y.astype(BF16))
        spread[y] = jnp.maximum(1.0 - away, 0.0).astype(BF16) * along
        return carry

    lax.fori_loop(0, ROWS, fill_spread, 0)

    keep_up = jnp.where(lat > 0, 1.0, 0.0)
    keep_down = jnp.where(lat < N_LAT - 1, 1.0, 0.0)

    def take_halo(turn, copies, taps, backward):
        for copy in copies:
            copy.wait_recv()
        fill_shifted(0, row_in[turn, 0].astype(F32) * keep_up)
        fill_shifted(ROWS + 1, row_in[turn, 1].astype(F32) * keep_down)
        total = []
        for side in range(2):
            above = corner_in[turn, side].astype(F32)[15:16, 0:CH] * keep_up
            below = corner_in[turn, 2 + side].astype(F32)[0:1, 0:CH] * keep_down
            column = jnp.concatenate([above, side_in[turn, side].astype(F32)[:, 0:CH], below], axis=0)
            sums = None
            for i in range(3):
                part = column[i : i + ROWS].astype(BF16)
                if backward:
                    term = nt(part, conv_ref[8 - (3 * i + 2 * side)])
                else:
                    term = nn(part, conv_ref[3 * i + 2 * side])
                sums = term if sums is None else sums + term
            total.append(sums)
        total = jnp.concatenate(total + [jnp.zeros((64, CH), F32)], axis=0)
        taps[:, TAPS:] = jnp.transpose(total)[:, 0 : 2 * ROWS].astype(BF16)

    def around(y):
        ends_at = row_iota((2 * ROWS, COLS))
        lane = lane_iota((2 * ROWS, COLS))
        hit = ((ends_at == y) & (lane == 0)) | ((ends_at == y + ROWS) & (lane == COLS - 1))
        return jnp.concatenate(
            [shifted[pl.ds(y, 3)].reshape(TAPS, COLS), hit.astype(F32).astype(BF16)], axis=0
        )

    take_halo(0, first_halo, taps_f, False)

    def forward_rows(pair, carry):
        y = pair * 2
        pre = nn(taps_f[...], jnp.concatenate([around(y), around(y + 1)], axis=1))
        gate = 1.0 / (1.0 + jnp.exp(-pre))
        moved = pre * gate
        tilt = gate * (1.0 + pre * (1.0 - gate))
        for k in range(2):
            cut = slice(COLS * k, COLS * (k + 1))
            field[y + k] = (x_ref[y + k].astype(F32) + moved[:, cut]).astype(BF16)
            slope[y + k] = tilt[:, cut].astype(BF16)
        return carry

    lax.fori_loop(0, ROWS // 2, forward_rows, 0)

    def send_wide(rows, out):
        wide[pl.ds(0, SLOTS, 2)] = rows[:, 0:128]
        wide[pl.ds(1, SLOTS, 2)] = jnp.concatenate([rows[:, 128:CH], jnp.zeros((SLOTS, 256 - CH), F32)], axis=1)
        out[...] = wide[...].reshape(N, 2 * CAP, 128).astype(BF16)

    def read_wide(held):
        wide[...] = held[...].astype(F32).reshape(2 * SLOTS, 128)
        return wide[pl.ds(0, SLOTS, 2)], wide[pl.ds(1, SLOTS, 2)]

    sampled = jnp.zeros((SLOTS, CH), F32)
    for eighth in range(4):
        rows = [8 * eighth + k for k in range(8)]
        sampled = sampled + nt(
            jnp.concatenate([spread[y] for y in rows], axis=1), jnp.concatenate([field[y] for y in rows], axis=1)
        )
    send_wide(sampled, answer_out)
    start_exchange(1, answer_out, answer_in)
    wait_received(1, answer_in)

    low_part, high_part = read_wide(answer_in)
    answers = jnp.concatenate([low_part, high_part], axis=1).astype(BF16)
    interp = nn(select[...], answers).astype(BF16)
    embedded = embedded0[...] + nt(in_low[...], interp)
    scale1 = lax.rsqrt(jnp.mean(embedded * embedded, axis=0, keepdims=True) + EPS)
    unit1 = embedded * scale1
    projected = nn(qkv_t[...], (unit1 * gain1[...]).astype(BF16)).astype(BF16)
    probs, mixed = [], []
    score_scale = 1.0 / 8.0

    def part_of(kind, head):
        at = kind * CH + head * HEAD_DIM
        return projected[at : at + HEAD_DIM]

    def turned(value):
        return jnp.transpose(value.astype(F32)).astype(BF16)

    for head in range(HEADS):
        score = nn(turned(part_of(1, head)), part_of(0, head)) * score_scale + scores_bias[...]
        weight = jnp.exp(score - jnp.max(score, axis=0, keepdims=True))
        prob = (weight * (1.0 / jnp.sum(weight, axis=0, keepdims=True))).astype(BF16)
        probs.append(prob)
        mixed.append(nn(part_of(2, head), prob))
    mixed = jnp.concatenate(mixed, axis=0).astype(BF16)
    residual = embedded + nn(out_t[...], mixed)
    scale2 = lax.rsqrt(jnp.mean(residual * residual, axis=0, keepdims=True) + EPS)
    unit2 = residual * scale2
    final = (unit2 * gain2[...]).astype(BF16)
    alive = (station < live).astype(F32)
    predicted = nn(head_t[...], final) * alive
    d_pred = (2.0 * alive * mask_t[...] * (predicted - observed_t[...])).astype(BF16)

    d_unit2 = nn(head_ref[...], d_pred) * gain2[...]
    d_residual = scale2 * (d_unit2 - unit2 * jnp.mean(d_unit2 * unit2, axis=0, keepdims=True))
    d_mixed = nn(out_ref[...], d_residual.astype(BF16)).astype(BF16)
    d_query, d_key, d_value = [], [], []
    for head in range(HEADS):
        d_here = d_mixed[head * HEAD_DIM : (head + 1) * HEAD_DIM]
        prob = probs[head]
        d_prob = nn(turned(part_of(2, head)), d_here)
        wide_prob = prob.astype(F32)
        d_score = d_prob - jnp.sum(d_prob * wide_prob, axis=0, keepdims=True)
        d_score = (wide_prob * d_score * score_scale).astype(BF16)
        d_query.append(nn(part_of(1, head), d_score))
        d_key.append(nt(part_of(0, head), d_score))
        d_value.append(nt(d_here, prob))
    d_projected = jnp.concatenate(d_query + d_key + d_value, axis=0).astype(BF16)
    d_unit1 = nn(qkv_ref[...], d_projected) * gain1[...]
    d_embedded = d_residual + scale1 * (d_unit1 - unit1 * jnp.mean(d_unit1 * unit1, axis=0, keepdims=True))
    d_interp = nn(in_low_t[...], d_embedded.astype(BF16)).astype(BF16)
    send_wide(nt(select_t[...], d_interp), grads_out)
    start_exchange(2, grads_out, grads_in)
    predicted_ref[...] = jnp.transpose(predicted)
    for copy in first_halo:
        copy.wait_send()
    wait_received(2, grads_in)

    low_part, high_part = read_wide(grads_in)
    grads_t[0:128] = jnp.transpose(low_part).astype(BF16)
    grads_t[128:CH] = jnp.transpose(high_part)[0 : CH - 128].astype(BF16)

    def scatter_rows(pair, ends):
        y = pair * 2
        both = nn(grads_t[...], jnp.concatenate([spread[y], spread[y + 1]], axis=1))
        for k in range(2):
            value = both[:, COLS * k : COLS * (k + 1)]
            grad_ref[y + k] = value
            value = value * slope[y + k].astype(F32)
            fill_shifted(y + k + 1, value)
            ends = gather_ends(y + k, value, ends)
        return ends

    ends = lax.fori_loop(0, ROWS // 2, scatter_rows, jnp.zeros((CH, COLS), F32))
    put_ends(1, ends)
    second_halo = halo_copies(1)
    for copy in second_halo:
        copy.start()
    take_halo(1, second_halo, taps_b, True)

    def backward_rows(pair, carry):
        y = pair * 2
        back = nn(taps_b[...], jnp.concatenate([around(y), around(y + 1)], axis=1))
        for k in range(2):
            grad_ref[y + k] = grad_ref[y + k] + back[:, COLS * k : COLS * (k + 1)]
        return carry

    lax.fori_loop(0, ROWS // 2, backward_rows, 0)
    for copy in second_halo:
        copy.wait_send()
    wait_sent(0, ask_out)
    wait_sent(1, answer_out)
    wait_sent(2, grads_out)


def on_device(
    grid_field,
    conv_weight,
    observed,
    hidden_mask,
    tile_route,
    station_spot,
    neighbours,
    neighbour_count,
    edge_bias,
    live_count,
    in_weight,
    norm_gain,
    qkv_weight,
    out_weight,
    final_gain,
    head_weight,
):
    vmem = pl.BlockSpec(memory_space=pltpu.VMEM)
    operands = (
        jnp.transpose(grid_field, (0, 2, 1)),
        conv_weight,
        observed,
        hidden_mask,
        tile_route.reshape(1, STATIONS),
        station_spot.reshape(1, STATIONS),
        neighbours.T,
        neighbour_count.reshape(1, STATIONS),
        edge_bias.T,
        live_count.reshape(1, 1),
        in_weight.T,
        norm_gain.reshape(1, CH),
        qkv_weight,
        out_weight,
        final_gain.reshape(1, CH),
        head_weight,
    )
    predicted, gradient = pl.pallas_call(
        kernel,
        out_shape=(
            jax.ShapeDtypeStruct((STATIONS, 128), F32),
            jax.ShapeDtypeStruct((ROWS, CH, COLS), F32),
        ),
        in_specs=[vmem] * len(operands),
        out_specs=(vmem, vmem),
        scratch_shapes=[
            pltpu.VMEM((ROWS + 2, 3, CH, COLS), BF16),
            pltpu.VMEM((CH, DEPTH), BF16),
            pltpu.VMEM((CH, DEPTH), BF16),
            pltpu.VMEM((ROWS, CH, COLS), BF16),
            pltpu.VMEM((ROWS, CH, COLS), BF16),
            pltpu.VMEM((ROWS, SLOTS, COLS), BF16),
            pltpu.VMEM((N, 2 * CAP, 128), BF16),
            pltpu.VMEM((N, 2 * CAP, 128), BF16),
            pltpu.VMEM((N, 2 * CAP, 128), BF16),
            pltpu.VMEM((N, 2 * CAP, 128), BF16),
            pltpu.VMEM((N, 1, 128), F32),
            pltpu.VMEM((N, 1, 128), F32),
            pltpu.VMEM((2 * SLOTS, 128), F32),
            pltpu.VMEM((2, 2, CH, COLS), BF16),
            pltpu.VMEM((2, 2 * ROWS, 256), BF16),
            pltpu.VMEM((2, 2, ROWS, 256), BF16),
            pltpu.VMEM((2, 4, 16, 256), BF16),
            pltpu.VMEM((STATIONS, SLOTS), BF16),
            pltpu.VMEM((SLOTS, STATIONS), BF16),
            pltpu.VMEM((STATIONS, STATIONS), F32),
            pltpu.VMEM((CH, SLOTS), BF16),
            pltpu.VMEM((CH, STATIONS), F32),
            pltpu.VMEM((CH, STATIONS), F32),
            pltpu.VMEM((CH, STATIONS), F32),
            pltpu.VMEM((CH, 256), BF16),
            pltpu.VMEM((CH, CH), BF16),
            pltpu.VMEM((3 * CH, CH), BF16),
            pltpu.VMEM((CH, CH), BF16),
            pltpu.VMEM((128, CH), BF16),
            pltpu.VMEM((128, STATIONS), F32),
            pltpu.VMEM((128, STATIONS), F32),
            pltpu.SemaphoreType.DMA((2, 8)),
            pltpu.SemaphoreType.DMA((2, 8)),
            pltpu.SemaphoreType.DMA((3,)),
            pltpu.SemaphoreType.DMA((3,)),
        ],
        compiler_params=pltpu.CompilerParams(
            collective_id=0, has_side_effects=True, vmem_limit_bytes=56 << 20
        ),
        name="whole",
    )(*operands)
    return predicted, jnp.transpose(gradient, (0, 2, 1))


def solution(mesh):
    return jax.shard_map(
        on_device,
        mesh=mesh,
        in_specs=(
            P("lat", "lon", None),
            P(),
            P(LAT_LON, None),
            P(LAT_LON, None),
            P(LAT_LON, None),
            P(LAT_LON),
            P(LAT_LON, None),
            P(LAT_LON),
            P(LAT_LON, None),
            P(LAT_LON),
            P(),
            P(),
            P(),
            P(),
            P(),
            P(),
        ),
        out_specs=(P(LAT_LON, None), P("lat", "lon", None)),
        check_vma=False,
    )
```

time: 386 us -> 79.9 us (0.21); the launches traced: 380 us -> 79.7 us
  other arithmetic: 156 us -> 0 us
  local copies, waits for them, and re-layouts: 110 us -> 5.46 us
  Pallas kernels: 0 us -> 73 us
  matrix products: 44.3 us -> 0 us
  starting transfers between devices: 38.8 us -> 0 us
  waiting for transfers between devices: 23.9 us -> 0 us
  blocking collectives: 4.98 us -> 0 us
    pallas_call x0 -> x1, Pallas kernels: none -> 73 us  [on_device(): pl.pallas_call(kernel, out_shape=(jax.ShapeDtypeStruct((STATIONS, 128), F...]
    scatter-add x3 -> x0, other arithmetic: 61.3 us -> none  [the longest x1 23.4 us: station_forward(): near_keys = key_rows[neighbours].reshape(station_rows, -1, HEADS, HEAD_DIM)]
    dot_general x11 -> x0, matrix products: 44.3 us -> none  [the longest x2 36.9 us: convolve(): lax.dot_general(flat, taps, (((1,), (contract,)), ((), ())), preferred_el...]
    convert_element_type x11 -> x0, other arithmetic: 42.7 us -> none  [the longest x1 17.5 us: on_device(): (grid_field.astype(jnp.float32) + jax.nn.silu(pre_act)).astype(jnp.bfloat16)]
    gather x4 -> x0, local copies, waits for them, and re-layouts: 42 us -> none  [the longest x1 17 us: station_forward(): value_rows[neighbours].reshape(station_rows, -1, HEADS, HEAD_DIM)]
    reshape x7 -> x0, local copies, waits for them, and re-layouts: 31 us -> none  [the longest x2 17.1 us: station_forward(): value_rows[neighbours].reshape(station_rows, -1, HEADS, HEAD_DIM)]
    all_to_all x3 -> x0, starting transfers between devices: 21.6 us -> none  [the longest x1 11.1 us: on_device(): lax.all_to_all(requests, LAT_LON, split_axis=0, concat_axis=0, tiled=True)]
    all_to_all x3 -> x0, waiting for transfers between devices: 20.1 us -> none  [the longest x1 10.3 us: on_device(): lax.all_to_all(outgoing.astype(jnp.bfloat16), LAT_LON, split_axis=0, conc...]
  transfers between devices with their start and end apart: 11 -> 0, of which waited for: 5 -> 0; matrix products, arithmetic and copies ran while one was open for 3% -> 0% of each run, Pallas kernels for 0% -> 0%
where the time goes in v2:
time: 79.9 us; the launch traced here: 79.7 us
  Pallas kernels  73 us (91%)
  local copies, waits for them, and re-layouts  5.46 us (7%)
  between operations  1.29 us (2%)
    pallas_call x1, Pallas kernels, on_device(): pl.pallas_call(kernel, out_shape=(jax.ShapeDtypeStruct((STATIONS, 128), F...  73 us
    unnamed x2, local copies, waits for them, and re-layouts  5.46 us

profile of v2, /device:TPU:0, one launch (start us, length us, event | category | flops | bytes accessed | tf_op | source)
XLA Modules:
  0.0 79.7 jit_solution(13871807713866614901)
XLA Ops:
  1.3 73.0 %whole.1 = (f32[256,128]{1,0:T(8,128)}, f32[32,192,128]{2,1,0:T(8,128)}) custom-call(bf16[32,192,128]{2,1,0:T(8,128)(2,1)} %bitcast.13, bf16[9,192,192]{2,1,0:T(8,128)(2,1)} %conv_ref.1, f32[256,128]{1,0:T(8,128)} %observed_ref.1, s32[256,128]{1,0:T(8,128)} %mask_ref.1, s32[1,256]{1,0:T(1,128)} %bitcast.17, s32[1,256]{1,0:T(1,128)} %bitcast.18, ...), custom_call_target="tpu_custom_call" | custom-call | tf_op jit(solution)/shard_map/whole/pallas_call | solution.py:480
  74.3 1.6 %copy.21 = f32[256,128]{1,0:T(8,128)} copy(f32[256,128]{1,0:T(8,128)} %get-tuple-element.8) | data formatting | bytes 262144
  75.9 3.9 %copy.22 = f32[32,128,192]{1,2,0:T(8,128)} copy(f32[32,128,192]{1,2,0:T(8,128)} %bitcast.12) | data formatting | bytes 6291456

commit v3 on v2

v3 whole, which is shorter than its diff:
```python
import jax
import jax.numpy as jnp
from jax import lax
from jax.experimental import pallas as pl
from jax.experimental.pallas import tpu as pltpu
from jax.sharding import PartitionSpec as P

CH = 192
HEADS = 3
HEAD_DIM = 64
ROWS = 32
COLS = 128
FINE = 4 * (COLS - 1)
CAP = 4
N = 128
N_LAT = 4
N_LON = 32
SLOTS = N * CAP
STATIONS = 256
TAPS = 9 * CH
DEPTH = TAPS + 2 * ROWS
EPS = 1e-06
F32 = jnp.float32
BF16 = jnp.bfloat16
LAT_LON = ("lat", "lon")


def nn(a, b):
    return lax.dot_general(a, b, (((1,), (0,)), ((), ())), preferred_element_type=F32)


def nt(a, b):
    return lax.dot_general(a, b, (((1,), (1,)), ((), ())), preferred_element_type=F32)


def lane_iota(shape):
    return lax.broadcasted_iota(jnp.int32, shape, len(shape) - 1)


def row_iota(shape):
    return lax.broadcasted_iota(jnp.int32, shape, len(shape) - 2)


def as_columns(row):
    return jnp.transpose(jnp.broadcast_to(row, (128, row.shape[1])))


def flipped(value):
    return jnp.transpose(value.astype(F32)).astype(BF16)


def sigmoid(v):
    return 0.5 * (1.0 + jnp.tanh(0.5 * v))


def fill_shifted(shifted, y, value):
    lane = lane_iota((CH, COLS))
    shifted[y, 1] = value.astype(BF16)
    shifted[y, 0] = jnp.where(lane == 0, 0.0, pltpu.roll(value, 1, 1)).astype(BF16)
    shifted[y, 2] = jnp.where(lane == COLS - 1, 0.0, pltpu.roll(value, COLS - 1, 1)).astype(BF16)


def around(shifted, y):
    ends_at = row_iota((2 * ROWS, COLS))
    lane = lane_iota((2 * ROWS, COLS))
    hit = ((ends_at == y) & (lane == 0)) | ((ends_at == y + ROWS) & (lane == COLS - 1))
    return jnp.concatenate([shifted[pl.ds(y, 3)].reshape(TAPS, COLS), hit.astype(F32).astype(BF16)], axis=0)


def kernel(*refs):
    (x_hbm, conv_hbm, observed_hbm, mask_hbm, tile_hbm, spot_hbm, neighbours_hbm, count_hbm) = refs[0:8]
    (bias_hbm, live_hbm, in_hbm, gain1_hbm, qkv_hbm, out_hbm, gain2_hbm, head_hbm) = refs[8:16]
    (predicted_hbm, dpre_hbm, dfield_hbm, taps_hbm) = refs[16:20]
    (x_ref, conv_ref, observed_ref, mask_ref, tile_ref, spot_ref, neighbours_ref, count_ref) = refs[20:28]
    (bias_ref, live_ref, in_ref, gain1_ref, qkv_ref, out_ref, gain2_ref, head_ref) = refs[28:36]
    (shifted, taps_f, taps_b, field, slope, spread, dpre, dfield, pick) = refs[36:45]
    (answer_out, answer_in, grads_out, grads_in, ask_out, ask_in, wide) = refs[45:52]
    (row_in, side_out, side_in, corner_in, select, select_t, scores_bias, grads_t) = refs[52:60]
    (embedded0, gain1, gain2, in_low, in_low_t, qkv_t, out_t, head_t, mask_t, observed_t) = refs[60:70]
    (ends_spread, slope_ends, predicted_out) = refs[70:73]
    (halo_send, halo_recv, a2a_send, a2a_recv, load_sem, store_sem) = refs[73:79]

    loads = [pltpu.make_async_copy(refs[k], refs[20 + k], load_sem.at[k]) for k in range(16)]
    for k in (4, 5, 0, 1, 2, 3, 6, 7, 8, 9, 10, 11, 12, 13, 14, 15):
        loads[k].start()
    lat = lax.axis_index("lat")
    lon = lax.axis_index("lon")
    me = lat * N_LON + lon
    barrier = pltpu.get_barrier_semaphore()

    def coords(peer):
        return (peer // N_LON, lax.rem(peer, N_LON))

    def greet(i, carry):
        pl.semaphore_signal(
            barrier, inc=1, device_id=coords(lax.rem(me + i, N)), device_id_type=pl.DeviceIdType.MESH
        )
        return carry

    lax.fori_loop(1, N, greet, 0)

    loads[4].wait()
    loads[5].wait()
    tile_row = tile_ref[...].astype(F32)
    tile_cols = as_columns(tile_row)
    tile_cols = jnp.concatenate([tile_cols, tile_cols], axis=1)
    square = (STATIONS, STATIONS)
    same = (tile_cols == tile_row) & (row_iota(square) < lane_iota(square))
    rank = jnp.sum(same.astype(F32), axis=0, keepdims=True)
    slot = tile_row * CAP + rank
    spot = spot_ref[...].astype(F32)
    spot_high = jnp.floor(spot * (1.0 / 256.0))
    spot_low = spot - 256.0 * spot_high
    part = row_iota((128, STATIONS))
    wanted = jnp.where(part < CAP, spot_high, spot_low)
    wanted = jnp.where((part & (CAP - 1)).astype(F32) == rank, wanted, 0.0)
    wanted = jnp.where(part < 2 * CAP, wanted, 0.0).astype(BF16)
    is_tile = (row_iota((N, STATIONS)).astype(F32) == tile_row).astype(BF16)
    ask_out[...] = nt(is_tile, wanted).reshape(N, 1, 128)

    end = row_iota((2 * ROWS, ROWS * COLS))
    end_cell = jnp.where(end < ROWS, end * COLS, (end - ROWS) * COLS + COLS - 1)
    pick[...] = (lane_iota((2 * ROWS, ROWS * COLS)) == end_cell).astype(F32).astype(BF16)
    side_out[...] = jnp.zeros((2, 2 * ROWS, 256), BF16)
    loads[0].wait()
    side_out[0, :, 0:CH] = nt(pick[...], jnp.concatenate([x_ref[y] for y in range(ROWS)], axis=1)).astype(BF16)

    up, down = lax.rem(lat + N_LAT - 1, N_LAT), lax.rem(lat + 1, N_LAT)
    left, right = lax.rem(lon + N_LON - 1, N_LON), lax.rem(lon + 1, N_LON)

    def halo_copies(turn, first, last):
        mine = side_out.at[turn]
        plan = [
            (mine.at[pl.ds(0, ROWS)], side_in.at[turn, 1], (lat, left)),
            (mine.at[pl.ds(ROWS, ROWS)], side_in.at[turn, 0], (lat, right)),
            (mine.at[pl.ds(0, 16)], corner_in.at[turn, 3], (up, left)),
            (mine.at[pl.ds(ROWS, 16)], corner_in.at[turn, 2], (up, right)),
            (mine.at[pl.ds(16, 16)], corner_in.at[turn, 1], (down, left)),
            (mine.at[pl.ds(ROWS + 16, 16)], corner_in.at[turn, 0], (down, right)),
            (first, row_in.at[turn, 1], (up, lon)),
            (last, row_in.at[turn, 0], (down, lon)),
        ]
        return [
            pltpu.make_async_remote_copy(
                src_ref=source,
                dst_ref=target,
                send_sem=halo_send.at[turn, k],
                recv_sem=halo_recv.at[turn, k],
                device_id=where,
                device_id_type=pl.DeviceIdType.MESH,
            )
            for k, (source, target, where) in enumerate(plan)
        ]

    def start_exchange(turn, source, target):
        def send(i, carry):
            peer = lax.rem(me + i, N)
            pltpu.make_async_remote_copy(
                src_ref=source.at[peer],
                dst_ref=target.at[me],
                send_sem=a2a_send.at[turn],
                recv_sem=a2a_recv.at[turn],
                device_id=coords(peer),
                device_id_type=pl.DeviceIdType.MESH,
            ).start()
            return carry

        lax.fori_loop(1, N, send, 0)
        target[me] = source[me]

    def wait_received(turn, target):
        rest = target.at[pl.ds(0, N - 1)]
        pltpu.make_async_copy(rest, rest, a2a_recv.at[turn]).wait()

    def wait_sent(turn, source):
        rest = source.at[pl.ds(0, N - 1)]
        pltpu.make_async_copy(rest, rest, a2a_send.at[turn]).wait()

    pl.semaphore_wait(barrier, N - 1)
    first_halo = halo_copies(0, x_ref.at[0], x_ref.at[ROWS - 1])
    for copy in first_halo:
        copy.start()
    start_exchange(0, ask_out, ask_in)

    def fill_row(y, carry):
        fill_shifted(shifted, y + 1, x_ref[y].astype(F32))
        return carry

    lax.fori_loop(0, ROWS, fill_row, 0, unroll=2)
    loads[1].wait()
    for tap in range(9):
        taps_f[:, CH * tap : CH * (tap + 1)] = flipped(conv_ref[tap])

    keep_up = jnp.where(lat > 0, 1.0, 0.0)
    keep_down = jnp.where(lat < N_LAT - 1, 1.0, 0.0)

    def side_terms(turn, taps, backward):
        total = []
        for side in range(2):
            above = corner_in[turn, side].astype(F32)[15:16, 0:CH] * keep_up
            below = corner_in[turn, 2 + side].astype(F32)[0:1, 0:CH] * keep_down
            column = jnp.concatenate([above, side_in[turn, side].astype(F32)[:, 0:CH], below], axis=0)
            sums = None
            for i in range(3):
                piece = column[i : i + ROWS].astype(BF16)
                if backward:
                    term = nt(piece, conv_ref[8 - (3 * i + 2 * side)])
                else:
                    term = nn(piece, conv_ref[3 * i + 2 * side])
                sums = term if sums is None else sums + term
            total.append(sums)
        total = jnp.concatenate(total + [jnp.zeros((64, CH), F32)], axis=0)
        taps[:, TAPS:] = jnp.transpose(total)[:, 0 : 2 * ROWS].astype(BF16)

    for copy in first_halo:
        copy.wait_recv()
    fill_shifted(shifted, 0, row_in[0, 0].astype(F32) * keep_up)
    fill_shifted(shifted, ROWS + 1, row_in[0, 1].astype(F32) * keep_down)
    side_terms(0, taps_f, False)

    def forward_rows(pair, carry):
        y = pair * 2
        pre = nn(taps_f[...], jnp.concatenate([around(shifted, y), around(shifted, y + 1)], axis=1))
        gate = sigmoid(pre)
        moved = pre * gate
        tilt = gate * (1.0 + pre * (1.0 - gate))
        for k in range(2):
            cut = slice(COLS * k, COLS * (k + 1))
            field[y + k] = (x_ref[y + k].astype(F32) + moved[:, cut]).astype(BF16)
            slope[y + k] = tilt[:, cut].astype(BF16)
        return carry

    lax.fori_loop(0, ROWS // 2, forward_rows, 0, unroll=4)

    wait_received(0, ask_in)
    asked = ask_in[...].reshape(N, 128).astype(BF16)
    repeat = (row_iota((SLOTS, N)) // CAP == lane_iota((SLOTS, N))).astype(BF16)
    asked = nn(repeat, asked)
    place = lane_iota((SLOTS, 128))
    turn_of = row_iota((SLOTS, 128)) & (CAP - 1)
    spots = jnp.where(place == turn_of, asked * 256.0, 0.0) + jnp.where(place == turn_of + CAP, asked, 0.0)
    spots = jnp.sum(spots, axis=1, keepdims=True)
    fine_row = jnp.floor((spots + 0.5) * (1.0 / FINE))
    fine_col = spots - FINE * fine_row
    at_row = jnp.broadcast_to((fine_row + 0.5) * 0.25, (SLOTS, COLS))
    at_col = jnp.broadcast_to((fine_col + 0.5) * 0.25, (SLOTS, COLS))
    along = jnp.maximum(1.0 - jnp.abs(at_col - place.astype(F32)), 0.0).astype(BF16)
    at_row16 = at_row.astype(BF16)

    def fill_spread(y, carry):
        away = jnp.abs(at_row16 - y.astype(BF16))
        spread[y] = jnp.maximum(1.0 - away, 0.0).astype(BF16) * along
        return carry

    lax.fori_loop(0, ROWS, fill_spread, 0, unroll=4)

    def send_wide(rows, out):
        wide[pl.ds(0, SLOTS, 2)] = rows[:, 0:128]
        wide[pl.ds(1, SLOTS, 2)] = jnp.concatenate([rows[:, 128:CH], jnp.zeros((SLOTS, 256 - CH), F32)], axis=1)
        out[...] = wide[...].reshape(N, 2 * CAP, 128).astype(BF16)

    def read_wide(held):
        wide[...] = held[...].astype(F32).reshape(2 * SLOTS, 128)
        return wide[pl.ds(0, SLOTS, 2)], wide[pl.ds(1, SLOTS, 2)]

    sampled = jnp.zeros((SLOTS, CH), F32)
    for eighth in range(4):
        rows = [8 * eighth + k for k in range(8)]
        sampled = sampled + nt(
            jnp.concatenate([spread[y] for y in rows], axis=1), jnp.concatenate([field[y] for y in rows], axis=1)
        )
    send_wide(sampled, answer_out)
    start_exchange(1, answer_out, answer_in)

    for k in (2, 3, 6, 7, 8, 9, 10, 11, 12, 13, 14, 15):
        loads[k].wait()
    select_t[...] = (row_iota((SLOTS, STATIONS)).astype(F32) == slot).astype(BF16)
    slot_cols = as_columns(slot)
    slot_cols = jnp.concatenate([slot_cols] * (SLOTS // 128), axis=1)
    select[...] = (lane_iota((STATIONS, SLOTS)).astype(F32) == slot_cols).astype(BF16)
    for wide_gain, gain in ((gain1, gain1_ref), (gain2, gain2_ref)):
        cols = as_columns(gain[...])
        wide_gain[...] = jnp.concatenate([cols, cols], axis=1)
    observed_t[...] = jnp.transpose(observed_ref[...])
    mask_t[...] = jnp.transpose(mask_ref[...].astype(F32))
    shown = (observed_t[...] * (1.0 - mask_t[...])).astype(BF16)
    embedded0[...] = nn(in_ref[:, 0:128], shown) + nn(in_ref[:, 128:256], mask_t[...].astype(BF16))
    low = in_ref[:, 256:448].astype(F32)
    in_low[...] = jnp.concatenate([low, jnp.zeros((CH, 64), F32)], axis=1).astype(BF16)
    in_low_t[...] = jnp.transpose(low).astype(BF16)
    qkv_t[...] = flipped(qkv_ref[...])
    out_t[...] = flipped(out_ref[...])
    head_t[...] = flipped(head_ref[...])

    live = live_ref[...].astype(F32)
    station = lane_iota((1, STATIONS)).astype(F32)
    near = neighbours_ref[...].astype(F32)
    used = (row_iota((16, STATIONS)).astype(F32) < count_ref[...].astype(F32)) & (near < live)
    near = jnp.where(used, near, -1.0)
    near = jnp.concatenate([near, station, jnp.full((7, STATIONS), -1.0, F32)], axis=0)
    bias = jnp.concatenate([bias_ref[...], jnp.zeros((8, STATIONS), F32)], axis=0)
    top = jnp.full((24, STATIONS), -1e30, F32)
    for j in range(17):
        top = jnp.where(near == near[j : j + 1], jnp.maximum(top, bias[j : j + 1]), top)
    together = jnp.zeros((24, STATIONS), F32)
    for j in range(17):
        together = together + jnp.where(near == near[j : j + 1], jnp.exp(bias[j : j + 1] - top), 0.0)
    level = top + jnp.log(together)
    other = row_iota(square).astype(F32)
    dense = jnp.full(square, -1e30, F32)
    for j in range(17):
        dense = jnp.where(other == near[j : j + 1], level[j : j + 1], dense)
    scores_bias[...] = dense

    wait_received(1, answer_in)

    low_part, high_part = read_wide(answer_in)
    answers = jnp.concatenate([low_part, high_part], axis=1).astype(BF16)
    interp = nn(select[...], answers).astype(BF16)
    embedded = embedded0[...] + nt(in_low[...], interp)
    scale1 = lax.rsqrt(jnp.mean(embedded * embedded, axis=0, keepdims=True) + EPS)
    unit1 = embedded * scale1
    projected = nn(qkv_t[...], (unit1 * gain1[...]).astype(BF16)).astype(BF16)
    probs, mixed = [], []
    score_scale = 1.0 / 8.0

    def part_of(kind, head):
        at = kind * CH + head * HEAD_DIM
        return projected[at : at + HEAD_DIM]

    for head in range(HEADS):
        score = nn(flipped(part_of(1, head)), part_of(0, head)) * score_scale + scores_bias[...]
        weight = jnp.exp(score - jnp.max(score, axis=0, keepdims=True))
        prob = (weight * (1.0 / jnp.sum(weight, axis=0, keepdims=True))).astype(BF16)
        probs.append(prob)
        mixed.append(nn(part_of(2, head), prob))
    mixed = jnp.concatenate(mixed, axis=0).astype(BF16)
    residual = embedded + nn(out_t[...], mixed)
    scale2 = lax.rsqrt(jnp.mean(residual * residual, axis=0, keepdims=True) + EPS)
    unit2 = residual * scale2
    final = (unit2 * gain2[...]).astype(BF16)
    alive = (station < live).astype(F32)
    predicted = nn(head_t[...], final) * alive
    d_pred = (2.0 * alive * mask_t[...] * (predicted - observed_t[...])).astype(BF16)

    d_unit2 = nn(head_ref[...], d_pred) * gain2[...]
    d_residual = scale2 * (d_unit2 - unit2 * jnp.mean(d_unit2 * unit2, axis=0, keepdims=True))
    d_mixed = nn(out_ref[...], d_residual.astype(BF16)).astype(BF16)
    d_query, d_key, d_value = [], [], []
    for head in range(HEADS):
        d_here = d_mixed[head * HEAD_DIM : (head + 1) * HEAD_DIM]
        prob = probs[head]
        d_prob = nn(flipped(part_of(2, head)), d_here)
        wide_prob = prob.astype(F32)
        d_score = d_prob - jnp.sum(d_prob * wide_prob, axis=0, keepdims=True)
        d_score = (wide_prob * d_score * score_scale).astype(BF16)
        d_query.append(nn(part_of(1, head), d_score))
        d_key.append(nt(part_of(0, head), d_score))
        d_value.append(nt(d_here, prob))
    d_projected = jnp.concatenate(d_query + d_key + d_value, axis=0).astype(BF16)
    d_unit1 = nn(qkv_ref[...], d_projected) * gain1[...]
    d_embedded = d_residual + scale1 * (d_unit1 - unit1 * jnp.mean(d_unit1 * unit1, axis=0, keepdims=True))
    d_interp = nn(in_low_t[...], d_embedded.astype(BF16)).astype(BF16)
    send_wide(nt(select_t[...], d_interp), grads_out)
    start_exchange(2, grads_out, grads_in)

    predicted_out[...] = jnp.transpose(predicted)
    stores = [pltpu.make_async_copy(predicted_out, predicted_hbm, store_sem.at[0])]
    stores[0].start()
    for tap in range(9):
        taps_b[:, CH * tap : CH * (tap + 1)] = conv_ref[8 - tap]
    slope_ends[...] = nt(pick[...], jnp.concatenate([slope[y] for y in range(ROWS)], axis=1))
    end_row = (place & (ROWS - 1)).astype(F32)
    end_col = jnp.where(place < ROWS, 0.0, COLS - 1.0)
    on_end = jnp.maximum(1.0 - jnp.abs(at_row - end_row), 0.0) * jnp.maximum(1.0 - jnp.abs(at_col - end_col), 0.0)
    ends_spread[...] = jnp.transpose(on_end)[0 : 2 * ROWS].astype(BF16)
    for copy in first_halo:
        copy.wait_send()
    wait_received(2, grads_in)

    low_part, high_part = read_wide(grads_in)
    arrived = jnp.concatenate([low_part, high_part], axis=1)
    at_ends = nn(ends_spread[...], arrived.astype(BF16))[:, 0:CH] * slope_ends[...]
    side_out[1, :, 0:CH] = at_ends.astype(BF16)
    grads_t[...] = jnp.transpose(arrived)[0:CH].astype(BF16)

    def scatter_pair(y0, y1):
        both = nn(grads_t[...], jnp.concatenate([spread[y0], spread[y1]], axis=1))
        for k, y in enumerate((y0, y1)):
            value = both[:, COLS * k : COLS * (k + 1)]
            dfield[y] = value
            dpre[y + 1] = (value * slope[y].astype(F32)).astype(BF16)

    scatter_pair(0, ROWS - 1)
    second_halo = halo_copies(1, dpre.at[1], dpre.at[ROWS])
    for copy in second_halo:
        copy.start()

    def store(source, target):
        copy = pltpu.make_async_copy(source, target, store_sem.at[len(stores)])
        copy.start()
        stores.append(copy)

    store(dfield.at[pl.ds(0, 1)], dfield_hbm.at[pl.ds(0, 1)])
    store(dfield.at[pl.ds(ROWS - 1, 1)], dfield_hbm.at[pl.ds(ROWS - 1, 1)])
    for third in range(3):

        def scatter_rows(pair, carry):
            y = 1 + 10 * third + 2 * pair
            scatter_pair(y, y + 1)
            return carry

        lax.fori_loop(0, 5, scatter_rows, 0, unroll=True)
        at = pl.ds(1 + 10 * third, 10)
        store(dfield.at[at], dfield_hbm.at[at])
        at = pl.ds(2 + 10 * third, 10)
        store(dpre.at[at], dpre_hbm.at[at])
    for copy in second_halo:
        copy.wait_recv()
    dpre[0] = (row_in[1, 0].astype(F32) * keep_up).astype(BF16)
    dpre[ROWS + 1] = (row_in[1, 1].astype(F32) * keep_down).astype(BF16)
    store(dpre.at[pl.ds(0, 2)], dpre_hbm.at[pl.ds(0, 2)])
    store(dpre.at[pl.ds(ROWS, 2)], dpre_hbm.at[pl.ds(ROWS, 2)])
    side_terms(1, taps_b, True)
    store(taps_b, taps_hbm)
    for copy in second_halo:
        copy.wait_send()
    wait_sent(0, ask_out)
    wait_sent(1, answer_out)
    wait_sent(2, grads_out)
    for copy in stores:
        copy.wait()


def back_kernel(*refs):
    (dpre_hbm, dfield_hbm, taps_hbm, predicted_hbm, grad_hbm, predicted_to) = refs[0:6]
    (dpre, dfield, taps, shifted, grad, sem) = refs[6:12]
    through = pltpu.make_async_copy(predicted_hbm, predicted_to, sem.at[0])
    load_taps = pltpu.make_async_copy(taps_hbm, taps, sem.at[1])

    def load(part):
        at = pl.ds(0, 10) if part == 0 else pl.ds(8 * part + 2, 8)
        fields = pl.ds(8 * part, 8)
        return (
            pltpu.make_async_copy(dpre_hbm.at[at], dpre.at[at], sem.at[2 + part]),
            pltpu.make_async_copy(dfield_hbm.at[fields], dfield.at[fields], sem.at[6 + part]),
        )

    def store(part):
        fields = pl.ds(8 * part, 8)
        return pltpu.make_async_copy(grad.at[fields], grad_hbm.at[fields], sem.at[10 + part])

    loads = [load(part) for part in range(4)]
    loads[0][0].start()
    load_taps.start()
    loads[0][1].start()
    for part in range(1, 4):
        for copy in loads[part]:
            copy.start()
    through.start()

    def shift_part(part):
        loads[part][0].wait()

        def shift_row(k, carry):
            fill_shifted(shifted, k, dpre[k].astype(F32))
            return carry

        first = 0 if part == 0 else 8 * part + 2
        lax.fori_loop(first, 8 * part + 10, shift_row, 0, unroll=True)

    shift_part(0)
    load_taps.wait()
    for part in range(4):
        loads[part][1].wait()

        def backward_rows(pair, carry):
            y = 8 * part + pair * 2
            back = nn(taps[...], jnp.concatenate([around(shifted, y), around(shifted, y + 1)], axis=1))
            for k in range(2):
                grad[y + k] = dfield[y + k] + back[:, COLS * k : COLS * (k + 1)]
            return carry

        lax.fori_loop(0, 4, backward_rows, 0, unroll=True)
        store(part).start()
        if part < 3:
            shift_part(part + 1)
    for part in range(4):
        store(part).wait()
    through.wait()


def on_device(
    grid_field,
    conv_weight,
    observed,
    hidden_mask,
    tile_route,
    station_spot,
    neighbours,
    neighbour_count,
    edge_bias,
    live_count,
    in_weight,
    norm_gain,
    qkv_weight,
    out_weight,
    final_gain,
    head_weight,
):
    operands = (
        jnp.transpose(grid_field, (0, 2, 1)),
        conv_weight,
        observed,
        hidden_mask,
        tile_route.reshape(1, STATIONS),
        station_spot.reshape(1, STATIONS),
        neighbours.T,
        neighbour_count.reshape(1, STATIONS),
        edge_bias.T,
        live_count.reshape(1, 1),
        in_weight.T,
        norm_gain.reshape(1, CH),
        qkv_weight,
        out_weight,
        final_gain.reshape(1, CH),
        head_weight,
    )
    anywhere = pl.BlockSpec(memory_space=pl.ANY)

    def vmem(*shape, kind=BF16):
        return pltpu.VMEM(shape, kind)

    predicted, dpre, dfield, taps = pl.pallas_call(
        kernel,
        out_shape=(
            jax.ShapeDtypeStruct((STATIONS, 128), F32),
            jax.ShapeDtypeStruct((ROWS + 2, CH, COLS), BF16),
            jax.ShapeDtypeStruct((ROWS, CH, COLS), F32),
            jax.ShapeDtypeStruct((CH, DEPTH), BF16),
        ),
        in_specs=[anywhere] * len(operands),
        out_specs=(anywhere,) * 4,
        scratch_shapes=[pltpu.VMEM(o.shape, o.dtype) for o in operands]
        + [
            vmem(ROWS + 2, 3, CH, COLS),
            vmem(CH, DEPTH),
            vmem(CH, DEPTH),
            vmem(ROWS, CH, COLS),
            vmem(ROWS, CH, COLS),
            vmem(ROWS, SLOTS, COLS),
            vmem(ROWS + 2, CH, COLS),
            vmem(ROWS, CH, COLS, kind=F32),
            vmem(2 * ROWS, ROWS * COLS),
            vmem(N, 2 * CAP, 128),
            vmem(N, 2 * CAP, 128),
            vmem(N, 2 * CAP, 128),
            vmem(N, 2 * CAP, 128),
            vmem(N, 1, 128, kind=F32),
            vmem(N, 1, 128, kind=F32),
            vmem(2 * SLOTS, 128, kind=F32),
            vmem(2, 2, CH, COLS),
            vmem(2, 2 * ROWS, 256),
            vmem(2, 2, ROWS, 256),
            vmem(2, 4, 16, 256),
            vmem(STATIONS, SLOTS),
            vmem(SLOTS, STATIONS),
            vmem(STATIONS, STATIONS, kind=F32),
            vmem(CH, SLOTS),
            vmem(CH, STATIONS, kind=F32),
            vmem(CH, STATIONS, kind=F32),
            vmem(CH, STATIONS, kind=F32),
            vmem(CH, 256),
            vmem(CH, CH),
            vmem(3 * CH, CH),
            vmem(CH, CH),
            vmem(128, CH),
            vmem(128, STATIONS, kind=F32),
            vmem(128, STATIONS, kind=F32),
            vmem(2 * ROWS, SLOTS),
            vmem(2 * ROWS, CH, kind=F32),
            vmem(STATIONS, 128, kind=F32),
            pltpu.SemaphoreType.DMA((2, 8)),
            pltpu.SemaphoreType.DMA((2, 8)),
            pltpu.SemaphoreType.DMA((3,)),
            pltpu.SemaphoreType.DMA((3,)),
            pltpu.SemaphoreType.DMA((16,)),
            pltpu.SemaphoreType.DMA((16,)),
        ],
        compiler_params=pltpu.CompilerParams(
            collective_id=0, has_side_effects=True, vmem_limit_bytes=56 << 20
        ),
        name="whole",
    )(*operands)
    gradient, predicted = pl.pallas_call(
        back_kernel,
        out_shape=(
            jax.ShapeDtypeStruct((ROWS, CH, COLS), F32),
            jax.ShapeDtypeStruct((STATIONS, 128), F32),
        ),
        in_specs=[anywhere] * 4,
        out_specs=(anywhere,) * 2,
        scratch_shapes=[
            vmem(ROWS + 2, CH, COLS),
            vmem(ROWS, CH, COLS, kind=F32),
            vmem(CH, DEPTH),
            vmem(ROWS + 2, 3, CH, COLS),
            vmem(ROWS, CH, COLS, kind=F32),
            pltpu.SemaphoreType.DMA((14,)),
        ],
        compiler_params=pltpu.CompilerParams(vmem_limit_bytes=60 << 20),
        name="back",
    )(dpre, dfield, taps, predicted)
    return predicted, jnp.transpose(gradient, (0, 2, 1))


def solution(mesh):
    return jax.shard_map(
        on_device,
        mesh=mesh,
        in_specs=(
            P("lat", "lon", None),
            P(),
            P(LAT_LON, None),
            P(LAT_LON, None),
            P(LAT_LON, None),
            P(LAT_LON),
            P(LAT_LON, None),
            P(LAT_LON),
            P(LAT_LON, None),
            P(LAT_LON),
            P(),
            P(),
            P(),
            P(),
            P(),
            P(),
        ),
        out_specs=(P(LAT_LON, None), P("lat", "lon", None)),
        check_vma=False,
    )
```

time: 79.9 us -> 60.6 us (0.76)
  Pallas kernels: 73 us -> 59.1 us
  local copies, waits for them, and re-layouts: 5.46 us -> 0 us
    pallas_call x1, Pallas kernels: 73 us -> 52.2 us  [on_device(): pl.pallas_call(kernel, out_shape=(jax.ShapeDtypeStruct((STATIONS, 128), F...]
    pallas_call x0 -> x1, Pallas kernels: none -> 6.87 us  [on_device(): pl.pallas_call(back_kernel, out_shape=(jax.ShapeDtypeStruct((ROWS, CH, CO...]
    unnamed x2 -> x0, local copies, waits for them, and re-layouts: 5.46 us -> none
where the time goes in v3:
time: 60.6 us; the launch traced here: 60.5 us
  Pallas kernels  59.1 us (98%)
  between operations  1.45 us (2%)
    pallas_call x1, Pallas kernels, on_device(): pl.pallas_call(kernel, out_shape=(jax.ShapeDtypeStruct((STATIONS, 128), F...  52.2 us
    pallas_call x1, Pallas kernels, on_device(): pl.pallas_call(back_kernel, out_shape=(jax.ShapeDtypeStruct((ROWS, CH, CO...  6.87 us

profile of v3, /device:TPU:0, one launch (start us, length us, event | category | flops | bytes accessed | tf_op | source)
XLA Modules:
  0.0 60.5 jit_solution(9881100212949812061)
XLA Ops:
  1.3 52.2 %whole.1 = (f32[256,128]{1,0:T(8,128)}, bf16[34,192,128]{2,1,0:T(8,128)(2,1)}, f32[32,192,128]{2,1,0:T(8,128)}, bf16[192,1792]{1,0:T(8,128)(2,1)}) custom-call(bf16[32,192,128]{2,1,0:T(8,128)(2,1)} %bitcast.12, bf16[9,192,192]{2,1,0:T(8,128)(2,1)} %refs_1_.1, f32[256,128]{1,0:T(8,128)} %refs_2_.1, s32[256,128]{1,0:T(8,128)} %refs_3_.1, s32[1,256]{1,0:T(1,128)} %bitcast.16, ...), custom_call_target="tpu_custom_call" | custom-call | tf_op jit(solution)/shard_map/whole/pallas_call | solution.py:534
  53.5 6.9 %back.1 = (f32[32,192,128]{2,1,0:T(8,128)}, f32[256,128]{1,0:T(8,128)}) custom-call(bf16[34,192,128]{2,1,0:T(8,128)(2,1)} %get-tuple-element.8.refs_0_, f32[32,192,128]{2,1,0:T(8,128)} %get-tuple-element.9.refs_1_, bf16[192,1792]{1,0:T(8,128)(2,1)} %get-tuple-element.10.refs_2_, f32[256,128]{1,0:T(8,128)} %get-tuple-element.11.refs_3_), custom_call_target="tpu_custom_call" | custom-call | tf_op jit(solution)/shard_map/back/pallas_call | solution.py:595

commit v4 on v3

--- a/solution.py
+++ b/solution.py
@@ -67,10 +67,33 @@
     return jnp.concatenate([shifted[pl.ds(y, 3)].reshape(TAPS, COLS), hit.astype(F32).astype(BF16)], axis=0)
 
 
+def poles(lat):
+    return jnp.where(lat > 0, 1.0, 0.0), jnp.where(lat < N_LAT - 1, 1.0, 0.0)
+
+
+def side_terms(side_in, corner_in, conv_ref, taps, keep, backward):
+    total = []
+    for side in range(2):
+        above = corner_in[side].astype(F32)[15:16, 0:CH] * keep[0]
+        below = corner_in[2 + side].astype(F32)[0:1, 0:CH] * keep[1]
+        column = jnp.concatenate([above, side_in[side].astype(F32)[:, 0:CH], below], axis=0)
+        sums = None
+        for i in range(3):
+            piece = column[i : i + ROWS].astype(BF16)
+            if backward:
+                term = nt(piece, conv_ref[8 - (3 * i + 2 * side)])
+            else:
+                term = nn(piece, conv_ref[3 * i + 2 * side])
+            sums = term if sums is None else sums + term
+        total.append(sums)
+    total = jnp.concatenate(total + [jnp.zeros((64, CH), F32)], axis=0)
+    taps[:, TAPS:] = jnp.transpose(total)[:, 0 : 2 * ROWS].astype(BF16)
+
+
 def kernel(*refs):
-    (x_hbm, conv_hbm, observed_hbm, mask_hbm, tile_hbm, spot_hbm, neighbours_hbm, count_hbm) = refs[0:8]
-    (bias_hbm, live_hbm, in_hbm, gain1_hbm, qkv_hbm, out_hbm, gain2_hbm, head_hbm) = refs[8:16]
-    (predicted_hbm, dpre_hbm, dfield_hbm, taps_hbm) = refs[16:20]
+    inputs = refs[0:16]
+    (predicted_hbm, dpre_hbm, dfield_hbm, taps_hbm, rows_hbm, sides_hbm, corners_hbm) = refs[16:23]
+    refs = refs[3:]
     (x_ref, conv_ref, observed_ref, mask_ref, tile_ref, spot_ref, neighbours_ref, count_ref) = refs[20:28]
     (bias_ref, live_ref, in_ref, gain1_ref, qkv_ref, out_ref, gain2_ref, head_ref) = refs[28:36]
     (shifted, taps_f, taps_b, field, slope, spread, dpre, dfield, pick) = refs[36:45]
@@ -80,7 +103,7 @@
     (ends_spread, slope_ends, predicted_out) = refs[70:73]
     (halo_send, halo_recv, a2a_send, a2a_recv, load_sem, store_sem) = refs[73:79]
 
-    loads = [pltpu.make_async_copy(refs[k], refs[20 + k], load_sem.at[k]) for k in range(16)]
+    loads = [pltpu.make_async_copy(inputs[k], refs[20 + k], load_sem.at[k]) for k in range(16)]
     for k in (4, 5, 0, 1, 2, 3, 6, 7, 8, 9, 10, 11, 12, 13, 14, 15):
         loads[k].start()
     lat = lax.axis_index("lat")
@@ -89,7 +112,7 @@
     barrier = pltpu.get_barrier_semaphore()
 
     def coords(peer):
-        return (peer // N_LON, lax.rem(peer, N_LON))
+        return (lax.div(peer, N_LON), lax.rem(peer, N_LON))
 
     def greet(i, carry):
         pl.semaphore_signal(
@@ -108,6 +131,8 @@
     same = (tile_cols == tile_row) & (row_iota(square) < lane_iota(square))
     rank = jnp.sum(same.astype(F32), axis=0, keepdims=True)
     slot = tile_row * CAP + rank
+    ahead = tile_row - me.astype(F32)
+    ahead = jnp.where(ahead < 0.0, ahead + N, ahead)
     spot = spot_ref[...].astype(F32)
     spot_high = jnp.floor(spot * (1.0 / 256.0))
     spot_low = spot - 256.0 * spot_high
@@ -115,7 +140,7 @@
     wanted = jnp.where(part < CAP, spot_high, spot_low)
     wanted = jnp.where((part & (CAP - 1)).astype(F32) == rank, wanted, 0.0)
     wanted = jnp.where(part < 2 * CAP, wanted, 0.0).astype(BF16)
-    is_tile = (row_iota((N, STATIONS)).astype(F32) == tile_row).astype(BF16)
+    is_tile = (row_iota((N, STATIONS)).astype(F32) == ahead).astype(BF16)
     ask_out[...] = nt(is_tile, wanted).reshape(N, 1, 128)
 
     end = row_iota((2 * ROWS, ROWS * COLS))
@@ -128,17 +153,17 @@
     up, down = lax.rem(lat + N_LAT - 1, N_LAT), lax.rem(lat + 1, N_LAT)
     left, right = lax.rem(lon + N_LON - 1, N_LON), lax.rem(lon + 1, N_LON)
 
-    def halo_copies(turn, first, last):
+    def halo_copies(turn, first, last, rows_to, sides_to, corners_to):
         mine = side_out.at[turn]
         plan = [
-            (mine.at[pl.ds(0, ROWS)], side_in.at[turn, 1], (lat, left)),
-            (mine.at[pl.ds(ROWS, ROWS)], side_in.at[turn, 0], (lat, right)),
-            (mine.at[pl.ds(0, 16)], corner_in.at[turn, 3], (up, left)),
-            (mine.at[pl.ds(ROWS, 16)], corner_in.at[turn, 2], (up, right)),
-            (mine.at[pl.ds(16, 16)], corner_in.at[turn, 1], (down, left)),
-            (mine.at[pl.ds(ROWS + 16, 16)], corner_in.at[turn, 0], (down, right)),
-            (first, row_in.at[turn, 1], (up, lon)),
-            (last, row_in.at[turn, 0], (down, lon)),
+            (mine.at[pl.ds(0, ROWS)], sides_to.at[1], (lat, left)),
+            (mine.at[pl.ds(ROWS, ROWS)], sides_to.at[0], (lat, right)),
+            (mine.at[pl.ds(0, 16)], corners_to.at[3], (up, left)),
+            (mine.at[pl.ds(ROWS, 16)], corners_to.at[2], (up, right)),
+            (mine.at[pl.ds(16, 16)], corners_to.at[1], (down, left)),
+            (mine.at[pl.ds(ROWS + 16, 16)], corners_to.at[0], (down, right)),
+            (first, rows_to.at[1], (up, lon)),
+            (last, rows_to.at[0], (down, lon)),
         ]
         return [
             pltpu.make_async_remote_copy(
@@ -152,21 +177,19 @@
             for k, (source, target, where) in enumerate(plan)
         ]
 
-    def start_exchange(turn, source, target):
+    def start_exchange(turn, source, target, by_tile, first=1, last=N):
         def send(i, carry):
-            peer = lax.rem(me + i, N)
             pltpu.make_async_remote_copy(
-                src_ref=source.at[peer],
-                dst_ref=target.at[me],
+                src_ref=source.at[i],
+                dst_ref=target.at[me if by_tile else N - i],
                 send_sem=a2a_send.at[turn],
                 recv_sem=a2a_recv.at[turn],
-                device_id=coords(peer),
+                device_id=coords(lax.rem(me + i, N)),
                 device_id_type=pl.DeviceIdType.MESH,
             ).start()
             return carry
 
-        lax.fori_loop(1, N, send, 0)
-        target[me] = source[me]
+        lax.fori_loop(first, last, send, 0)
 
     def wait_received(turn, target):
         rest = target.at[pl.ds(0, N - 1)]
@@ -177,10 +200,11 @@
         pltpu.make_async_copy(rest, rest, a2a_send.at[turn]).wait()
 
     pl.semaphore_wait(barrier, N - 1)
-    first_halo = halo_copies(0, x_ref.at[0], x_ref.at[ROWS - 1])
+    first_halo = halo_copies(0, x_ref.at[0], x_ref.at[ROWS - 1], row_in, side_in, corner_in)
     for copy in first_halo:
         copy.start()
-    start_exchange(0, ask_out, ask_in)
+    start_exchange(0, ask_out, ask_in, False)
+    ask_in[0] = ask_out[0]
 
     def fill_row(y, carry):
         fill_shifted(shifted, y + 1, x_ref[y].astype(F32))
@@ -191,32 +215,12 @@
     for tap in range(9):
         taps_f[:, CH * tap : CH * (tap + 1)] = flipped(conv_ref[tap])
 
-    keep_up = jnp.where(lat > 0, 1.0, 0.0)
-    keep_down = jnp.where(lat < N_LAT - 1, 1.0, 0.0)
-
-    def side_terms(turn, taps, backward):
-        total = []
-        for side in range(2):
-            above = corner_in[turn, side].astype(F32)[15:16, 0:CH] * keep_up
-            below = corner_in[turn, 2 + side].astype(F32)[0:1, 0:CH] * keep_down
-            column = jnp.concatenate([above, side_in[turn, side].astype(F32)[:, 0:CH], below], axis=0)
-            sums = None
-            for i in range(3):
-                piece = column[i : i + ROWS].astype(BF16)
-                if backward:
-                    term = nt(piece, conv_ref[8 - (3 * i + 2 * side)])
-                else:
-                    term = nn(piece, conv_ref[3 * i + 2 * side])
-                sums = term if sums is None else sums + term
-            total.append(sums)
-        total = jnp.concatenate(total + [jnp.zeros((64, CH), F32)], axis=0)
-        taps[:, TAPS:] = jnp.transpose(total)[:, 0 : 2 * ROWS].astype(BF16)
-
+    keep = poles(lat)
     for copy in first_halo:
         copy.wait_recv()
-    fill_shifted(shifted, 0, row_in[0, 0].astype(F32) * keep_up)
-    fill_shifted(shifted, ROWS + 1, row_in[0, 1].astype(F32) * keep_down)
-    side_terms(0, taps_f, False)
+    fill_shifted(shifted, 0, row_in[0].astype(F32) * keep[0])
+    fill_shifted(shifted, ROWS + 1, row_in[1].astype(F32) * keep[1])
+    side_terms(side_in, corner_in, conv_ref, taps_f, keep, False)
 
     def forward_rows(pair, carry):
         y = pair * 2
@@ -254,27 +258,34 @@
 
     lax.fori_loop(0, ROWS, fill_spread, 0, unroll=4)
 
-    def send_wide(rows, out):
-        wide[pl.ds(0, SLOTS, 2)] = rows[:, 0:128]
-        wide[pl.ds(1, SLOTS, 2)] = jnp.concatenate([rows[:, 128:CH], jnp.zeros((SLOTS, 256 - CH), F32)], axis=1)
-        out[...] = wide[...].reshape(N, 2 * CAP, 128).astype(BF16)
+    def put_wide(half, rows, out):
+        count = SLOTS // 2
+        at = half * SLOTS
+        wide[pl.ds(at, count, 2)] = rows[:, 0:128]
+        wide[pl.ds(at + 1, count, 2)] = jnp.concatenate([rows[:, 128:CH], jnp.zeros((count, 256 - CH), F32)], axis=1)
+        out[pl.ds(half * (N // 2), N // 2)] = wide[pl.ds(at, SLOTS)].reshape(N // 2, 2 * CAP, 128).astype(BF16)
 
     def read_wide(held):
         wide[...] = held[...].astype(F32).reshape(2 * SLOTS, 128)
         return wide[pl.ds(0, SLOTS, 2)], wide[pl.ds(1, SLOTS, 2)]
 
-    sampled = jnp.zeros((SLOTS, CH), F32)
-    for eighth in range(4):
-        rows = [8 * eighth + k for k in range(8)]
-        sampled = sampled + nt(
-            jnp.concatenate([spread[y] for y in rows], axis=1), jnp.concatenate([field[y] for y in rows], axis=1)
-        )
-    send_wide(sampled, answer_out)
-    start_exchange(1, answer_out, answer_in)
+    for half in range(2):
+        of_half = pl.ds(half * (SLOTS // 2), SLOTS // 2)
+        sampled = None
+        for part in range(4):
+            rows = [8 * part + k for k in range(8)]
+            term = nt(
+                jnp.concatenate([spread[y, of_half] for y in rows], axis=1),
+                jnp.concatenate([field[y] for y in rows], axis=1),
+            )
+            sampled = term if sampled is None else sampled + term
+        put_wide(half, sampled, answer_out)
+        start_exchange(1, answer_out, answer_in, True, max(1, half * (N // 2)), (half + 1) * (N // 2))
+    answer_in[me] = answer_out[0]
 
     for k in (2, 3, 6, 7, 8, 9, 10, 11, 12, 13, 14, 15):
         loads[k].wait()
-    select_t[...] = (row_iota((SLOTS, STATIONS)).astype(F32) == slot).astype(BF16)
+    select_t[...] = (row_iota((SLOTS, STATIONS)).astype(F32) == ahead * CAP + rank).astype(BF16)
     slot_cols = as_columns(slot)
     slot_cols = jnp.concatenate([slot_cols] * (SLOTS // 128), axis=1)
     select[...] = (lane_iota((STATIONS, SLOTS)).astype(F32) == slot_cols).astype(BF16)
@@ -361,14 +372,19 @@
     d_unit1 = nn(qkv_ref[...], d_projected) * gain1[...]
     d_embedded = d_residual + scale1 * (d_unit1 - unit1 * jnp.mean(d_unit1 * unit1, axis=0, keepdims=True))
     d_interp = nn(in_low_t[...], d_embedded.astype(BF16)).astype(BF16)
-    send_wide(nt(select_t[...], d_interp), grads_out)
-    start_exchange(2, grads_out, grads_in)
+    for half in range(2):
+        put_wide(half, nt(select_t[pl.ds(half * (SLOTS // 2), SLOTS // 2)], d_interp), grads_out)
+        start_exchange(2, grads_out, grads_in, False, max(1, half * (N // 2)), (half + 1) * (N // 2))
+    grads_in[0] = grads_out[0]
 
     predicted_out[...] = jnp.transpose(predicted)
     stores = [pltpu.make_async_copy(predicted_out, predicted_hbm, store_sem.at[0])]
     stores[0].start()
     for tap in range(9):
         taps_b[:, CH * tap : CH * (tap + 1)] = conv_ref[8 - tap]
+    taps_b[:, TAPS:] = jnp.zeros((CH, 2 * ROWS), BF16)
+    stores.append(pltpu.make_async_copy(taps_b, taps_hbm, store_sem.at[1]))
+    stores[1].start()
     slope_ends[...] = nt(pick[...], jnp.concatenate([slope[y] for y in range(ROWS)], axis=1))
     end_row = (place & (ROWS - 1)).astype(F32)
     end_col = jnp.where(place < ROWS, 0.0, COLS - 1.0)
@@ -389,10 +405,10 @@
         for k, y in enumerate((y0, y1)):
             value = both[:, COLS * k : COLS * (k + 1)]
             dfield[y] = value
-            dpre[y + 1] = (value * slope[y].astype(F32)).astype(BF16)
+            dpre[y] = (value * slope[y].astype(F32)).astype(BF16)
 
     scatter_pair(0, ROWS - 1)
-    second_halo = halo_copies(1, dpre.at[1], dpre.at[ROWS])
+    second_halo = halo_copies(1, dpre.at[0], dpre.at[ROWS - 1], rows_hbm, sides_hbm, corners_hbm)
     for copy in second_halo:
         copy.start()
 
@@ -403,6 +419,8 @@
 
     store(dfield.at[pl.ds(0, 1)], dfield_hbm.at[pl.ds(0, 1)])
     store(dfield.at[pl.ds(ROWS - 1, 1)], dfield_hbm.at[pl.ds(ROWS - 1, 1)])
+    store(dpre.at[pl.ds(0, 1)], dpre_hbm.at[pl.ds(0, 1)])
+    store(dpre.at[pl.ds(ROWS - 1, 1)], dpre_hbm.at[pl.ds(ROWS - 1, 1)])
     for third in range(3):
 
         def scatter_rows(pair, carry):
@@ -413,16 +431,9 @@
         lax.fori_loop(0, 5, scatter_rows, 0, unroll=True)
         at = pl.ds(1 + 10 * third, 10)
         store(dfield.at[at], dfield_hbm.at[at])
-        at = pl.ds(2 + 10 * third, 10)
         store(dpre.at[at], dpre_hbm.at[at])
     for copy in second_halo:
         copy.wait_recv()
-    dpre[0] = (row_in[1, 0].astype(F32) * keep_up).astype(BF16)
-    dpre[ROWS + 1] = (row_in[1, 1].astype(F32) * keep_down).astype(BF16)
-    store(dpre.at[pl.ds(0, 2)], dpre_hbm.at[pl.ds(0, 2)])
-    store(dpre.at[pl.ds(ROWS, 2)], dpre_hbm.at[pl.ds(ROWS, 2)])
-    side_terms(1, taps_b, True)
-    store(taps_b, taps_hbm)
     for copy in second_halo:
         copy.wait_send()
     wait_sent(0, ask_out)
@@ -432,56 +443,62 @@
         copy.wait()
 
 
+PARTS = ((0, 4), (4, 10), (14, 10), (24, 8))
+
+
 def back_kernel(*refs):
-    (dpre_hbm, dfield_hbm, taps_hbm, predicted_hbm, grad_hbm, predicted_to) = refs[0:6]
-    (dpre, dfield, taps, shifted, grad, sem) = refs[6:12]
-    through = pltpu.make_async_copy(predicted_hbm, predicted_to, sem.at[0])
-    load_taps = pltpu.make_async_copy(taps_hbm, taps, sem.at[1])
+    (dpre_hbm, dfield_hbm, predicted_hbm, grad_hbm, predicted_to) = refs[0:2] + refs[7:10]
+    (dpre, dfield, taps, row_in, side_in, corner_in, conv_ref, shifted, grad, sem) = refs[10:20]
+    keep = poles(lax.axis_index("lat"))
+    small = [pltpu.make_async_copy(refs[k], refs[10 + k], sem.at[k]) for k in range(2, 7)]
+    load_taps, load_rows, load_sides, load_corners, load_conv = small
+    through = pltpu.make_async_copy(predicted_hbm, predicted_to, sem.at[7])
 
     def load(part):
-        at = pl.ds(0, 10) if part == 0 else pl.ds(8 * part + 2, 8)
-        fields = pl.ds(8 * part, 8)
+        first, count = PARTS[part]
+        begin = first + 1 if part else 0
+        end = min(first + count + 1, ROWS)
+        at, fields = pl.ds(begin, end - begin), pl.ds(first, count)
         return (
-            pltpu.make_async_copy(dpre_hbm.at[at], dpre.at[at], sem.at[2 + part]),
-            pltpu.make_async_copy(dfield_hbm.at[fields], dfield.at[fields], sem.at[6 + part]),
+            pltpu.make_async_copy(dpre_hbm.at[at], dpre.at[at], sem.at[8 + part]),
+            pltpu.make_async_copy(dfield_hbm.at[fields], dfield.at[fields], sem.at[12 + part]),
         )
 
     def store(part):
-        fields = pl.ds(8 * part, 8)
-        return pltpu.make_async_copy(grad.at[fields], grad_hbm.at[fields], sem.at[10 + part])
+        fields = pl.ds(*PARTS[part])
+        return pltpu.make_async_copy(grad.at[fields], grad_hbm.at[fields], sem.at[16 + part])
 
     loads = [load(part) for part in range(4)]
-    loads[0][0].start()
-    load_taps.start()
-    loads[0][1].start()
+    for copy in (load_sides, load_corners, load_conv, load_rows, loads[0][0], load_taps, loads[0][1]):
+        copy.start()
     for part in range(1, 4):
         for copy in loads[part]:
             copy.start()
     through.start()
 
     def shift_part(part):
+        first, count = PARTS[part]
         loads[part][0].wait()
-
-        def shift_row(k, carry):
-            fill_shifted(shifted, k, dpre[k].astype(F32))
-            return carry
-
-        first = 0 if part == 0 else 8 * part + 2
-        lax.fori_loop(first, 8 * part + 10, shift_row, 0, unroll=True)
-
+        if part == 0:
+            fill_shifted(shifted, 0, row_in[0].astype(F32) * keep[0])
+        for y in range(first + 1 if part else 0, min(first + count + 1, ROWS)):
+            fill_shifted(shifted, y + 1, dpre[y].astype(F32))
+        if part == 3:
+            fill_shifted(shifted, ROWS + 1, row_in[1].astype(F32) * keep[1])
+
+    load_rows.wait()
     shift_part(0)
-    load_taps.wait()
+    for copy in (load_taps, load_sides, load_corners, load_conv):
+        copy.wait()
+    side_terms(side_in, corner_in, conv_ref, taps, keep, True)
     for part in range(4):
         loads[part][1].wait()
-
-        def backward_rows(pair, carry):
-            y = 8 * part + pair * 2
+        first, count = PARTS[part]
+        for pair in range(count // 2):
+            y = first + pair * 2
             back = nn(taps[...], jnp.concatenate([around(shifted, y), around(shifted, y + 1)], axis=1))
             for k in range(2):
                 grad[y + k] = dfield[y + k] + back[:, COLS * k : COLS * (k + 1)]
-            return carry
-
-        lax.fori_loop(0, 4, backward_rows, 0, unroll=True)
         store(part).start()
         if part < 3:
             shift_part(part + 1)
@@ -531,16 +548,19 @@
     def vmem(*shape, kind=BF16):
         return pltpu.VMEM(shape, kind)
 
-    predicted, dpre, dfield, taps = pl.pallas_call(
+    predicted, dpre, dfield, taps, rows, sides, corners = pl.pallas_call(
         kernel,
         out_shape=(
             jax.ShapeDtypeStruct((STATIONS, 128), F32),
-            jax.ShapeDtypeStruct((ROWS + 2, CH, COLS), BF16),
+            jax.ShapeDtypeStruct((ROWS, CH, COLS), BF16),
             jax.ShapeDtypeStruct((ROWS, CH, COLS), F32),
             jax.ShapeDtypeStruct((CH, DEPTH), BF16),
+            jax.ShapeDtypeStruct((2, CH, COLS), BF16),
+            jax.ShapeDtypeStruct((2, ROWS, 256), BF16),
+            jax.ShapeDtypeStruct((4, 16, 256), BF16),
         ),
         in_specs=[anywhere] * len(operands),
-        out_specs=(anywhere,) * 4,
+        out_specs=(anywhere,) * 7,
         scratch_shapes=[pltpu.VMEM(o.shape, o.dtype) for o in operands]
         + [
             vmem(ROWS + 2, 3, CH, COLS),
@@ -549,7 +569,7 @@
             vmem(ROWS, CH, COLS),
             vmem(ROWS, CH, COLS),
             vmem(ROWS, SLOTS, COLS),
-            vmem(ROWS + 2, CH, COLS),
+            vmem(ROWS, CH, COLS),
             vmem(ROWS, CH, COLS, kind=F32),
             vmem(2 * ROWS, ROWS * COLS),
             vmem(N, 2 * CAP, 128),
@@ -559,10 +579,10 @@
             vmem(N, 1, 128, kind=F32),
             vmem(N, 1, 128, kind=F32),
             vmem(2 * SLOTS, 128, kind=F32),
-            vmem(2, 2, CH, COLS),
+            vmem(2, CH, COLS),
             vmem(2, 2 * ROWS, 256),
-            vmem(2, 2, ROWS, 256),
-            vmem(2, 4, 16, 256),
+            vmem(2, ROWS, 256),
+            vmem(4, 16, 256),
             vmem(STATIONS, SLOTS),
             vmem(SLOTS, STATIONS),
             vmem(STATIONS, STATIONS, kind=F32),
@@ -598,19 +618,23 @@
             jax.ShapeDtypeStruct((ROWS, CH, COLS), F32),
             jax.ShapeDtypeStruct((STATIONS, 128), F32),
         ),
-        in_specs=[anywhere] * 4,
-        out_specs=(anywhere,) * 2,
+        in_specs=[anywhere] * 8,
+        out_specs=(anywhere, anywhere),
         scratch_shapes=[
-            vmem(ROWS + 2, CH, COLS),
+            vmem(ROWS, CH, COLS),
             vmem(ROWS, CH, COLS, kind=F32),
             vmem(CH, DEPTH),
+            vmem(2, CH, COLS),
+            vmem(2, ROWS, 256),
+            vmem(4, 16, 256),
+            vmem(9, CH, CH),
             vmem(ROWS + 2, 3, CH, COLS),
             vmem(ROWS, CH, COLS, kind=F32),
-            pltpu.SemaphoreType.DMA((14,)),
+            pltpu.SemaphoreType.DMA((20,)),
         ],
         compiler_params=pltpu.CompilerParams(vmem_limit_bytes=60 << 20),
         name="back",
-    )(dpre, dfield, taps, predicted)
+    )(dpre, dfield, taps, rows, sides, corners, conv_weight, predicted)
     return predicted, jnp.transpose(gradient, (0, 2, 1))
 
 

time: 60.6 us -> 57.8 us (0.954)
  Pallas kernels: 59.1 us -> 56.3 us
    pallas_call x1, Pallas kernels: 52.2 us -> 48.4 us  [on_device(): pl.pallas_call(kernel, out_shape=(jax.ShapeDtypeStruct((STATIONS, 128), F...]
    pallas_call x1, Pallas kernels: 6.87 us -> 7.84 us  [on_device(): pl.pallas_call(back_kernel, out_shape=(jax.ShapeDtypeStruct((ROWS, CH, CO...]
where the time goes in v4:
time: 57.8 us; the launch traced here: 57.7 us
  Pallas kernels  56.3 us (97%)
  between operations  1.45 us (3%)
    pallas_call x1, Pallas kernels, on_device(): pl.pallas_call(kernel, out_shape=(jax.ShapeDtypeStruct((STATIONS, 128), F...  48.4 us
    pallas_call x1, Pallas kernels, on_device(): pl.pallas_call(back_kernel, out_shape=(jax.ShapeDtypeStruct((ROWS, CH, CO...  7.84 us

profile of v4, /device:TPU:0, one launch (start us, length us, event | category | flops | bytes accessed | tf_op | source)
XLA Modules:
  0.0 57.7 jit_solution(6686232646996827849)
XLA Ops:
  1.3 48.4 %whole.1 = (f32[256,128]{1,0:T(8,128)}, bf16[32,192,128]{2,1,0:T(8,128)(2,1)}, f32[32,192,128]{2,1,0:T(8,128)}, bf16[192,1792]{1,0:T(8,128)(2,1)}, bf16[2,192,12...) custom-call(bf16[32,192,128]{2,1,0:T(8,128)(2,1)} %bitcast.12, ...), custom_call_target="tpu_custom_call" | custom-call | tf_op jit(solution)/shard_map/whole/pallas_call | solution.py:551
  49.7 7.8 %back.1 = (f32[32,192,128]{2,1,0:T(8,128)}, f32[256,128]{1,0:T(8,128)}) custom-call(bf16[32,192,128]{2,1,0:T(8,128)(2,1)} %get-tuple-element.11.refs_0_, f32[32,192,128]{2,1,0:T(8,128)} %get-tuple-element.12.refs_1_, bf16[192,1792]{1,0:T(8,128)(2,1)} %get-tuple-element.13.refs_2_, bf16[2,192,128]{2,1,0:T(8,128)(2,1)} %get-tuple-element.14.refs_3_, ...), custom_call_target="tpu_custom_call" | custom-call | tf_op jit(solution)/shard_map/back/pallas_call | solution.py:615

commit v5 on v4

--- a/solution.py
+++ b/solution.py
@@ -23,6 +23,9 @@
 F32 = jnp.float32
 BF16 = jnp.bfloat16
 LAT_LON = ("lat", "lon")
+HOPS = (0, 1, 2, 1)
+GROUPS = sorted(((dx, dz) for dx in range(4) for dz in range(4)), key=lambda d: -HOPS[d[0]] - HOPS[d[1]])
+OWN = 8 * GROUPS.index((0, 0)) + 5
 
 
 def nn(a, b):
@@ -100,8 +103,8 @@
     (answer_out, answer_in, grads_out, grads_in, ask_out, ask_in, wide) = refs[45:52]
     (row_in, side_out, side_in, corner_in, select, select_t, scores_bias, grads_t) = refs[52:60]
     (embedded0, gain1, gain2, in_low, in_low_t, qkv_t, out_t, head_t, mask_t, observed_t) = refs[60:70]
-    (ends_spread, slope_ends, predicted_out) = refs[70:73]
-    (halo_send, halo_recv, a2a_send, a2a_recv, load_sem, store_sem) = refs[73:79]
+    (ends_spread, slope_ends, predicted_out, before) = refs[70:74]
+    (halo_send, halo_recv, a2a_send, a2a_recv, load_sem, store_sem) = refs[74:80]
 
     loads = [pltpu.make_async_copy(inputs[k], refs[20 + k], load_sem.at[k]) for k in range(16)]
     for k in (4, 5, 0, 1, 2, 3, 6, 7, 8, 9, 10, 11, 12, 13, 14, 15):
@@ -109,6 +112,8 @@
     lat = lax.axis_index("lat")
     lon = lax.axis_index("lon")
     me = lat * N_LON + lon
+    at_z, at_core = lax.div(lon, 8), lax.rem(lon, 2)
+    at_y = lax.rem(lax.div(lon, 2), 4)
     barrier = pltpu.get_barrier_semaphore()
 
     def coords(peer):
@@ -131,8 +136,22 @@
     same = (tile_cols == tile_row) & (row_iota(square) < lane_iota(square))
     rank = jnp.sum(same.astype(F32), axis=0, keepdims=True)
     slot = tile_row * CAP + rank
-    ahead = tile_row - me.astype(F32)
-    ahead = jnp.where(ahead < 0.0, ahead + N, ahead)
+
+    def ring(value, here):
+        ahead = value - here.astype(F32)
+        return jnp.where(ahead < 0.0, ahead + 4.0, ahead)
+
+    tile_x = jnp.floor(tile_row * (1.0 / 32.0))
+    tile_z = jnp.floor((tile_row - 32.0 * tile_x) * (1.0 / 8.0))
+    tile_pair = jnp.floor(tile_row * 0.5)
+    tile_y = tile_pair - 4.0 * jnp.floor(tile_pair * 0.25)
+    step = 4.0 * ring(tile_x, lat) + ring(tile_z, at_z)
+    group = jnp.zeros_like(step)
+    for index, (dx, dz) in enumerate(GROUPS):
+        group = jnp.where(step == 4.0 * dx + dz, float(index), group)
+    back_y = ring(2.0 - ring(tile_y, at_y), jnp.int32(0))
+    same_core = 1.0 - jnp.abs(tile_row - 2.0 * tile_pair - at_core.astype(F32))
+    ahead = 8.0 * group + 2.0 * back_y + same_core
     spot = spot_ref[...].astype(F32)
     spot_high = jnp.floor(spot * (1.0 / 256.0))
     spot_low = spot - 256.0 * spot_high
@@ -177,19 +196,31 @@
             for k, (source, target, where) in enumerate(plan)
         ]
 
-    def start_exchange(turn, source, target, by_tile, first=1, last=N):
-        def send(i, carry):
-            pltpu.make_async_remote_copy(
-                src_ref=source.at[i],
-                dst_ref=target.at[me if by_tile else N - i],
-                send_sem=a2a_send.at[turn],
-                recv_sem=a2a_recv.at[turn],
-                device_id=coords(lax.rem(me + i, N)),
-                device_id_type=pl.DeviceIdType.MESH,
-            ).start()
-            return carry
-
-        lax.fori_loop(first, last, send, 0)
+    def start_exchange(turn, source, target, by_tile, first=0, last=16):
+        for group in range(first, last):
+            dx, dz = GROUPS[group]
+            opposite = GROUPS.index((-dx % 4, -dz % 4))
+
+            def send(k, carry):
+                d = lax.div(k, 2)
+                e = k - 2 * d
+                x, z = lax.rem(lat + dx, 4), lax.rem(at_z + dz, 4)
+                y, core = lax.rem(at_y + 6 - d, 4), lax.rem(at_core + 1 - e, 2)
+                pltpu.make_async_remote_copy(
+                    src_ref=source.at[8 * group + k],
+                    dst_ref=target.at[me if by_tile else 8 * opposite + 2 * lax.rem(4 - d, 4) + e],
+                    send_sem=a2a_send.at[turn],
+                    recv_sem=a2a_recv.at[turn],
+                    device_id=(x, (z * 4 + y) * 2 + core),
+                    device_id_type=pl.DeviceIdType.MESH,
+                ).start()
+                return carry
+
+            if OWN // 8 == group:
+                lax.fori_loop(0, OWN % 8, send, 0)
+                lax.fori_loop(OWN % 8 + 1, 8, send, 0)
+            else:
+                lax.fori_loop(0, 8, send, 0)
 
     def wait_received(turn, target):
         rest = target.at[pl.ds(0, N - 1)]
@@ -204,7 +235,7 @@
     for copy in first_halo:
         copy.start()
     start_exchange(0, ask_out, ask_in, False)
-    ask_in[0] = ask_out[0]
+    ask_in[OWN] = ask_out[OWN]
 
     def fill_row(y, carry):
         fill_shifted(shifted, y + 1, x_ref[y].astype(F32))
@@ -227,11 +258,10 @@
         pre = nn(taps_f[...], jnp.concatenate([around(shifted, y), around(shifted, y + 1)], axis=1))
         gate = sigmoid(pre)
         moved = pre * gate
-        tilt = gate * (1.0 + pre * (1.0 - gate))
         for k in range(2):
             cut = slice(COLS * k, COLS * (k + 1))
             field[y + k] = (x_ref[y + k].astype(F32) + moved[:, cut]).astype(BF16)
-            slope[y + k] = tilt[:, cut].astype(BF16)
+            before[y + k] = pre[:, cut]
         return carry
 
     lax.fori_loop(0, ROWS // 2, forward_rows, 0, unroll=4)
@@ -280,8 +310,8 @@
             )
             sampled = term if sampled is None else sampled + term
         put_wide(half, sampled, answer_out)
-        start_exchange(1, answer_out, answer_in, True, max(1, half * (N // 2)), (half + 1) * (N // 2))
-    answer_in[me] = answer_out[0]
+        start_exchange(1, answer_out, answer_in, True, half * 8, half * 8 + 8)
+    answer_in[me] = answer_out[OWN]
 
     for k in (2, 3, 6, 7, 8, 9, 10, 11, 12, 13, 14, 15):
         loads[k].wait()
@@ -374,8 +404,8 @@
     d_interp = nn(in_low_t[...], d_embedded.astype(BF16)).astype(BF16)
     for half in range(2):
         put_wide(half, nt(select_t[pl.ds(half * (SLOTS // 2), SLOTS // 2)], d_interp), grads_out)
-        start_exchange(2, grads_out, grads_in, False, max(1, half * (N // 2)), (half + 1) * (N // 2))
-    grads_in[0] = grads_out[0]
+        start_exchange(2, grads_out, grads_in, False, half * 8, half * 8 + 8)
+    grads_in[OWN] = grads_out[OWN]
 
     predicted_out[...] = jnp.transpose(predicted)
     stores = [pltpu.make_async_copy(predicted_out, predicted_hbm, store_sem.at[0])]
@@ -385,6 +415,14 @@
     taps_b[:, TAPS:] = jnp.zeros((CH, 2 * ROWS), BF16)
     stores.append(pltpu.make_async_copy(taps_b, taps_hbm, store_sem.at[1]))
     stores[1].start()
+
+    def fill_slope(y, carry):
+        pre = before[y]
+        gate = sigmoid(pre)
+        slope[y] = (gate * (1.0 + pre * (1.0 - gate))).astype(BF16)
+        return carry
+
+    lax.fori_loop(0, ROWS, fill_slope, 0, unroll=2)
     slope_ends[...] = nt(pick[...], jnp.concatenate([slope[y] for y in range(ROWS)], axis=1))
     end_row = (place & (ROWS - 1)).astype(F32)
     end_col = jnp.where(place < ROWS, 0.0, COLS - 1.0)
@@ -476,32 +514,42 @@
             copy.start()
     through.start()
 
-    def shift_part(part):
+    def rows_of(part):
         first, count = PARTS[part]
-        loads[part][0].wait()
-        if part == 0:
+        return list(range(first + 1 if part else -1, min(first + count + 1, ROWS))) + ([ROWS] if part == 3 else [])
+
+    def shift_row(y):
+        if y < 0:
             fill_shifted(shifted, 0, row_in[0].astype(F32) * keep[0])
-        for y in range(first + 1 if part else 0, min(first + count + 1, ROWS)):
+        elif y == ROWS:
+            fill_shifted(shifted, ROWS + 1, row_in[1].astype(F32) * keep[1])
+        else:
             fill_shifted(shifted, y + 1, dpre[y].astype(F32))
-        if part == 3:
-            fill_shifted(shifted, ROWS + 1, row_in[1].astype(F32) * keep[1])
-
-    load_rows.wait()
-    shift_part(0)
-    for copy in (load_taps, load_sides, load_corners, load_conv):
+
+    for copy in (load_sides, load_corners, load_conv, load_taps):
         copy.wait()
     side_terms(side_in, corner_in, conv_ref, taps, keep, True)
+    load_rows.wait()
+    loads[0][0].wait()
+    for y in rows_of(0):
+        shift_row(y)
     for part in range(4):
         loads[part][1].wait()
         first, count = PARTS[part]
+        coming = []
+        if part < 3:
+            loads[part + 1][0].wait()
+            coming = rows_of(part + 1)
         for pair in range(count // 2):
             y = first + pair * 2
             back = nn(taps[...], jnp.concatenate([around(shifted, y), around(shifted, y + 1)], axis=1))
             for k in range(2):
                 grad[y + k] = dfield[y + k] + back[:, COLS * k : COLS * (k + 1)]
+            share = -(-len(coming) // (count // 2 - pair))
+            for row in coming[:share]:
+                shift_row(row)
+            coming = coming[share:]
         store(part).start()
-        if part < 3:
-            shift_part(part + 1)
     for part in range(4):
         store(part).wait()
     through.wait()
@@ -600,6 +648,7 @@
             vmem(2 * ROWS, SLOTS),
             vmem(2 * ROWS, CH, kind=F32),
             vmem(STATIONS, 128, kind=F32),
+            vmem(ROWS, CH, COLS, kind=F32),
             pltpu.SemaphoreType.DMA((2, 8)),
             pltpu.SemaphoreType.DMA((2, 8)),
             pltpu.SemaphoreType.DMA((3,)),

time: 57.8 us -> 55.6 us (0.962)
  Pallas kernels: 56.3 us -> 54.1 us
    pallas_call x1, Pallas kernels: 48.4 us -> 46.9 us  [on_device(): pl.pallas_call(kernel, out_shape=(jax.ShapeDtypeStruct((STATIONS, 128), F...]
    pallas_call x1, Pallas kernels: 7.84 us -> 7.14 us  [on_device(): pl.pallas_call(back_kernel, out_shape=(jax.ShapeDtypeStruct((ROWS, CH, CO...]
where the time goes in v5:
time: 55.6 us; the launch traced here: 55.5 us
  Pallas kernels  54.1 us (97%)
  between operations  1.45 us (3%)
    pallas_call x1, Pallas kernels, on_device(): pl.pallas_call(kernel, out_shape=(jax.ShapeDtypeStruct((STATIONS, 128), F...  46.9 us
    pallas_call x1, Pallas kernels, on_device(): pl.pallas_call(back_kernel, out_shape=(jax.ShapeDtypeStruct((ROWS, CH, CO...  7.14 us

profile of v5, /device:TPU:0, one launch (start us, length us, event | category | flops | bytes accessed | tf_op | source)
XLA Modules:
  0.0 55.5 jit_solution(6488109868240338210)
XLA Ops:
  1.3 46.9 %whole.1 = (f32[256,128]{1,0:T(8,128)}, bf16[32,192,128]{2,1,0:T(8,128)(2,1)}, f32[32,192,128]{2,1,0:T(8,128)}, bf16[192,1792]{1,0:T(8,128)(2,1)}, bf16[2,192,12...) custom-call(bf16[32,192,128]{2,1,0:T(8,128)(2,1)} %bitcast.12, ...), custom_call_target="tpu_custom_call" | custom-call | tf_op jit(solution)/shard_map/whole/pallas_call | solution.py:599
  48.2 7.1 %back.1 = (f32[32,192,128]{2,1,0:T(8,128)}, f32[256,128]{1,0:T(8,128)}) custom-call(bf16[32,192,128]{2,1,0:T(8,128)(2,1)} %get-tuple-element.11.refs_0_, f32[32,192,128]{2,1,0:T(8,128)} %get-tuple-element.12.refs_1_, bf16[192,1792]{1,0:T(8,128)(2,1)} %get-tuple-element.13.refs_2_, bf16[2,192,128]{2,1,0:T(8,128)(2,1)} %get-tuple-element.14.refs_3_, ...), custom_call_target="tpu_custom_call" | custom-call | tf_op jit(solution)/shard_map/back/pallas_call | solution.py:664

commit v6 on v5

--- a/solution.py
+++ b/solution.py
@@ -63,11 +63,20 @@
     shifted[y, 2] = jnp.where(lane == COLS - 1, 0.0, pltpu.roll(value, COLS - 1, 1)).astype(BF16)
 
 
-def around(shifted, y):
+def end_hits(y):
     ends_at = row_iota((2 * ROWS, COLS))
     lane = lane_iota((2 * ROWS, COLS))
     hit = ((ends_at == y) & (lane == 0)) | ((ends_at == y + ROWS) & (lane == COLS - 1))
-    return jnp.concatenate([shifted[pl.ds(y, 3)].reshape(TAPS, COLS), hit.astype(F32).astype(BF16)], axis=0)
+    return hit.astype(F32).astype(BF16)
+
+
+def around(shifted, y):
+    return jnp.concatenate([shifted[pl.ds(y, 3)].reshape(TAPS, COLS), end_hits(y)], axis=0)
+
+
+PARTS = ((0, 4), (4, 10), (14, 10), (24, 8))
+EARLY = 2
+COMING = (tuple(range(0, 5)), tuple(range(5, 15)), (), tuple(range(23, 32)))
 
 
 def poles(lat):
@@ -467,9 +476,20 @@
             return carry
 
         lax.fori_loop(0, 5, scatter_rows, 0, unroll=True)
+        at = (pl.ds(1, 10), pl.ds(11, 3), pl.ds(24, 7))[third]
+        store(dfield.at[at], dfield_hbm.at[at])
         at = pl.ds(1 + 10 * third, 10)
-        store(dfield.at[at], dfield_hbm.at[at])
         store(dpre.at[at], dpre_hbm.at[at])
+    first, count = PARTS[EARLY]
+    for y in range(first - 1, first + 3):
+        fill_shifted(shifted, y + 1, dpre[y].astype(F32))
+    for y in range(first, first + count, 2):
+        back = nn(taps_b[...], jnp.concatenate([around(shifted, y), around(shifted, y + 1)], axis=1))
+        for k in range(2):
+            dfield[y + k] = dfield[y + k] + back[:, COLS * k : COLS * (k + 1)]
+            if y + 2 < first + count:
+                fill_shifted(shifted, y + k + 4, dpre[y + k + 3].astype(F32))
+    store(dfield.at[pl.ds(first, count)], dfield_hbm.at[pl.ds(first, count)])
     for copy in second_halo:
         copy.wait_recv()
     for copy in second_halo:
@@ -481,9 +501,6 @@
         copy.wait()
 
 
-PARTS = ((0, 4), (4, 10), (14, 10), (24, 8))
-
-
 def back_kernel(*refs):
     (dpre_hbm, dfield_hbm, predicted_hbm, grad_hbm, predicted_to) = refs[0:2] + refs[7:10]
     (dpre, dfield, taps, row_in, side_in, corner_in, conv_ref, shifted, grad, sem) = refs[10:20]
@@ -493,30 +510,24 @@
     through = pltpu.make_async_copy(predicted_hbm, predicted_to, sem.at[7])
 
     def load(part):
-        first, count = PARTS[part]
-        begin = first + 1 if part else 0
-        end = min(first + count + 1, ROWS)
-        at, fields = pl.ds(begin, end - begin), pl.ds(first, count)
-        return (
-            pltpu.make_async_copy(dpre_hbm.at[at], dpre.at[at], sem.at[8 + part]),
-            pltpu.make_async_copy(dfield_hbm.at[fields], dfield.at[fields], sem.at[12 + part]),
-        )
+        fields = pl.ds(*PARTS[part])
+        copies = [pltpu.make_async_copy(dfield_hbm.at[fields], dfield.at[fields], sem.at[12 + part])]
+        if COMING[part]:
+            at = pl.ds(COMING[part][0], len(COMING[part]))
+            copies.append(pltpu.make_async_copy(dpre_hbm.at[at], dpre.at[at], sem.at[8 + part]))
+        return copies
 
     def store(part):
         fields = pl.ds(*PARTS[part])
         return pltpu.make_async_copy(grad.at[fields], grad_hbm.at[fields], sem.at[16 + part])
 
     loads = [load(part) for part in range(4)]
-    for copy in (load_sides, load_corners, load_conv, load_rows, loads[0][0], load_taps, loads[0][1]):
+    for copy in (load_sides, load_corners, load_conv, load_rows, loads[0][1], load_taps, loads[0][0]):
         copy.start()
     for part in range(1, 4):
-        for copy in loads[part]:
+        for copy in reversed(loads[part]):
             copy.start()
     through.start()
-
-    def rows_of(part):
-        first, count = PARTS[part]
-        return list(range(first + 1 if part else -1, min(first + count + 1, ROWS))) + ([ROWS] if part == 3 else [])
 
     def shift_row(y):
         if y < 0:
@@ -530,19 +541,26 @@
         copy.wait()
     side_terms(side_in, corner_in, conv_ref, taps, keep, True)
     load_rows.wait()
-    loads[0][0].wait()
-    for y in rows_of(0):
+    loads[0][1].wait()
+    for y in (-1,) + COMING[0]:
         shift_row(y)
+    end_taps = taps[:, TAPS:]
     for part in range(4):
-        loads[part][1].wait()
+        loads[part][0].wait()
         first, count = PARTS[part]
         coming = []
-        if part < 3:
-            loads[part + 1][0].wait()
-            coming = rows_of(part + 1)
+        if part == 0:
+            loads[1][1].wait()
+            coming = COMING[1]
+        elif part == 1:
+            loads[3][1].wait()
+            coming = COMING[3] + (ROWS,)
         for pair in range(count // 2):
             y = first + pair * 2
-            back = nn(taps[...], jnp.concatenate([around(shifted, y), around(shifted, y + 1)], axis=1))
+            if part == EARLY:
+                back = nn(end_taps, jnp.concatenate([end_hits(y), end_hits(y + 1)], axis=1))
+            else:
+                back = nn(taps[...], jnp.concatenate([around(shifted, y), around(shifted, y + 1)], axis=1))
             for k in range(2):
                 grad[y + k] = dfield[y + k] + back[:, COLS * k : COLS * (k + 1)]
             share = -(-len(coming) // (count // 2 - pair))

time: 55.6 us -> 54.7 us (0.984)
  Pallas kernels: 54.1 us -> 53.1 us
    pallas_call x1, Pallas kernels: 7.14 us -> 6.38 us  [on_device(): pl.pallas_call(back_kernel, out_shape=(jax.ShapeDtypeStruct((ROWS, CH, CO...]
where the time goes in v6:
time: 54.7 us; the launch traced here: 54.6 us
  Pallas kernels  53.1 us (97%)
  between operations  1.45 us (3%)
    pallas_call x1, Pallas kernels, on_device(): pl.pallas_call(kernel, out_shape=(jax.ShapeDtypeStruct((STATIONS, 128), F...  46.7 us
    pallas_call x1, Pallas kernels, on_device(): pl.pallas_call(back_kernel, out_shape=(jax.ShapeDtypeStruct((ROWS, CH, CO...  6.38 us

profile of v6, /device:TPU:0, one launch (start us, length us, event | category | flops | bytes accessed | tf_op | source)
XLA Modules:
  0.0 54.6 jit_solution(15642885215671007023)
XLA Ops:
  1.3 46.7 %whole.1 = (f32[256,128]{1,0:T(8,128)}, bf16[32,192,128]{2,1,0:T(8,128)(2,1)}, f32[32,192,128]{2,1,0:T(8,128)}, bf16[192,1792]{1,0:T(8,128)(2,1)}, bf16[2,192,12...) custom-call(bf16[32,192,128]{2,1,0:T(8,128)(2,1)} %bitcast.12, ...), custom_call_target="tpu_custom_call" | custom-call | tf_op jit(solution)/shard_map/whole/pallas_call | solution.py:617
  48.0 6.4 %back.1 = (f32[32,192,128]{2,1,0:T(8,128)}, f32[256,128]{1,0:T(8,128)}) custom-call(bf16[32,192,128]{2,1,0:T(8,128)(2,1)} %get-tuple-element.11.refs_0_, f32[32,192,128]{2,1,0:T(8,128)} %get-tuple-element.12.refs_1_, bf16[192,1792]{1,0:T(8,128)(2,1)} %get-tuple-element.13.refs_2_, bf16[2,192,128]{2,1,0:T(8,128)(2,1)} %get-tuple-element.14.refs_3_, ...), custom_call_target="tpu_custom_call" | custom-call | tf_op jit(solution)/shard_map/back/pallas_call | solution.py:682

commit v7 on v6

--- a/solution.py
+++ b/solution.py
@@ -74,9 +74,9 @@
     return jnp.concatenate([shifted[pl.ds(y, 3)].reshape(TAPS, COLS), end_hits(y)], axis=0)
 
 
-PARTS = ((0, 4), (4, 10), (14, 10), (24, 8))
+PARTS = ((0, 4), (4, 6), (10, 14), (24, 8))
 EARLY = 2
-COMING = (tuple(range(0, 5)), tuple(range(5, 15)), (), tuple(range(23, 32)))
+COMING = (tuple(range(0, 5)), tuple(range(5, 11)), (), tuple(range(23, 32)))
 
 
 def poles(lat):
@@ -476,8 +476,9 @@
             return carry
 
         lax.fori_loop(0, 5, scatter_rows, 0, unroll=True)
-        at = (pl.ds(1, 10), pl.ds(11, 3), pl.ds(24, 7))[third]
-        store(dfield.at[at], dfield_hbm.at[at])
+        at = (pl.ds(1, 9), None, pl.ds(24, 7))[third]
+        if at is not None:
+            store(dfield.at[at], dfield_hbm.at[at])
         at = pl.ds(1 + 10 * third, 10)
         store(dpre.at[at], dpre_hbm.at[at])
     first, count = PARTS[EARLY]

time: 54.7 us -> 54.5 us (level)
  no operation moved by 1% of the time
where the time goes in v7:
time: 54.5 us; the launch traced here: 54.3 us
  Pallas kernels  52.8 us (97%)
  between operations  1.45 us (3%)
    pallas_call x1, Pallas kernels, on_device(): pl.pallas_call(kernel, out_shape=(jax.ShapeDtypeStruct((STATIONS, 128), F...  46.7 us
    pallas_call x1, Pallas kernels, on_device(): pl.pallas_call(back_kernel, out_shape=(jax.ShapeDtypeStruct((ROWS, CH, CO...  6.1 us

profile of v7, /device:TPU:0, one launch (start us, length us, event | category | flops | bytes accessed | tf_op | source)
XLA Modules:
  0.0 54.3 jit_solution(7736451715860489814)
XLA Ops:
  1.3 46.7 %whole.1 = (f32[256,128]{1,0:T(8,128)}, bf16[32,192,128]{2,1,0:T(8,128)(2,1)}, f32[32,192,128]{2,1,0:T(8,128)}, bf16[192,1792]{1,0:T(8,128)(2,1)}, bf16[2,192,12...) custom-call(bf16[32,192,128]{2,1,0:T(8,128)(2,1)} %bitcast.12, ...), custom_call_target="tpu_custom_call" | custom-call | tf_op jit(solution)/shard_map/whole/pallas_call | solution.py:618
  48.0 6.1 %back.1 = (f32[32,192,128]{2,1,0:T(8,128)}, f32[256,128]{1,0:T(8,128)}) custom-call(bf16[32,192,128]{2,1,0:T(8,128)(2,1)} %get-tuple-element.11.refs_0_, f32[32,192,128]{2,1,0:T(8,128)} %get-tuple-element.12.refs_1_, bf16[192,1792]{1,0:T(8,128)(2,1)} %get-tuple-element.13.refs_2_, bf16[2,192,128]{2,1,0:T(8,128)(2,1)} %get-tuple-element.14.refs_3_, ...), custom_call_target="tpu_custom_call" | custom-call | tf_op jit(solution)/shard_map/back/pallas_call | solution.py:683
